TPU v7x, 32 devices: a whole 2x2x4 slice. The times are simulated.
32 devices in a mesh: ctx: 8 (over y, x, core), fsdp: 4 (over z).
Axes of the slice: x: 2, y: 2, z: 4, core: 2. Of those that a mesh axis runs over, the one named last changes fastest.
Arguments:
- inputs: bfloat16 [4, 1024, 768], P('fsdp', 'ctx'), may hold values from -6 to 6
- segments: int32 [4, 1024], P('fsdp', 'ctx'), may hold values from 0 to 1, as said below
- query_weight: bfloat16 [768, 768], P('fsdp'), may hold values from -0.21875 to 0.21875
- query_bias: bfloat16 [768], P('fsdp'), may hold values from -1.75 to 1.75
- key_weight: bfloat16 [768, 768], P('fsdp'), may hold values from -0.21875 to 0.21875
- value_weight: bfloat16 [768, 768], P('fsdp'), may hold values from -0.21875 to 0.21875
- value_bias: bfloat16 [768], P('fsdp'), may hold values from -0.125 to 0.125
- output_weight: bfloat16 [768, 768], P('fsdp'), may hold values from -3.5 to 3.5
- output_bias: bfloat16 [768], P('fsdp'), may hold values from -1.75 to 1.75
- first_gain: bfloat16 [768], P('fsdp'), may hold values from 0.099609375 to 1.8984375
- first_shift: bfloat16 [768], P('fsdp'), may hold values from -1.75 to 1.75
- inner_weight: bfloat16 [768, 3072], P('fsdp'), may hold values from -0.21875 to 0.21875
- inner_bias: bfloat16 [3072], P('fsdp'), may hold values from -1.75 to 1.75
- outer_weight: bfloat16 [3072, 768], P('fsdp'), may hold values from -0.109375 to 0.109375
- outer_bias: bfloat16 [768], P('fsdp'), may hold values from -1.75 to 1.75
- second_gain: bfloat16 [768], P('fsdp'), may hold values from 0.099609375 to 1.8984375
- second_shift: bfloat16 [768], P('fsdp'), may hold values from -1.75 to 1.75
- cotangent: bfloat16 [4, 1024, 768], P('fsdp', 'ctx'), may hold values from -8 to 8
Outputs:
- output: bfloat16 [4, 1024, 768], P('fsdp', 'ctx')
- grad_input: bfloat16 [4, 1024, 768], P('fsdp', 'ctx')
- grad_query_weight: float32 [768, 768], P('fsdp')
- grad_query_bias: float32 [768], P('fsdp')
- grad_key_weight: float32 [768, 768], P('fsdp')
- grad_value_weight: float32 [768, 768], P('fsdp')
- grad_value_bias: float32 [768], P('fsdp')
- grad_output_weight: float32 [768, 768], P('fsdp')
- grad_output_bias: float32 [768], P('fsdp')
- grad_first_gain: float32 [768], P('fsdp')
- grad_first_shift: float32 [768], P('fsdp')
- grad_inner_weight: float32 [768, 3072], P('fsdp')
- grad_inner_bias: float32 [3072], P('fsdp')
- grad_outer_weight: float32 [3072, 768], P('fsdp')
- grad_outer_bias: float32 [768], P('fsdp')
- grad_second_gain: float32 [768], P('fsdp')
- grad_second_shift: float32 [768], P('fsdp')
Inputs may be any that keep to these rules, and one draw needn't show every extreme that they name: `segments`: position p of a sequence is stored at entry (p mod R) * 128 + p div R, with R = 8. Taken in order of position, document numbers never fall and step by one; each document holds roughly a quarter to seven quarters of 512 positions.
All inputs are finite; a program needn't handle non-finite values.
Results may differ from a plain program's by a relative error of at most 0.02.
Values may be sent and summed in bfloat16 or wider, within the bound.
No kernel may reach another device: no remote copies, remote signals or barrier semaphores. Data moves between devices by JAX's collectives and lax.ppermute only.
A program may use at most 128 MiB of HBM per device.

v0:
```python
import jax
import jax.numpy as jnp
from jax import lax
from jax.sharding import PartitionSpec as P

HEADS = 12
HEAD_DIM = 64


NEGATIVE = -1000000000.0
EPSILON = 1e-12


def passed_along(block, axis, distance):
    devices = range(lax.axis_size(axis))
    route = [((i - distance) % len(devices), i) for i in devices]
    return lax.ppermute(block, axis, route)


def layer_norm(values, norm_gain, norm_shift):
    center = values - jnp.mean(values, -1, keepdims=True)
    spread = jnp.mean(center * center, -1, keepdims=True)
    return center * lax.rsqrt(spread + EPSILON) * norm_gain + norm_shift


def gelu_exact(values):
    return jax.nn.gelu(values, approximate=False)


def product(leading, trailing):
    return jnp.dot(leading, trailing, preferred_element_type=jnp.float32)


def product_right_t(leading, trailing):
    return jnp.einsum("ta,ba->tb", leading, trailing, preferred_element_type=jnp.float32)


def product_left_t(leading, trailing):
    return jnp.einsum("ta,tb->ab", leading, trailing, preferred_element_type=jnp.float32)


def column_total(values):
    return jnp.sum(values.astype(jnp.float32), 0)


def block_size(extent):
    for candidate in (1024, 512, 256, 128, 64, 32, 16, 8, 4, 2, 1):
        return candidate
    return extent


def over_blocks(step_fn, fold_carry, arrays, extent):
    block_rows = block_size(extent)
    if block_rows == extent:
        return step_fn(fold_carry, arrays, 0)

    def scan_step(run_state, block_index):
        offset = block_index * block_rows
        block_parts = tuple(
            (lax.dynamic_slice_in_dim(member, offset, block_rows, 0) for member in arrays)
        )
        return (step_fn(run_state, block_parts, offset), None)

    finished, unused = lax.scan(
        scan_step, fold_carry, jnp.arange(extent // block_rows, dtype=jnp.int32)
    )
    return finished


def per_device(
    inputs,
    segments,
    query_weight,
    query_bias,
    key_weight,
    value_weight,
    value_bias,
    output_weight,
    output_bias,
    first_gain,
    first_shift,
    inner_weight,
    inner_bias,
    outer_weight,
    outer_bias,
    second_gain,
    second_shift,
    cotangent,
):
    (
        w_query,
        b_query,
        w_key,
        w_value,
        b_value,
        w_output,
        b_output,
        gain_first,
        shift_first,
        w_inner,
        b_inner,
        w_outer,
        b_outer,
        gain_second,
        shift_second,
    ) = (
        lax.all_gather(query_weight, "fsdp", axis=0, tiled=True),
        lax.all_gather(query_bias, "fsdp", axis=0, tiled=True),
        lax.all_gather(key_weight, "fsdp", axis=0, tiled=True),
        lax.all_gather(value_weight, "fsdp", axis=0, tiled=True),
        lax.all_gather(value_bias, "fsdp", axis=0, tiled=True),
        lax.all_gather(output_weight, "fsdp", axis=0, tiled=True),
        lax.all_gather(output_bias, "fsdp", axis=0, tiled=True),
        lax.all_gather(first_gain, "fsdp", axis=0, tiled=True),
        lax.all_gather(first_shift, "fsdp", axis=0, tiled=True),
        lax.all_gather(inner_weight, "fsdp", axis=0, tiled=True),
        lax.all_gather(inner_bias, "fsdp", axis=0, tiled=True),
        lax.all_gather(outer_weight, "fsdp", axis=0, tiled=True),
        lax.all_gather(outer_bias, "fsdp", axis=0, tiled=True),
        lax.all_gather(second_gain, "fsdp", axis=0, tiled=True),
        lax.all_gather(second_shift, "fsdp", axis=0, tiled=True),
    )
    head_scale = HEAD_DIM ** (-0.5)
    tokens = inputs[0]
    own_segment = segments[0]
    token_count = tokens.shape[0]
    per_head = (token_count, HEADS, HEAD_DIM)
    full_segment = lax.all_gather(own_segment, "ctx", axis=0, tiled=True)
    queries = (product(tokens, w_query) + b_query).astype(jnp.bfloat16)
    key_rows = product(tokens, w_key).astype(jnp.bfloat16)
    values = (product(tokens, w_value) + b_value).astype(jnp.bfloat16)
    queries_heads = queries.reshape(per_head)
    keys_heads = key_rows.reshape(per_head)
    values_heads = values.reshape(per_head)
    start_state = (
        jnp.full((HEADS, token_count), NEGATIVE, jnp.float32),
        jnp.zeros((HEADS, token_count), jnp.float32),
        jnp.zeros(per_head, jnp.float32),
    )
    piece = (
        lax.all_gather(key_rows, "ctx", axis=0, tiled=True),
        lax.all_gather(values, "ctx", axis=0, tiled=True),
    )
    start = jnp.int32(0)

    def step_fn(run_state, block_parts, offset):
        run_top, run_total, run_accum = run_state
        key_block = block_parts[0].reshape(-1, HEADS, HEAD_DIM)
        value_block = block_parts[1].reshape(-1, HEADS, HEAD_DIM)
        key_segment = lax.dynamic_slice_in_dim(full_segment, start + offset, key_block.shape[0], 0)
        allowed = (own_segment[:, None] == key_segment[None, :])[None]
        scores = (
            jnp.einsum("qhe,khe->hqk", queries_heads, key_block, preferred_element_type=jnp.float32)
            * head_scale
        )
        scores = jnp.where(allowed, scores, NEGATIVE)
        new_top = jnp.maximum(run_top, jnp.max(scores, -1))
        weights = jnp.where(allowed, jnp.exp(scores - new_top[:, :, None]), 0.0)
        factor = jnp.exp(run_top - new_top)
        run_total = run_total * factor + jnp.sum(weights, -1)
        update = jnp.einsum(
            "hqk,khe->qhe",
            weights.astype(jnp.bfloat16),
            value_block,
            preferred_element_type=jnp.float32,
        )
        run_accum = run_accum * factor.T[:, :, None] + update
        return (new_top, run_total, run_accum)

    run_top, run_total, run_accum = over_blocks(step_fn, start_state, piece, piece[0].shape[0])
    context = run_accum / run_total.T[:, :, None]
    logsum = run_top + jnp.log(run_total)
    context_low = context.reshape(token_count, -1).astype(jnp.bfloat16)
    residual_one = tokens.astype(jnp.float32) + product(context_low, w_output) + b_output
    normed_one, first_pull = jax.vjp(
        layer_norm, residual_one, gain_first.astype(jnp.float32), shift_first.astype(jnp.float32)
    )
    normed_low = normed_one.astype(jnp.bfloat16)
    inner_pre = product(normed_low, w_inner) + b_inner
    activated, gelu_pull = jax.vjp(gelu_exact, inner_pre)
    activated_low = activated.astype(jnp.bfloat16)
    summed = normed_one + product(activated_low, w_outer) + b_outer
    result, second_pull = jax.vjp(
        layer_norm, summed, gain_second.astype(jnp.float32), shift_second.astype(jnp.float32)
    )
    grad_summed, grad_gain_second, grad_shift_second = second_pull(cotangent[0].astype(jnp.float32))
    grad_outer_low = grad_summed.astype(jnp.bfloat16)
    grad_b_outer = column_total(grad_outer_low)
    grad_w_outer = product_left_t(activated_low, grad_outer_low)
    (grad_inner,) = gelu_pull(product_right_t(grad_outer_low, w_outer))
    grad_inner_low = grad_inner.astype(jnp.bfloat16)
    grad_b_inner = column_total(grad_inner_low)
    grad_w_inner = product_left_t(normed_low, grad_inner_low)
    grad_normed = grad_summed + product_right_t(grad_inner_low, w_inner)
    grad_residual, grad_gain_first, grad_shift_first = first_pull(grad_normed)
    grad_branch_low = grad_residual.astype(jnp.bfloat16)
    grad_b_output = column_total(grad_branch_low)
    grad_w_output = product_left_t(context_low, grad_branch_low)
    grad_context_low = product_right_t(grad_branch_low, w_output).astype(jnp.bfloat16)
    grad_context_heads = grad_context_low.reshape(per_head)
    row_delta = jnp.sum(grad_context_heads.astype(jnp.float32) * context, -1).T
    empty_heads = jnp.zeros(per_head, jnp.float32)
    cycle_count = lax.axis_size("ctx")
    own_place = lax.axis_index("ctx")

    def cycle_step(step, cycle_state):
        key_piece, value_piece, grad_key_acc, grad_value_acc, grad_query_acc = cycle_state
        anchor = jnp.mod(own_place - step, cycle_count)
        key_segment = lax.dynamic_slice_in_dim(full_segment, anchor * token_count, token_count, 0)
        allowed = (own_segment[:, None] == key_segment[None, :])[None]
        scores = (
            jnp.einsum("qhe,khe->hqk", queries_heads, key_piece, preferred_element_type=jnp.float32)
            * head_scale
        )
        soft_scores = jnp.where(allowed, jnp.exp(scores - logsum[:, :, None]), 0.0)
        grad_probs = jnp.einsum(
            "qhe,khe->hqk", grad_context_heads, value_piece, preferred_element_type=jnp.float32
        )
        grad_scores = (soft_scores * (grad_probs - row_delta[:, :, None])).astype(jnp.bfloat16)
        grad_query_acc = grad_query_acc + jnp.einsum(
            "hqk,khe->qhe", grad_scores, key_piece, preferred_element_type=jnp.float32
        )
        grad_key_acc = grad_key_acc + jnp.einsum(
            "hqk,qhe->khe", grad_scores, queries_heads, preferred_element_type=jnp.float32
        )
        grad_value_acc = grad_value_acc + jnp.einsum(
            "hqk,qhe->khe",
            soft_scores.astype(jnp.bfloat16),
            grad_context_heads,
            preferred_element_type=jnp.float32,
        )
        key_piece, value_piece = passed_along((key_piece, value_piece), "ctx", 1)
        grad_key_acc, grad_value_acc = (
            passed_along(grad_key_acc.astype(jnp.bfloat16), "ctx", 1).astype(grad_key_acc.dtype),
            passed_along(grad_value_acc.astype(jnp.bfloat16), "ctx", 1).astype(
                grad_value_acc.dtype
            ),
        )
        return (key_piece, value_piece, grad_key_acc, grad_value_acc, grad_query_acc)

    cycle_start = (keys_heads, values_heads, empty_heads, empty_heads, empty_heads)
    unused_keys, unused_values, grad_key_sum, grad_value_sum, grad_query_sum = lax.fori_loop(
        0, cycle_count, cycle_step, cycle_start
    )
    grad_query_low = (grad_query_sum * head_scale).reshape(token_count, -1).astype(jnp.bfloat16)
    grad_key_low = (grad_key_sum * head_scale).reshape(token_count, -1).astype(jnp.bfloat16)
    grad_value_low = grad_value_sum.reshape(token_count, -1).astype(jnp.bfloat16)
    grad_w_query = product_left_t(tokens, grad_query_low)
    grad_b_query = column_total(grad_query_low)
    grad_w_key = product_left_t(tokens, grad_key_low)
    grad_w_value = product_left_t(tokens, grad_value_low)
    grad_b_value = column_total(grad_value_low)
    grad_tokens = (
        grad_residual
        + product_right_t(grad_query_low, w_query)
        + product_right_t(grad_key_low, w_key)
        + product_right_t(grad_value_low, w_value)
    )
    s_wq, s_bq, s_wk, s_wv, s_bv, s_wo, s_bo, s_ga, s_sa, s_wi, s_bi, s_wu, s_bu, s_gb, s_sb = (
        lax.psum_scatter(
            grad_w_query.astype(jnp.bfloat16), "fsdp", scatter_dimension=0, tiled=True
        ).astype(jnp.float32),
        lax.psum_scatter(
            grad_b_query.astype(jnp.bfloat16), "fsdp", scatter_dimension=0, tiled=True
        ).astype(jnp.float32),
        lax.psum_scatter(
            grad_w_key.astype(jnp.bfloat16), "fsdp", scatter_dimension=0, tiled=True
        ).astype(jnp.float32),
        lax.psum_scatter(
            grad_w_value.astype(jnp.bfloat16), "fsdp", scatter_dimension=0, tiled=True
        ).astype(jnp.float32),
        lax.psum_scatter(
            grad_b_value.astype(jnp.bfloat16), "fsdp", scatter_dimension=0, tiled=True
        ).astype(jnp.float32),
        lax.psum_scatter(
            grad_w_output.astype(jnp.bfloat16), "fsdp", scatter_dimension=0, tiled=True
        ).astype(jnp.float32),
        lax.psum_scatter(
            grad_b_output.astype(jnp.bfloat16), "fsdp", scatter_dimension=0, tiled=True
        ).astype(jnp.float32),
        lax.psum_scatter(
            grad_gain_first.astype(jnp.bfloat16), "fsdp", scatter_dimension=0, tiled=True
        ).astype(jnp.float32),
        lax.psum_scatter(
            grad_shift_first.astype(jnp.bfloat16), "fsdp", scatter_dimension=0, tiled=True
        ).astype(jnp.float32),
        lax.psum_scatter(
            grad_w_inner.astype(jnp.bfloat16), "fsdp", scatter_dimension=0, tiled=True
        ).astype(jnp.float32),
        lax.psum_scatter(
            grad_b_inner.astype(jnp.bfloat16), "fsdp", scatter_dimension=0, tiled=True
        ).astype(jnp.float32),
        lax.psum_scatter(
            grad_w_outer.astype(jnp.bfloat16), "fsdp", scatter_dimension=0, tiled=True
        ).astype(jnp.float32),
        lax.psum_scatter(
            grad_b_outer.astype(jnp.bfloat16), "fsdp", scatter_dimension=0, tiled=True
        ).astype(jnp.float32),
        lax.psum_scatter(
            grad_gain_second.astype(jnp.bfloat16), "fsdp", scatter_dimension=0, tiled=True
        ).astype(jnp.float32),
        lax.psum_scatter(
            grad_shift_second.astype(jnp.bfloat16), "fsdp", scatter_dimension=0, tiled=True
        ).astype(jnp.float32),
    )
    totals = lax.psum(
        (s_wq, s_bq, s_wk, s_wv, s_bv, s_wo, s_bo, s_ga, s_sa, s_wi, s_bi, s_wu, s_bu, s_gb, s_sb),
        "ctx",
    )
    return (
        result.astype(jnp.bfloat16)[None],
        grad_tokens.astype(jnp.bfloat16)[None],
        totals[0],
        totals[1],
        totals[2],
        totals[3],
        totals[4],
        totals[5],
        totals[6],
        totals[7],
        totals[8],
        totals[9],
        totals[10],
        totals[11],
        totals[12],
        totals[13],
        totals[14],
    )


def solution(mesh):
    return jax.shard_map(
        per_device,
        mesh=mesh,
        in_specs=(
            P("fsdp", "ctx", None),
            P("fsdp", "ctx"),
            P("fsdp", None),
            P("fsdp"),
            P("fsdp", None),
            P("fsdp", None),
            P("fsdp"),
            P("fsdp", None),
            P("fsdp"),
            P("fsdp"),
            P("fsdp"),
            P("fsdp", None),
            P("fsdp"),
            P("fsdp", None),
            P("fsdp"),
            P("fsdp"),
            P("fsdp"),
            P("fsdp", "ctx", None),
        ),
        out_specs=(
            P("fsdp", "ctx", None),
            P("fsdp", "ctx", None),
            P("fsdp", None),
            P("fsdp"),
            P("fsdp", None),
            P("fsdp", None),
            P("fsdp"),
            P("fsdp", None),
            P("fsdp"),
            P("fsdp"),
            P("fsdp"),
            P("fsdp", None),
            P("fsdp"),
            P("fsdp", None),
            P("fsdp"),
            P("fsdp"),
            P("fsdp"),
        ),
        check_vma=False,
    )
```

profile of v0, /device:TPU:0, one launch (start us, length us, event | category | flops | bytes accessed | tf_op | source)
XLA Modules:
  0.0 971.3 jit_solution(11838158099280438394)
XLA Ops:
  9.5 33.3 %all-gather.13.cloned.1.call-done = bf16[768,768]{1,0:T(8,128)(2,1)} async-done(((bf16[192,768]{1,0:T(8,128)(2,1)}), bf16[768,768]{1,0:T(8,128)(2,1)}) %all-gather.13.cloned.1.call-update) | async-done | bytes 1179664 | tf_op jit(solution)/shard_map/all_gather | solution.py:109
  48.3 17.4 %all-reduce.19 = (bf16[768]{0:T(1024)(128)(2,1)S(1)}, bf16[768]{0:T(1024)(128)(2,1)S(1)}, bf16[768]{0:T(1024)(128)(2,1)S(1)}, bf16[768]{0:T(1024)(128)(2,1)S(1)}...) all-reduce(bf16[768]{0:T(1024)(128)(2,1)S(1)} %dynamic-update-slice, ...), channel_id=1, replica_groups=mesh['ctx'=8,'fsdp'=4] {'fsdp'}, use_global_device_ids=true, to_apply=%add.1 | all-reduce | flops 5376 | bytes 21504
  65.7 8.8 all-gather.17.cloned.1.call-done
  79.0 13.2 %all-gather.1 = bf16[4,1,768]{2,1,0:T(2,128)(2,1)S(1)} all-gather(bf16[1,1,768]{2,1,0:T(2,128)(2,1)S(1)} %reshape.238), channel_id=1, replica_groups=mesh['ctx'=8,'fsdp'=4] {'fsdp'}, dimensions={0}, use_global_device_ids=true | all-gather | bytes 7680 | tf_op jit(solution)/shard_map/all_gather | solution.py:117
  92.2 10.4 %all-gather = s32[1,1024]{1,0:T(1,128)} all-gather(s32[1,128]{1,0:T(1,128)} %param.21), channel_id=2, replica_groups=mesh['ctx'=8,'fsdp'=4] {'ctx'}, dimensions={1}, use_global_device_ids=true | all-gather | bytes 4608 | tf_op jit(solution)/shard_map/all_gather | solution.py:128
  107.4 25.4 %all-gather.15.cloned.1.call-done = bf16[1024,768]{1,0:T(8,128)(2,1)} async-done(((bf16[128,768]{1,0:T(8,128)(2,1)}), bf16[1024,768]{1,0:T(8,128)(2,1)}) %all-gather.15.cloned.1.call-update) | async-done | bytes 1572880 | tf_op jit(solution)/shard_map/all_gather | solution.py:141
  132.8 2.6 copy.55
  135.4 25.5 %all-gather.19.cloned.1.call-done = bf16[1024,768]{1,0:T(8,128)(2,1)} async-done(((bf16[128,768]{1,0:T(8,128)(2,1)}), bf16[1024,768]{1,0:T(8,128)(2,1)}) %all-gather.19.cloned.1.call-update) | async-done | bytes 1572880 | tf_op jit(solution)/shard_map/all_gather | solution.py:142
  160.8 2.6 copy.56
  163.4 2.7 fusion.11
  168.7 2.6 fusion.70
  171.3 21.4 %all-gather.21.cloned.1.call-done = bf16[768,768]{1,0:T(8,128)(2,1)} async-done(((bf16[192,768]{1,0:T(8,128)(2,1)}), bf16[768,768]{1,0:T(8,128)(2,1)}) %all-gather.21.cloned.1.call-update) | async-done | bytes 1179664 | tf_op jit(solution)/shard_map/all_gather | solution.py:112
  194.6 88.2 %all-gather.23.cloned.1.call-done = bf16[768,3072]{1,0:T(8,128)(2,1)} async-done(((bf16[192,3072]{1,0:T(8,128)(2,1)}), bf16[768,3072]{1,0:T(8,128)(2,1)}) %all-gather.23.cloned.1.call-update) | async-done | bytes 4718608 | tf_op jit(solution)/shard_map/all_gather | solution.py:116
  282.9 8.4 multiply_convert_fusion
  291.2 81.1 %all-gather.25.cloned.1.call-done = bf16[3072,768]{1,0:T(8,128)(2,1)} async-done(((bf16[768,768]{1,0:T(8,128)(2,1)}), bf16[3072,768]{1,0:T(8,128)(2,1)}) %all-gather.25.cloned.1.call-update) | async-done | bytes 4718608 | tf_op jit(solution)/shard_map/all_gather | solution.py:118
  372.3 3.4 fusion.72
  385.8 122.6 %while.24 = (s32[]{:T(128)}, bf16[128,12,64]{0,2,1:T(8,128)(2,1)}, bf16[128,12,64]{0,2,1:T(8,128)(2,1)S(1)}, f32[128,12,64]{0,2,1:T(8,128)S(1)}, f32[128,12,64]{...) while((s32[]{:T(128)}, bf16[128,12,64]{0,2,1:T(8,128)(2,1)}, ...), condition=%wide.region_12.13_spmd.clone, body=%wide.region_11.12_spmd.clone.sunk | while | flops 128204816 | bytes 12040708 | solution.py:242
  395.3 3.4 collective-permute-done.2
  425.7 4.1 collective-permute-done.2
  441.4 2.8 collective-permute-done.2
  456.4 3.4 collective-permute-done.2
  486.8 4.1 collective-permute-done.2
  502.5 2.8 collective-permute-done.2
  517.0 3.6 convolution_convert_fusion.1
  521.8 3.6 convolution_convert_fusion
  531.1 17.7 %all-reduce.18 = (bf16[768]{0:T(1024)(128)(2,1)S(1)}, bf16[768]{0:T(1024)(128)(2,1)}, bf16[768]{0:T(1024)(128)(2,1)}, bf16[768]{0:T(1024)(128)(2,1)}, bf16[768]{...) all-reduce(bf16[768]{0:T(1024)(128)(2,1)} %dynamic-update-slice.7, ...), channel_id=1, replica_groups=mesh['ctx'=8,'fsdp'=4] {'fsdp'}, use_global_device_ids=true, to_apply=%add.7 | all-reduce | flops 9984 | bytes 39936
  564.0 5.2 reduce-scatter.23.cloned.1.call-done
  570.4 29.7 %reduce-scatter.21.cloned.1.call-done = bf16[192,768]{1,0:T(8,128)(2,1)} async-done(((bf16[768,768]{1,0:T(8,128)(2,1)}), bf16[192,768]{1,0:T(8,128)(2,1)}) %reduce-scatter.21.cloned.1.call-update) | async-done | bytes 294928
  601.2 29.0 %reduce-scatter.13.cloned.1.call-done = bf16[192,768]{1,0:T(8,128)(2,1)} async-done(((bf16[768,768]{1,0:T(8,128)(2,1)}), bf16[192,768]{1,0:T(8,128)(2,1)}) %reduce-scatter.13.cloned.1.call-update) | async-done | bytes 294928 | tf_op jit(solution)/shard_map/reduce_scatter | solution.py:275
  630.2 86.3 %reduce-scatter.15.cloned.1.call-done = bf16[192,3072]{1,0:T(8,128)(2,1)} async-done(((bf16[768,3072]{1,0:T(8,128)(2,1)}), bf16[192,3072]{1,0:T(8,128)(2,1)}) %reduce-scatter.15.cloned.1.call-update) | async-done | bytes 1179664 | tf_op jit(solution)/shard_map/reduce_scatter | solution.py:287
  716.5 88.0 %reduce-scatter.17.cloned.1.call-done = bf16[768,768]{1,0:T(8,128)(2,1)} async-done(((bf16[3072,768]{1,0:T(8,128)(2,1)}), bf16[768,768]{1,0:T(8,128)(2,1)}) %reduce-scatter.17.cloned.1.call-update) | async-done | bytes 1179664 | tf_op jit(solution)/shard_map/reduce_scatter | solution.py:293
  804.5 156.0 %all-reduce.21 = (f32[192,768]{0,1:T(8,128)}, f32[192]{0:T(256)}, f32[192,768]{0,1:T(8,128)S(1)}, f32[192,768]{0,1:T(8,128)S(1)}, f32[192]{0:T(256)}, /*index=5*...) all-reduce(bf16[192,768]{0,1:T(8,128)(2,1)S(1)} %copy.64, ...), channel_id=1, replica_groups=mesh['ctx'=8,'fsdp'=4] {'ctx'}, use_global_device_ids=true, to_apply=%region_14.15 | all-reduce | flops 1771776 | bytes 10635264 | tf_op jit(solution)/shard_map/psum | solution.py:306
  (391 shorter events, 167.5 us)
Async XLA Ops:
  7.3 35.6 %all-gather.13.cloned.1.call-start = ((), (), s32[]{:S(2)}) async-start(), calls=%async_computation.7 | async-start | bytes 1474560 | tf_op jit(solution)/shard_map/all_gather | solution.py:109
  8.0 66.5 %all-gather.17.cloned.1.call-start = ((), (), s32[]{:S(2)}) async-start(), calls=%async_computation.9 | async-start | bytes 1474560 | tf_op jit(solution)/shard_map/all_gather | solution.py:110
  8.8 96.9 %all-gather.11.cloned.1.call-start = ((), (), s32[]{:S(2)}) async-start(), calls=%async_computation.6 | async-start | bytes 1474560 | tf_op jit(solution)/shard_map/all_gather | solution.py:107
  9.5 123.3 %all-gather.15.cloned.1.call-start = ((), (), s32[]{:S(2)}) async-start(), calls=%async_computation.8 | async-start | bytes 1769472 | tf_op jit(solution)/shard_map/all_gather | solution.py:141
  45.3 115.5 %all-gather.19.cloned.1.call-start = ((), (), s32[]{:S(2)}) async-start(), calls=%async_computation.10 | async-start | bytes 1769472 | tf_op jit(solution)/shard_map/all_gather | solution.py:142
  76.8 115.9 %all-gather.21.cloned.1.call-start = ((), (), s32[]{:S(2)}) async-start(), calls=%async_computation.11 | async-start | bytes 1474560 | tf_op jit(solution)/shard_map/all_gather | solution.py:112
  77.4 205.5 %all-gather.23.cloned.1.call-start = ((), (), s32[]{:S(2)}) async-start(), calls=%async_computation.12 | async-start | bytes 5898240 | tf_op jit(solution)/shard_map/all_gather | solution.py:116
  78.1 294.2 %all-gather.25.cloned.1.call-start = ((), (), s32[]{:S(2)}) async-start(), calls=%async_computation.13 | async-start | bytes 5898240 | tf_op jit(solution)/shard_map/all_gather | solution.py:118
  78.9 484.0 %reduce-scatter.19.cloned.1.call-start = ((), (), s32[]{:S(2)}) async-start(), calls=%async_computation.17 | async-start | bytes 1474560
  386.8 15.0 %collective-permute-start = (bf16[128,12,64]{0,2,1:T(8,128)(2,1)S(1)}, bf16[128,12,64]{0,2,1:T(8,128)(2,1)}, u32[]{:S(2)}, u32[]{:S(2)}) collective-permute-start(bf16[128,12,64]{0,2,1:T(8,128)(2,1)S(1)} %copy.84), channel_id=1, source_target_pairs={{28,0},{0,4},{4,8},{8,12},{12,16},{16,20},{20,24},{24,28},{29,1},{... | collective-permute-start | bytes 589832 | tf_op jit(solution)/shard_map/while/body/eval_jaxpr/ppermute | solution.py:17
  386.8 15.0 %collective-permute-start.1 = (bf16[128,12,64]{0,2,1:T(8,128)(2,1)S(1)}, bf16[128,12,64]{0,2,1:T(8,128)(2,1)S(1)}, u32[]{:S(2)}, u32[]{:S(2)}) collective-permute-start(bf16[128,12,64]{0,2,1:T(8,128)(2,1)S(1)} %copy.85), channel_id=1, source_target_pairs={{28,0},{0,4},{4,8},{8,12},{12,16},{16,20},{20,24},{24,28},{29,1},{... | collective-permute-start | bytes 589832 | tf_op jit(solution)/shard_map/while/body/eval_jaxpr/ppermute | solution.py:17
  393.4 7.5 collective-permute-start.3
  402.7 14.1 %collective-permute-start = (bf16[128,12,64]{0,2,1:T(8,128)(2,1)S(1)}, bf16[128,12,64]{0,2,1:T(8,128)(2,1)}, u32[]{:S(2)}, u32[]{:S(2)}) collective-permute-start(bf16[128,12,64]{0,2,1:T(8,128)(2,1)S(1)} %copy.84), channel_id=1, source_target_pairs={{28,0},{0,4},{4,8},{8,12},{12,16},{16,20},{20,24},{24,28},{29,1},{... | collective-permute-start | bytes 589832 | tf_op jit(solution)/shard_map/while/body/eval_jaxpr/ppermute | solution.py:17
  402.8 14.1 %collective-permute-start.1 = (bf16[128,12,64]{0,2,1:T(8,128)(2,1)S(1)}, bf16[128,12,64]{0,2,1:T(8,128)(2,1)S(1)}, u32[]{:S(2)}, u32[]{:S(2)}) collective-permute-start(bf16[128,12,64]{0,2,1:T(8,128)(2,1)S(1)} %copy.85), channel_id=1, source_target_pairs={{28,0},{0,4},{4,8},{8,12},{12,16},{16,20},{20,24},{24,28},{29,1},{... | collective-permute-start | bytes 589832 | tf_op jit(solution)/shard_map/while/body/eval_jaxpr/ppermute | solution.py:17
  408.4 7.5 collective-permute-start.3
  417.8 15.0 %collective-permute-start = (bf16[128,12,64]{0,2,1:T(8,128)(2,1)S(1)}, bf16[128,12,64]{0,2,1:T(8,128)(2,1)}, u32[]{:S(2)}, u32[]{:S(2)}) collective-permute-start(bf16[128,12,64]{0,2,1:T(8,128)(2,1)S(1)} %copy.84), channel_id=1, source_target_pairs={{28,0},{0,4},{4,8},{8,12},{12,16},{16,20},{20,24},{24,28},{29,1},{... | collective-permute-start | bytes 589832 | tf_op jit(solution)/shard_map/while/body/eval_jaxpr/ppermute | solution.py:17
  417.8 15.0 %collective-permute-start.1 = (bf16[128,12,64]{0,2,1:T(8,128)(2,1)S(1)}, bf16[128,12,64]{0,2,1:T(8,128)(2,1)S(1)}, u32[]{:S(2)}, u32[]{:S(2)}) collective-permute-start(bf16[128,12,64]{0,2,1:T(8,128)(2,1)S(1)} %copy.85), channel_id=1, source_target_pairs={{28,0},{0,4},{4,8},{8,12},{12,16},{16,20},{20,24},{24,28},{29,1},{... | collective-permute-start | bytes 589832 | tf_op jit(solution)/shard_map/while/body/eval_jaxpr/ppermute | solution.py:17
  433.8 13.5 %collective-permute-start = (bf16[128,12,64]{0,2,1:T(8,128)(2,1)S(1)}, bf16[128,12,64]{0,2,1:T(8,128)(2,1)}, u32[]{:S(2)}, u32[]{:S(2)}) collective-permute-start(bf16[128,12,64]{0,2,1:T(8,128)(2,1)S(1)} %copy.84), channel_id=1, source_target_pairs={{28,0},{0,4},{4,8},{8,12},{12,16},{16,20},{20,24},{24,28},{29,1},{... | collective-permute-start | bytes 589832 | tf_op jit(solution)/shard_map/while/body/eval_jaxpr/ppermute | solution.py:17
  433.8 13.5 %collective-permute-start.1 = (bf16[128,12,64]{0,2,1:T(8,128)(2,1)S(1)}, bf16[128,12,64]{0,2,1:T(8,128)(2,1)S(1)}, u32[]{:S(2)}, u32[]{:S(2)}) collective-permute-start(bf16[128,12,64]{0,2,1:T(8,128)(2,1)S(1)} %copy.85), channel_id=1, source_target_pairs={{28,0},{0,4},{4,8},{8,12},{12,16},{16,20},{20,24},{24,28},{29,1},{... | collective-permute-start | bytes 589832 | tf_op jit(solution)/shard_map/while/body/eval_jaxpr/ppermute | solution.py:17
  448.2 14.7 %collective-permute-start = (bf16[128,12,64]{0,2,1:T(8,128)(2,1)S(1)}, bf16[128,12,64]{0,2,1:T(8,128)(2,1)}, u32[]{:S(2)}, u32[]{:S(2)}) collective-permute-start(bf16[128,12,64]{0,2,1:T(8,128)(2,1)S(1)} %copy.84), channel_id=1, source_target_pairs={{28,0},{0,4},{4,8},{8,12},{12,16},{16,20},{20,24},{24,28},{29,1},{... | collective-permute-start | bytes 589832 | tf_op jit(solution)/shard_map/while/body/eval_jaxpr/ppermute | solution.py:17
  448.2 14.7 %collective-permute-start.1 = (bf16[128,12,64]{0,2,1:T(8,128)(2,1)S(1)}, bf16[128,12,64]{0,2,1:T(8,128)(2,1)S(1)}, u32[]{:S(2)}, u32[]{:S(2)}) collective-permute-start(bf16[128,12,64]{0,2,1:T(8,128)(2,1)S(1)} %copy.85), channel_id=1, source_target_pairs={{28,0},{0,4},{4,8},{8,12},{12,16},{16,20},{20,24},{24,28},{29,1},{... | collective-permute-start | bytes 589832 | tf_op jit(solution)/shard_map/while/body/eval_jaxpr/ppermute | solution.py:17
  463.9 14.1 %collective-permute-start = (bf16[128,12,64]{0,2,1:T(8,128)(2,1)S(1)}, bf16[128,12,64]{0,2,1:T(8,128)(2,1)}, u32[]{:S(2)}, u32[]{:S(2)}) collective-permute-start(bf16[128,12,64]{0,2,1:T(8,128)(2,1)S(1)} %copy.84), channel_id=1, source_target_pairs={{28,0},{0,4},{4,8},{8,12},{12,16},{16,20},{20,24},{24,28},{29,1},{... | collective-permute-start | bytes 589832 | tf_op jit(solution)/shard_map/while/body/eval_jaxpr/ppermute | solution.py:17
  463.9 14.1 %collective-permute-start.1 = (bf16[128,12,64]{0,2,1:T(8,128)(2,1)S(1)}, bf16[128,12,64]{0,2,1:T(8,128)(2,1)S(1)}, u32[]{:S(2)}, u32[]{:S(2)}) collective-permute-start(bf16[128,12,64]{0,2,1:T(8,128)(2,1)S(1)} %copy.85), channel_id=1, source_target_pairs={{28,0},{0,4},{4,8},{8,12},{12,16},{16,20},{20,24},{24,28},{29,1},{... | collective-permute-start | bytes 589832 | tf_op jit(solution)/shard_map/while/body/eval_jaxpr/ppermute | solution.py:17
  479.0 15.0 %collective-permute-start = (bf16[128,12,64]{0,2,1:T(8,128)(2,1)S(1)}, bf16[128,12,64]{0,2,1:T(8,128)(2,1)}, u32[]{:S(2)}, u32[]{:S(2)}) collective-permute-start(bf16[128,12,64]{0,2,1:T(8,128)(2,1)S(1)} %copy.84), channel_id=1, source_target_pairs={{28,0},{0,4},{4,8},{8,12},{12,16},{16,20},{20,24},{24,28},{29,1},{... | collective-permute-start | bytes 589832 | tf_op jit(solution)/shard_map/while/body/eval_jaxpr/ppermute | solution.py:17
  479.0 15.0 %collective-permute-start.1 = (bf16[128,12,64]{0,2,1:T(8,128)(2,1)S(1)}, bf16[128,12,64]{0,2,1:T(8,128)(2,1)S(1)}, u32[]{:S(2)}, u32[]{:S(2)}) collective-permute-start(bf16[128,12,64]{0,2,1:T(8,128)(2,1)S(1)} %copy.85), channel_id=1, source_target_pairs={{28,0},{0,4},{4,8},{8,12},{12,16},{16,20},{20,24},{24,28},{29,1},{... | collective-permute-start | bytes 589832 | tf_op jit(solution)/shard_map/while/body/eval_jaxpr/ppermute | solution.py:17
  494.9 13.5 %collective-permute-start = (bf16[128,12,64]{0,2,1:T(8,128)(2,1)S(1)}, bf16[128,12,64]{0,2,1:T(8,128)(2,1)}, u32[]{:S(2)}, u32[]{:S(2)}) collective-permute-start(bf16[128,12,64]{0,2,1:T(8,128)(2,1)S(1)} %copy.84), channel_id=1, source_target_pairs={{28,0},{0,4},{4,8},{8,12},{12,16},{16,20},{20,24},{24,28},{29,1},{... | collective-permute-start | bytes 589832 | tf_op jit(solution)/shard_map/while/body/eval_jaxpr/ppermute | solution.py:17
  494.9 13.5 %collective-permute-start.1 = (bf16[128,12,64]{0,2,1:T(8,128)(2,1)S(1)}, bf16[128,12,64]{0,2,1:T(8,128)(2,1)S(1)}, u32[]{:S(2)}, u32[]{:S(2)}) collective-permute-start(bf16[128,12,64]{0,2,1:T(8,128)(2,1)S(1)} %copy.85), channel_id=1, source_target_pairs={{28,0},{0,4},{4,8},{8,12},{12,16},{16,20},{20,24},{24,28},{29,1},{... | collective-permute-start | bytes 589832 | tf_op jit(solution)/shard_map/while/body/eval_jaxpr/ppermute | solution.py:17
  511.2 58.0 %reduce-scatter.23.cloned.1.call-start = ((), (), s32[]{:S(2)}) async-start(), calls=%async_computation.19 | async-start | bytes 1474560
  513.2 86.9 %reduce-scatter.21.cloned.1.call-start = ((), (), s32[]{:S(2)}) async-start(), calls=%async_computation.18 | async-start | bytes 1474560
  515.3 114.8 %reduce-scatter.13.cloned.1.call-start = ((), (), s32[]{:S(2)}) async-start(), calls=%async_computation.14 | async-start | bytes 1474560 | tf_op jit(solution)/shard_map/reduce_scatter | solution.py:275
  516.9 199.6 %reduce-scatter.15.cloned.1.call-start = ((), (), s32[]{:S(2)}) async-start(), calls=%async_computation.15 | async-start | bytes 5898240 | tf_op jit(solution)/shard_map/reduce_scatter | solution.py:287
  520.7 283.8 %reduce-scatter.17.cloned.1.call-start = ((), (), s32[]{:S(2)}) async-start(), calls=%async_computation.16 | async-start | bytes 5898240 | tf_op jit(solution)/shard_map/reduce_scatter | solution.py:293
  (74 other events, 2841.7 us)
Sparse Core Ops, SparseCore 0:
  9.7 33.1 all-gather.12
  44.4 30.0 all-gather.16
  76.1 29.5 all-gather.10
  108.0 24.7 all-gather.14
  135.1 25.6 all-gather.18
  162.3 30.3 all-gather.20
  194.3 88.5 all-gather.22
  284.4 87.8 all-gather.24
  511.3 27.4 reduce-scatter.18
  541.0 28.1 reduce-scatter.22
  572.1 27.8 reduce-scatter.20
  602.2 27.8 reduce-scatter.12
  632.5 83.9 reduce-scatter.14
  718.6 85.7 reduce-scatter.16
where the time goes:
time: 974 us; the launch traced here: 971 us
  waiting for transfers between devices  562 us (58%)
  blocking collectives  215 us (22%)
  matrix products  73.4 us (8%)
  other arithmetic  40.6 us (4%)
  local copies, waits for them, and re-layouts  40.1 us (4%)
  starting transfers between devices  23.2 us (2%)
  between operations  16.8 us (2%)
    psum x1, blocking collectives, per_device(): lax.psum((s_wq, s_bq, s_wk, s_wv, s_bv, s_wo, s_bo, s_ga, s_sa, s_wi, s_b...  156 us
    all_gather x1, waiting for transfers between devices, per_device(): lax.all_gather(inner_weight, 'fsdp', axis=0, tiled=True)  88.2 us
    reduce_scatter x1, waiting for transfers between devices, per_device(): lax.psum_scatter(grad_w_outer.astype(jnp.bfloat16), 'fsdp', scatter_dimen...  88 us
    reduce_scatter x1, waiting for transfers between devices, per_device(): lax.psum_scatter(grad_w_inner.astype(jnp.bfloat16), 'fsdp', scatter_dimen...  86.3 us
    all_gather x1, waiting for transfers between devices, per_device(): lax.all_gather(outer_weight, 'fsdp', axis=0, tiled=True)  81.1 us
    unnamed x17, waiting for transfers between devices  39 us
    unnamed x2, blocking collectives  35.1 us
    ppermute x32, waiting for transfers between devices, passed_along(): return lax.ppermute(block, axis, route)  34.9 us
  transfers between devices with their start and end apart: 46, of which 29 were waited for; matrix products, arithmetic and copies ran while one was open for 13% of the time, Pallas kernels for 0%

commit v1 on v0

v1 whole, which is shorter than its diff:
```python
import functools

import jax
import jax.numpy as jnp
from jax import lax
from jax.experimental import pallas as pl
from jax.experimental.pallas import tpu as pltpu
from jax.sharding import PartitionSpec as P

HEAD_DIM = 64
NEGATIVE = -1000000000.0
EPSILON = 1e-12
LOW = jnp.bfloat16
WIDE = jnp.float32

CORE, SIDE, ROW = 1, 2, 4
TEAM = 8
CHIPS = 4
VMEM_BYTES = 56 << 20


def partner(block, axis, bit):
    devices = range(lax.axis_size(axis))
    return lax.ppermute(block, axis, [(i, i ^ bit) for i in devices])


def dot(left, right):
    return jnp.dot(left, right, preferred_element_type=WIDE)


def dot_rt(left, right):
    return lax.dot_general(left, right, (((1,), (1,)), ((), ())), preferred_element_type=WIDE)


def dot_lt(left, right):
    return lax.dot_general(left, right, (((0,), (0,)), ((), ())), preferred_element_type=WIDE)


def shape(dims, dtype=LOW):
    return jax.ShapeDtypeStruct(tuple(dims), dtype)


def kernel(body, outs, *args, scratch=(), flops=0):
    spec = pl.BlockSpec(memory_space=pltpu.VMEM)
    nbytes = sum(a.size * a.dtype.itemsize for a in args)
    nbytes += sum(functools.reduce(lambda m, n: m * n, o.shape, 1) * o.dtype.itemsize for o in outs)
    return pl.pallas_call(
        body,
        out_shape=list(outs),
        in_specs=[pl.BlockSpec(memory_space=pltpu.SMEM)] + [spec] * (len(args) - 1),
        out_specs=[spec] * len(outs),
        scratch_shapes=list(scratch),
        compiler_params=pltpu.CompilerParams(vmem_limit_bytes=VMEM_BYTES),
        cost_estimate=pl.CostEstimate(
            flops=int(flops), bytes_accessed=int(nbytes), transcendentals=0
        ),
    )(*args)


def places(where):
    index, place = where[0], where[1]
    core, side, row = index & 1, (index >> 1) & 1, (index >> 2) & 1
    return core, side, row, (index >> 1) & 3, place


def rows_from(start, count):
    return pl.ds(pl.multiple_of(start, 16), count)


def normalized(values):
    center = values - jnp.mean(values, -1, keepdims=True)
    inverse = lax.rsqrt(jnp.mean(center * center, -1, keepdims=True) + EPSILON)
    return center * inverse, inverse


def norm_back(grad, unit, inverse, gain):
    scaled = grad * gain
    return inverse * (
        scaled
        - jnp.mean(scaled, -1, keepdims=True)
        - unit * jnp.mean(scaled * unit, -1, keepdims=True)
    )


def prepare_first(where, x, seg, wq, wk, wv, bias, own, mine):
    core, _, _, chip, _ = places(where)
    tokens, width = x.shape[1:]
    part, half = width // 4, width // 8
    own[:tokens] = x[0]
    seg_row = jnp.broadcast_to(seg[...].astype(WIDE), (16, tokens)).astype(LOW)
    own[tokens:, :tokens] = seg_row
    own[tokens:, tokens:] = jnp.zeros((16, width - tokens), LOW)
    for j, weight in enumerate((wq, wk, wv)):
        block = weight[rows_from(core * half, half)]
        for k in range(CHIPS):

            @pl.when(chip == k)
            def _():
                mine[:half, j * part : (j + 1) * part] = block[:, k * part : (k + 1) * part]

    mine[half:] = bias[...]


def prepare_rest(where, wo, wi, wu, vectors, first, second):
    core, side, row, _, _ = places(where)
    part, width = wo.shape
    quarter = part // 4
    span = width // 2
    t = 2 * row + core
    first[:quarter] = wo[rows_from(t * quarter, quarter)]
    block = wi[rows_from(t * quarter, quarter)]
    for s in range(2):

        @pl.when(side == s)
        def _():
            for k in range(4):
                start = k * width + s * span
                at_row = quarter * (1 + k // 2)
                first[at_row : at_row + quarter, (k % 2) * span : (k % 2 + 1) * span] = block[
                    :, start : start + span
                ]

    first[3 * quarter :] = vectors[...]
    second[...] = wu[rows_from(side * span + t * (span // 4), span // 4)]


def assemble_first(where, wo, wi, vectors, *refs):
    pieces, (w_output, w_inner, vec, b_inner, stage) = refs[:12], refs[12:]
    core, side, row, _, place = places(where)
    part, width = wo.shape
    quarter, span = part // 4, width // 2
    stage[place] = vectors[...].astype(WIDE)
    for n, piece in enumerate(pieces):
        far_core, far_row, r = n // 6, (n // 3) % 2, n % 3 + 1
        k = place ^ r
        t = 2 * (row ^ far_row) + (core ^ far_core)
        base = rows_from(k * part + t * quarter, quarter)
        w_output[base] = piece[:quarter]
        w_inner[base, :width] = piece[quarter : 2 * quarter]
        w_inner[base, width:] = piece[2 * quarter : 3 * quarter]
        if n < 3:
            stage[k] = piece[3 * quarter :].astype(WIDE)
    base = rows_from(place * part, part)
    w_output[base] = wo[...]
    for s in range(2):

        @pl.when(side == s)
        def _():
            for k in range(4):
                start = k * width + s * span
                w_inner[base, k * span : (k + 1) * span] = wi[:, start : start + span]

    for k in range(4):
        block = stage[k]
        for i in range(6):
            line, start = divmod(i * part, width)
            vec[i : i + 1, k * part : (k + 1) * part] = block[line : line + 1, start : start + part]
        for s in range(2):

            @pl.when(side == s)
            def _():
                line, start = divmod(6 * part + s * span, width)
                b_inner[:, k * span : (k + 1) * span] = block[line : line + 1, start : start + span]

    vec[6:] = jnp.zeros((2, width), WIDE)


def assemble_second(where, wu, *refs):
    pieces, (w_outer,) = refs[:12], refs[12:]
    core, side, row, _, place = places(where)
    span = wu.shape[1] // 2
    for n, piece in enumerate(pieces):
        far_core, far_row, r = n // 6, (n // 3) % 2, n % 3 + 1
        t = 2 * (row ^ far_row) + (core ^ far_core)
        w_outer[rows_from((place ^ r) * span + t * (span // 4), span // 4)] = piece[...]
    w_outer[rows_from(place * span, span)] = wu[rows_from(side * span, span)]


def project(where, x0, x1, x2, x3, *refs):
    pieces, (rows_in, w_qkv, queries, keys_values, segs, stage) = refs[:8], refs[8:]
    core, _, _, chip, place = places(where)
    width = x0.shape[1]
    tokens = rows_in.shape[0] // CHIPS
    part, half = width // 4, width // 8
    for s, x in enumerate((x0, x1, x2, x3)):
        rows_in[s * tokens : (s + 1) * tokens] = x[:tokens]
        segs[s : s + 1] = x[tokens : tokens + 1, :tokens].astype(WIDE)
    segs[CHIPS:] = jnp.zeros((8 - CHIPS, tokens), WIDE)
    for n, piece in enumerate(pieces):
        far_core, r = n // 4, n % 4
        k = place ^ r
        w_qkv[rows_from(k * part + (core ^ far_core) * half, half)] = piece[:half]
        if n < 4:
            stage[k] = piece[half:].astype(WIDE)
    bias = stage[chip]
    out = dot(rows_in[...], w_qkv[...])
    scale = HEAD_DIM ** (-0.5)
    queries[...] = ((out[:, :part] + bias[:1, :part]).astype(LOW).astype(WIDE) * scale).astype(LOW)
    keys_values[:, :part] = out[:, part : 2 * part].astype(LOW)
    keys_values[:, part:] = (out[:, 2 * part :] + bias[:1, part : 2 * part]).astype(LOW)


def attend(queries, seg_query, keys_values, seg_key, context, probs):
    part = queries.shape[1]
    block = seg_key.shape[1]
    seg_columns = seg_key[...].T
    allowed = jnp.concatenate(
        [seg_columns[:, b : b + 1] == seg_query[...] for b in range(seg_key.shape[0])]
    )
    for h in range(part // HEAD_DIM):
        keys = keys_values[:, h * HEAD_DIM : (h + 1) * HEAD_DIM]
        values = keys_values[:, part + h * HEAD_DIM : part + (h + 1) * HEAD_DIM]
        scores = dot_rt(keys, queries[:, h * HEAD_DIM : (h + 1) * HEAD_DIM])
        scores = jnp.where(allowed, scores, NEGATIVE)
        weights = jnp.exp(scores - jnp.max(scores, 0, keepdims=True))
        weights = (weights * (1.0 / jnp.sum(weights, 0, keepdims=True))).astype(LOW)
        probs[h] = weights
        out = dot_lt(values, weights)
        context[:, h * HEAD_DIM : (h + 1) * HEAD_DIM] = out.T.astype(LOW)


def attend_back(queries, keys_values, grad_context, probs, grad_queries, grad_keys_values):
    part = queries.shape[1]
    first = pl.program_id(0) == 0

    @pl.when(first)
    def _():
        grad_keys_values[...] = jnp.zeros(grad_keys_values.shape, WIDE)

    scale = HEAD_DIM ** (-0.5)
    for h in range(part // HEAD_DIM):
        span = slice(h * HEAD_DIM, (h + 1) * HEAD_DIM)
        span_v = slice(part + h * HEAD_DIM, part + (h + 1) * HEAD_DIM)
        keys, values = keys_values[:, span], keys_values[:, span_v]
        grads = grad_context[:, span]
        soft = probs[h]
        grad_values = dot(soft, grads)
        grad_probs = dot_rt(values, grads)
        wide = soft.astype(WIDE)
        delta = jnp.sum(wide * grad_probs, 0, keepdims=True)
        grad_scores = (wide * (grad_probs - delta)).astype(LOW)
        grad_queries[:, span] = (dot_lt(keys, grad_scores) * scale).T.astype(LOW)
        grad_keys_values[:, span] += dot(grad_scores, queries[:, span])
        grad_keys_values[:, span_v] += grad_values


def attention_blocks(queries, keys_values):
    count, keys = queries.shape[0], keys_values.shape[0]
    return min(count, 128 * max(1, 2048 // keys))


def attention(queries, seg_query, keys_values, seg_key):
    count, part = queries.shape
    keys = keys_values.shape[0]
    heads = part // HEAD_DIM
    block = attention_blocks(queries, keys_values)
    whole = lambda a: pl.BlockSpec(a.shape, lambda i: (0,) * a.ndim)
    return pl.pallas_call(
        attend,
        grid=(count // block,),
        in_specs=[
            pl.BlockSpec((block, part), lambda i: (i, 0)),
            pl.BlockSpec((1, block), lambda i: (0, i)),
            whole(keys_values),
            whole(seg_key),
        ],
        out_specs=[
            pl.BlockSpec((block, part), lambda i: (i, 0)),
            pl.BlockSpec((heads, keys, block), lambda i: (0, 0, i)),
        ],
        out_shape=[shape((count, part)), shape((heads, keys, count))],
        compiler_params=pltpu.CompilerParams(vmem_limit_bytes=VMEM_BYTES),
        cost_estimate=pl.CostEstimate(
            flops=4 * count * keys * part, bytes_accessed=4 << 20, transcendentals=count * keys * 3
        ),
    )(queries, seg_query, keys_values, seg_key)


def attention_back(queries, keys_values, grad_context, probs):
    count, part = queries.shape
    keys = keys_values.shape[0]
    block = attention_blocks(queries, keys_values)
    whole = lambda a: pl.BlockSpec(a.shape, lambda i: (0,) * a.ndim)
    rows = pl.BlockSpec((block, part), lambda i: (i, 0))
    return pl.pallas_call(
        attend_back,
        grid=(count // block,),
        in_specs=[
            rows,
            whole(keys_values),
            rows,
            pl.BlockSpec((probs.shape[0], keys, block), lambda i: (0, 0, i)),
        ],
        out_specs=[rows, pl.BlockSpec((keys, 2 * part), lambda i: (0, 0))],
        out_shape=[shape((count, part)), shape((keys, 2 * part), WIDE)],
        compiler_params=pltpu.CompilerParams(vmem_limit_bytes=VMEM_BYTES),
        cost_estimate=pl.CostEstimate(
            flops=8 * count * keys * part, bytes_accessed=6 << 20, transcendentals=0
        ),
    )(queries, keys_values, grad_context, probs)


def swapped(block):
    tokens = block.shape[0] // 2
    return jnp.concatenate([block[tokens:], block[:tokens]])


def forward(where, c0, c1, c2, c3, rows_in, w_output, vec, w_inner, b_inner, w_outer, *outs):
    outer_part, context_low, unit_one, inverse_one, normed_low, activated, slope, stage = outs
    _, _, _, chip, _ = places(where)
    count, part = c0.shape
    stage[chip] = c0[...]
    stage[chip ^ 1] = swapped(c1[...])
    stage[chip ^ 2] = c2[...]
    stage[chip ^ 3] = swapped(c3[...])
    for k in range(CHIPS):
        context_low[:, k * part : (k + 1) * part] = stage[k]
    residual = rows_in[:count].astype(WIDE) + dot(context_low[...], w_output[...]) + vec[0:1]
    unit, inverse = normalized(residual)
    unit_one[...] = unit
    inverse_one[...] = inverse
    normed_low[...] = (unit * vec[1:2] + vec[2:3]).astype(LOW)
    inner_pre = dot(normed_low[...], w_inner[...]) + b_inner[...]
    cdf = 0.5 * (1.0 + lax.erf(inner_pre * (0.5**0.5)))
    activated[...] = (inner_pre * cdf).astype(LOW)
    slope[...] = cdf + inner_pre * jnp.exp(-0.5 * inner_pre * inner_pre) * 0.3989422804014327
    outer_part[...] = dot(activated[...], w_outer[...]).astype(LOW)


def backward(where, part_own, part_far, unit_one, vec, cot, cot_far, slope, w_outer, w_inner, *outs):
    result, grad_summed, grad_outer, grad_inner, inner_part, sums, sums_inner = outs
    tokens = cot.shape[1]
    summed = unit_one[...] * vec[1:2] + vec[2:3] + vec[3:4]
    summed += part_own[...].astype(WIDE) + swapped(part_far[...]).astype(WIDE)
    unit, inverse = normalized(summed)
    result[0] = (unit[:tokens] * vec[4:5] + vec[5:6]).astype(LOW)
    c = jnp.concatenate([cot[0], cot_far[...]]).astype(WIDE)
    grad = norm_back(c, unit, inverse, vec[4:5])
    grad_summed[...] = grad
    grad_outer[...] = grad.astype(LOW)
    grad_inner[...] = (dot_rt(grad_outer[...], w_outer[...]) * slope[...]).astype(LOW)
    inner_part[...] = dot_rt(grad_inner[...], w_inner[...]).astype(LOW)
    sums[0:1] = jnp.sum(grad_outer[...].astype(WIDE), 0, keepdims=True)
    sums[1:2] = jnp.sum(c * unit, 0, keepdims=True)
    sums[2:3] = jnp.sum(c, 0, keepdims=True)
    sums[3:] = jnp.zeros((5, sums.shape[1]), WIDE)
    sums_inner[...] = jnp.sum(grad_inner[...].astype(WIDE), 0, keepdims=True)


def weight_grads(where, left, right, keep, send, stage):
    core, _, row, _, place = places(where)
    stage[...] = dot_lt(left[...], right[...]).astype(LOW)
    part = stage.shape[0] // 4
    n = part // 4
    for r in range(4):
        for y in range(2):
            for c, out in enumerate((keep, send)):
                start = (place ^ r) * part + (2 * (row ^ y) + (core ^ c)) * n
                out[r, y, :n] = stage[rows_from(start, n)]


def norm_backward(where, grad_summed, part_own, part_far, unit_one, inverse_one, vec, w_output, *outs):
    grad_own, grad_low, grad_context, grad_context_row, sums = outs
    _, _, _, chip, _ = places(where)
    tokens = grad_own.shape[0]
    part = grad_context.shape[1]
    grad = grad_summed[...] + part_own[...].astype(WIDE) + swapped(part_far[...]).astype(WIDE)
    unit = unit_one[...]
    branch = norm_back(grad, unit, inverse_one[...], vec[1:2])
    grad_own[...] = branch[:tokens]
    grad_low[...] = branch.astype(LOW)
    grad_context[...] = dot_rt(grad_low[...], w_output[rows_from(chip * part, part)]).astype(LOW)
    grad_context_row[...] = dot_rt(
        grad_low[...], w_output[rows_from((chip ^ 2) * part, part)]
    ).astype(LOW)
    sums[0:1] = jnp.sum(grad_low[...].astype(WIDE), 0, keepdims=True)
    sums[1:2] = jnp.sum(grad * unit, 0, keepdims=True)
    sums[2:3] = jnp.sum(grad, 0, keepdims=True)
    sums[3:] = jnp.zeros((5, sums.shape[1]), WIDE)


def output_grads(where, context_low, grad_low, sums_one, sums_two, sums_inner, keep, send, stage):
    core, side, row, _, place = places(where)
    width = grad_low.shape[1]
    part, span = width // 4, width // 2
    n = part // 4
    for s in range(2):

        @pl.when(side == s)
        def _():
            stage[...] = dot_lt(
                context_low[...], grad_low[:, s * span : (s + 1) * span]
            ).astype(LOW)

    for r in range(4):
        for y in range(2):
            for c, out in enumerate((keep, send)):
                start = (place ^ r) * part + (2 * (row ^ y) + (core ^ c)) * n
                out[r, y, :n] = stage[rows_from(start, n)]
    for k in range(4):
        cut = slice(k * part, (k + 1) * part)
        small = jnp.concatenate(
            [
                jnp.concatenate([sums_one[0:1, cut], sums_one[1:2, cut]], 1),
                jnp.concatenate([sums_one[2:3, cut], sums_two[0:1, cut]], 1),
                jnp.concatenate([sums_two[1:2, cut], sums_two[2:3, cut]], 1),
                sums_inner[:, k * span : (k + 1) * span],
                jnp.zeros((12, span), WIDE),
            ]
        ).astype(LOW)
        for y in range(2):
            keep[place ^ k, y, n:] = small
            send[place ^ k, y, n:] = small


def input_grads(where, grad_queries, grad_kv, grad_kv_far, w_qkv, grad_residual, *outs):
    grad_qkv, own, s1, s2, s3 = outs
    part = grad_queries.shape[1]
    tokens = own.shape[0]
    grad_qkv[:, :part] = grad_queries[...]
    grad_qkv[:, part:] = (grad_kv[...] + grad_kv_far[...].astype(WIDE)).astype(LOW)
    grads = dot_rt(grad_qkv[...], w_qkv[...])
    own[...] = grad_residual[...] + grads[:tokens]
    for s, out in enumerate((s1, s2, s3)):
        out[...] = grads[(s + 1) * tokens : (s + 2) * tokens].astype(LOW)


def projection_grads(where, rows_in, grad_qkv, keep, send, stage):
    core, _, _, _, place = places(where)
    stage[...] = dot_lt(rows_in[...], grad_qkv[...]).astype(LOW)
    half = stage.shape[0] // 8
    total = jnp.sum(grad_qkv[...].astype(WIDE), 0, keepdims=True)
    total = jnp.broadcast_to(total, (16, total.shape[1])).astype(LOW)
    for r in range(4):
        for c, out in enumerate((keep, send)):
            start = (2 * (place ^ r) + (core ^ c)) * half
            out[r, :half] = stage[rows_from(start, half)]
            out[r, half:] = total


def add_rows(where, kept, received, keep, send):
    total = kept[...].astype(WIDE) + received[...].astype(WIDE)
    keep[...] = total[:, 0].astype(LOW)
    send[...] = total[:, 1].astype(LOW)


def add_near(where, kept, received, keep, send):
    total = kept[...].astype(WIDE) + received[...].astype(WIDE)
    for r in range(2):
        keep[r] = total[2 * r].astype(LOW)
        send[r] = total[2 * r + 1].astype(LOW)


def add_far(where, kept, received, keep, send):
    total = kept[...].astype(WIDE) + received[...].astype(WIDE)
    keep[...] = total[0].astype(LOW)
    send[...] = total[1].astype(LOW)


def add_last(where, kept, received, out):
    out[...] = (kept[...].astype(WIDE) + received[...].astype(WIDE)).astype(LOW)


def unpack_outer(where, *refs):
    pieces, (out,) = refs[:8], refs[8:]
    core, _, _, chip, _ = places(where)
    n = pieces[0].shape[0]
    for m, piece in enumerate(pieces):
        far = chip ^ (m % 4)
        start = ((far & 1) * 4 + 2 * (far >> 1) + (core ^ (m // 4))) * n
        out[rows_from(start, n)] = piece[...].astype(WIDE)


def unpack_inner(where, *refs):
    pieces, (out,) = refs[:8], refs[8:]
    core, side, _, chip, _ = places(where)
    n = pieces[0].shape[0]
    span = pieces[0].shape[1] // 4
    for m, piece in enumerate(pieces):
        far = chip ^ (m % 4)
        base = rows_from((2 * (far >> 1) + (core ^ (m // 4))) * n, n)
        for s in range(2):

            @pl.when((far & 1) == s)
            def _():
                for k in range(4):
                    start = (2 * k + s) * span
                    out[base, start : start + span] = piece[:, k * span : (k + 1) * span].astype(
                        WIDE
                    )


def unpack_output(where, *refs):
    pieces, (out, vec, bias, stage) = refs[:8], refs[8:]
    core, side, _, chip, _ = places(where)
    span = pieces[0].shape[1]
    n = pieces[0].shape[0] - 16
    part = span // 2
    for m, piece in enumerate(pieces):
        far = chip ^ (m % 4)
        base = rows_from((2 * (far >> 1) + (core ^ (m // 4))) * n, n)
        for s in range(2):

            @pl.when((far & 1) == s)
            def _():
                out[base, s * span : (s + 1) * span] = piece[:n].astype(WIDE)

    small = pieces[0][n:].astype(WIDE)
    for i in range(6):
        vec[i : i + 1] = small[i // 2 : i // 2 + 1, (i % 2) * part : (i % 2 + 1) * part]
    vec[6:] = jnp.zeros((2, part), WIDE)
    stage[side] = small
    stage[side ^ 1] = pieces[1][n:].astype(WIDE)
    for s in range(2):
        bias[:, s * span : (s + 1) * span] = stage[s, 3:4]


def unpack_projections(where, *refs):
    pieces, (out_q, out_k, out_v, bias, stage) = refs[:8], refs[8:]
    core, _, _, chip, place = places(where)
    half = pieces[0].shape[0] - 16
    part = 2 * half
    for m, piece in enumerate(pieces):
        stage[core ^ (m // 4), chip ^ (m % 4)] = piece[...]
    for c in range(2):
        for k in range(CHIPS):
            for j, out in enumerate((out_q, out_k, out_v)):
                out[c * half : (c + 1) * half, k * part : (k + 1) * part] = stage[
                    c, k, :half, j * part : (j + 1) * part
                ].astype(WIDE)
    small = stage[0, place][half:].astype(WIDE)
    for j in range(3):
        bias[j : j + 1] = small[:1, j * part : (j + 1) * part]
    bias[3:] = jnp.zeros((5, part), WIDE)


def per_device(
    inputs,
    segments,
    query_weight,
    query_bias,
    key_weight,
    value_weight,
    value_bias,
    output_weight,
    output_bias,
    first_gain,
    first_shift,
    inner_weight,
    inner_bias,
    outer_weight,
    outer_bias,
    second_gain,
    second_shift,
    cotangent,
):
    where = jnp.stack([lax.axis_index("ctx"), lax.axis_index("fsdp")]).astype(jnp.int32)
    groups = lax.axis_size("ctx") // TEAM
    lines = [[m + TEAM * g for g in range(groups)] for m in range(TEAM)]
    tokens, width = inputs.shape[1:]
    part = query_weight.shape[0]
    hidden = outer_weight.shape[0]
    count, pair = CHIPS * tokens, 2 * tokens
    half, quarter, span = part // 2, part // 4, hidden // 2

    biases = jnp.pad(jnp.concatenate([query_bias, value_bias])[None], ((0, 15), (0, part)))
    own, mine = kernel(
        prepare_first,
        [shape((tokens + 16, width)), shape((half + 16, 3 * part))],
        where,
        inputs,
        segments,
        query_weight,
        key_weight,
        value_weight,
        biases,
    )
    seen = [own] + [partner(own, "ctx", s << 1) for s in (1, 2, 3)]
    line = [mine] + [partner(mine, "fsdp", r) for r in (1, 2, 3)]
    line += [partner(piece, "ctx", CORE) for piece in line]

    vectors = jnp.concatenate(
        [output_bias, first_gain, first_shift, outer_bias, second_gain, second_shift, inner_bias]
    )
    vectors = jnp.pad(vectors, (0, 16 * width - vectors.shape[0])).reshape(16, width)
    first, second = kernel(
        prepare_rest,
        [shape((3 * quarter + 16, width)), shape((span // 4, width))],
        where,
        output_weight,
        inner_weight,
        outer_weight,
        vectors,
    )

    def gathered(piece):
        far, near = partner(piece, "fsdp", 2), partner(piece, "fsdp", 1)
        found = [near, far, partner(far, "fsdp", 1)]
        found += [partner(block, "ctx", ROW) for block in found]
        return found + [partner(block, "ctx", CORE) for block in found]

    w_output, w_inner, vec, b_inner = kernel(
        assemble_first,
        [
            shape((width, width)),
            shape((width, 4 * span)),
            shape((8, width), WIDE),
            shape((1, 4 * span), WIDE),
        ],
        where,
        output_weight,
        inner_weight,
        vectors,
        *gathered(first),
        scratch=[pltpu.VMEM((4, 16, width), WIDE)],
    )
    (w_outer,) = kernel(
        assemble_second, [shape((4 * span, width))], where, outer_weight, *gathered(second)
    )

    rows_in, w_qkv, queries, kv_own, segs = kernel(
        project,
        [
            shape((count, width)),
            shape((width, 3 * part)),
            shape((count, part)),
            shape((count, 2 * part)),
            shape((8, tokens), WIDE),
        ],
        where,
        *seen,
        *line,
        scratch=[pltpu.VMEM((4, 16, 3 * part), WIDE)],
        flops=6 * count * width * part,
    )
    segs = segs[:CHIPS]
    kv = jnp.concatenate([kv_own, partner(kv_own, "ctx", CORE)])
    seg_key = jnp.concatenate([segs, partner(segs, "ctx", CORE)])
    if groups > 1:
        kv = lax.all_gather(kv, "ctx", axis=0, tiled=True, axis_index_groups=lines)
        seg_key = lax.all_gather(seg_key, "ctx", axis=0, tiled=True, axis_index_groups=lines)
    context, probs = attention(queries, segs.reshape(1, count), kv, seg_key)

    c0, c_row = context[:pair], context[pair:]
    outer_part, context_low, unit_one, inverse_one, normed_low, activated, slope = kernel(
        forward,
        [
            shape((pair, width)),
            shape((pair, width)),
            shape((pair, width), WIDE),
            shape((pair, 1), WIDE),
            shape((pair, width)),
            shape((pair, 4 * span)),
            shape((pair, 4 * span), WIDE),
        ],
        where,
        c0,
        partner(c0, "ctx", SIDE),
        partner(c_row, "ctx", ROW),
        partner(c_row, "ctx", SIDE | ROW),
        rows_in,
        w_output,
        vec,
        w_inner,
        b_inner,
        w_outer,
        scratch=[pltpu.VMEM((CHIPS, pair, part), LOW)],
        flops=2 * pair * width * (width + 8 * span),
    )
    result, grad_summed, grad_outer, grad_inner, inner_part, sums_one, sums_inner = kernel(
        backward,
        [
            shape((1, tokens, width)),
            shape((pair, width), WIDE),
            shape((pair, width)),
            shape((pair, 4 * span)),
            shape((pair, width)),
            shape((8, width), WIDE),
            shape((1, 4 * span), WIDE),
        ],
        where,
        outer_part,
        partner(outer_part, "ctx", SIDE),
        unit_one,
        vec,
        cotangent,
        partner(cotangent[0], "ctx", SIDE),
        slope,
        w_outer,
        w_inner,
        flops=2 * pair * width * 8 * span,
    )
    inner_far = partner(inner_part, "ctx", SIDE)

    def grads_of(left, right):
        rows, columns = left.shape[1], right.shape[1]
        cut = shape((4, 2, rows // 16, columns))
        return kernel(
            weight_grads,
            [cut, cut],
            where,
            left,
            right,
            scratch=[pltpu.VMEM((rows, columns), LOW)],
            flops=2 * pair * rows * columns,
        )

    outer_kept, outer_sent = grads_of(activated, grad_outer)
    inner_kept, inner_sent = grads_of(normed_low, grad_inner)
    grad_residual, grad_low, grad_context, grad_context_row, sums_two = kernel(
        norm_backward,
        [
            shape((tokens, width), WIDE),
            shape((pair, width)),
            shape((pair, part)),
            shape((pair, part)),
            shape((8, width), WIDE),
        ],
        where,
        grad_summed,
        inner_part,
        inner_far,
        unit_one,
        inverse_one,
        vec,
        w_output,
        flops=4 * pair * width * part,
    )
    grad_context = jnp.concatenate([grad_context, partner(grad_context_row, "ctx", ROW)])
    cut = shape((4, 2, quarter + 16, width // 2))
    output_kept, output_sent = kernel(
        output_grads,
        [cut, cut],
        where,
        context_low,
        grad_low,
        sums_one,
        sums_two,
        sums_inner,
        scratch=[pltpu.VMEM((width, width // 2), LOW)],
        flops=pair * width * width,
    )
    grad_queries, grad_kv = attention_back(queries, kv, grad_context, probs)
    if groups > 1:
        grad_kv = grad_kv.reshape(groups, 2, count, 2 * part).transpose(1, 0, 2, 3)
        grad_kv = lax.psum_scatter(
            grad_kv.reshape(2, groups * count, 2 * part),
            "ctx",
            scatter_dimension=1,
            tiled=True,
            axis_index_groups=lines,
        ).reshape(2 * count, 2 * part)
    grad_kv_far = partner(grad_kv[count:].astype(LOW), "ctx", CORE)
    grad_qkv, grad_tokens, *grads_sent = kernel(
        input_grads,
        [shape((count, 3 * part)), shape((tokens, width), WIDE)] + [shape((tokens, width))] * 3,
        where,
        grad_queries,
        grad_kv[:count],
        grad_kv_far,
        w_qkv,
        grad_residual,
        flops=6 * count * width * part,
    )
    cut = shape((4, half + 16, 3 * part))
    qkv_kept, qkv_sent = kernel(
        projection_grads,
        [cut, cut],
        where,
        rows_in,
        grad_qkv,
        scratch=[pltpu.VMEM((width, 3 * part), LOW)],
        flops=6 * count * width * part,
    )
    for s, block in enumerate(grads_sent):
        grad_tokens = grad_tokens + partner(block, "ctx", (s + 1) << 1).astype(WIDE)

    def summed(kept, sent):
        received = partner(sent, "ctx", CORE)
        if kept.ndim == 4:
            kept, sent = kernel(add_rows, [shape(kept.shape[:1] + kept.shape[2:])] * 2, where, kept, received)
            received = partner(sent, "ctx", ROW)
        piece = kept.shape[1:]
        kept, sent = kernel(add_near, [shape((2,) + piece)] * 2, where, kept, received)
        received = partner(sent, "fsdp", 1)
        kept, sent = kernel(add_far, [shape(piece)] * 2, where, kept, received)
        (total,) = kernel(add_last, [shape(piece)], where, kept, partner(sent, "fsdp", 2))
        if groups > 1:
            total = lax.psum(total.astype(WIDE), "ctx", axis_index_groups=lines).astype(LOW)
        chips = [total] + [partner(total, "ctx", s << 1) for s in (1, 2, 3)]
        return chips + [partner(block, "ctx", CORE) for block in chips]

    (g_outer,) = kernel(
        unpack_outer, [shape((hidden, width), WIDE)], where, *summed(outer_kept, outer_sent)
    )
    (g_inner,) = kernel(
        unpack_inner, [shape((part, 4 * hidden), WIDE)], where, *summed(inner_kept, inner_sent)
    )
    g_output, g_vec, g_b_inner = kernel(
        unpack_output,
        [shape((part, width), WIDE), shape((8, part), WIDE), shape((1, hidden), WIDE)],
        where,
        *summed(output_kept, output_sent),
        scratch=[pltpu.VMEM((2, 16, width // 2), WIDE)],
    )
    g_query, g_key, g_value, g_bias = kernel(
        unpack_projections,
        [shape((part, width), WIDE)] * 3 + [shape((8, part), WIDE)],
        where,
        *summed(qkv_kept, qkv_sent),
        scratch=[pltpu.VMEM((2, CHIPS, half + 16, 3 * part), LOW)],
    )
    return (
        result,
        grad_tokens.astype(LOW)[None],
        g_query,
        g_bias[0],
        g_key,
        g_value,
        g_bias[2],
        g_output,
        g_vec[3],
        g_vec[4],
        g_vec[5],
        g_inner,
        g_b_inner[0],
        g_outer,
        g_vec[0],
        g_vec[1],
        g_vec[2],
    )


def solution(mesh):
    rows, cuts, whole = P("fsdp", "ctx", None), P("fsdp", None), P("fsdp")
    params = (cuts, whole, cuts, cuts, whole, cuts, whole, whole, whole)
    params += (cuts, whole, cuts, whole, whole, whole)
    return jax.shard_map(
        per_device,
        mesh=mesh,
        in_specs=(rows, P("fsdp", "ctx")) + params + (rows,),
        out_specs=(rows, rows) + params,
        check_vma=False,
    )
```

time: 974 us -> 279 us (0.29)
  waiting for transfers between devices: 562 us -> 57.6 us
  blocking collectives: 215 us -> 0 us
  Pallas kernels: 0 us -> 107 us
  matrix products: 73.4 us -> 0 us
  starting transfers between devices: 23.2 us -> 78.9 us
  other arithmetic: 40.6 us -> 4.95 us
  between operations: 16.8 us -> 1.57 us
  local copies, waits for them, and re-layouts: 40.1 us -> 28.2 us
    all_gather x8 -> x0, waiting for transfers between devices: 285 us -> none  [the longest x1 88.2 us: per_device(): lax.all_gather(inner_weight, 'fsdp', axis=0, tiled=True)]
    reduce_scatter x3 -> x0, waiting for transfers between devices: 203 us -> none  [the longest x1 88 us: per_device(): lax.psum_scatter(grad_w_outer.astype(jnp.bfloat16), 'fsdp', scatter_dimen...]
    psum x1 -> x0, blocking collectives: 156 us -> none  [per_device(): lax.psum((s_wq, s_bq, s_wk, s_wv, s_bv, s_wo, s_bo, s_ga, s_sa, s_wi, s_b...]
    pallas_call x0 -> x34, Pallas kernels: none -> 107 us  [the longest x32 89.7 us: kernel(): pl.pallas_call(body, out_shape=list(outs), in_specs=[pl.BlockSpec(memory_...]
    dot_general x60 -> x0, matrix products: 73.4 us -> none  [the longest x6 19.7 us: product(): return jnp.dot(leading, trailing, preferred_element_type=jnp.float32)]
    ppermute x32 -> x90, starting transfers between devices: 22.4 us -> 78.9 us  [partner(): return lax.ppermute(block, axis, [(i, i ^ bit) for i in devices])]
    unnamed x17 -> x0, waiting for transfers between devices: 39 us -> none
    unnamed x2 -> x0, blocking collectives: 35.1 us -> none
  transfers between devices with their start and end apart: 46 -> 90, of which waited for: 29 -> 17; matrix products, arithmetic and copies ran while one was open for 13% -> 5% of each run, Pallas kernels for 0% -> 32%
where the time goes in v1:
time: 279 us; the launch traced here: 278 us
  Pallas kernels  107 us (38%)
  starting transfers between devices  78.9 us (28%)
  waiting for transfers between devices  57.6 us (21%)
  local copies, waits for them, and re-layouts  28.2 us (10%)
  other arithmetic  4.95 us (2%)
    pallas_call x32, Pallas kernels, kernel(): pl.pallas_call(body, out_shape=list(outs), in_specs=[pl.BlockSpec(memory_...  89.7 us
    ppermute x90, starting transfers between devices, partner(): return lax.ppermute(block, axis, [(i, i ^ bit) for i in devices])  78.9 us
    ppermute x90, waiting for transfers between devices, partner(): return lax.ppermute(block, axis, [(i, i ^ bit) for i in devices])  57.6 us
    unnamed x189, local copies, waits for them, and re-layouts  14.2 us
    pallas_call x1, Pallas kernels, attention_back(): pl.pallas_call(attend_back, grid=(count // block,), in_specs=[rows, whole...  9.39 us
    pallas_call x1, Pallas kernels, attention(): pl.pallas_call(attend, grid=(count // block,), in_specs=[pl.BlockSpec((bl...  7.7 us
  transfers between devices with their start and end apart: 90, of which 17 were waited for; matrix products, arithmetic and copies ran while one was open for 5% of the time, Pallas kernels for 32%

profile of v1, /device:TPU:0, one launch (start us, length us, event | category | flops | bytes accessed | tf_op | source)
XLA Modules:
  0.0 278.0 jit_solution(17226221846391969779)
XLA Ops:
  0.7 4.8 %concatenate.18 = bf16[1920]{0:T(1024)(128)(2,1)S(1)} concatenate(bf16[192]{0:T(256)(128)(2,1)} %param.26, bf16[192]{0:T(256)(128)(2,1)} %param.27, bf16[192]{0:T(256)(128)(2,1)} %param.28, bf16[192]{0:T(256)(128)(2,1)} %param.32, bf16[192]{0:T(256)(128)(2,1)} %param.33, bf16[192]{0:T(256)(128)(2,1)} %param.34, bf16[768]{0:T(1024)(128)(2,1)} %param.30), dimensions={0} | concatenate | bytes 7680 | tf_op jit(solution)/shard_map/concatenate | solution.py:582
  6.7 2.5 shard_map.308
  9.2 4.0 %collective-permute-start.28 = (bf16[96,768]{1,0:T(8,128)(2,1)}, bf16[96,768]{1,0:T(8,128)(2,1)S(1)}, u32[]{:S(2)}, u32[]{:S(2)}) collective-permute-start(bf16[96,768]{1,0:T(8,128)(2,1)} %get-tuple-element.107), channel_id=1, source_target_pairs={{0,2},{1,3},{2,0},{3,1},{4,6},{5,7},{6,4},{7,5},{8,10},{9,11},{10,... | collective-permute-start | bytes 442376 | tf_op jit(solution)/shard_map/ppermute | solution.py:24
  20.5 2.5 collective-permute-start.2
  24.8 5.8 %collective-permute-start.27 = (bf16[96,768]{1,0:T(8,128)(2,1)}, bf16[96,768]{1,0:T(8,128)(2,1)S(1)}, u32[]{:S(2)}, u32[]{:S(2)}) collective-permute-start(bf16[96,768]{1,0:T(8,128)(2,1)} %get-tuple-element.107), channel_id=1, source_target_pairs={{0,1},{1,0},{2,3},{3,2},{4,5},{5,4},{6,7},{7,6},{8,9},{9,8},{10,11... | collective-permute-start | bytes 442376 | tf_op jit(solution)/shard_map/ppermute | solution.py:24
  36.0 4.1 %collective-permute-start.15 = (bf16[160,768]{1,0:T(8,128)(2,1)}, bf16[160,768]{1,0:T(8,128)(2,1)S(1)}, u32[]{:S(2)}, u32[]{:S(2)}) collective-permute-start(bf16[160,768]{1,0:T(8,128)(2,1)} %get-tuple-element.102), channel_id=1, source_target_pairs={{0,1},{1,0},{2,3},{3,2},{4,5},{5,4},{6,7},{7,6},{8,9},{9,8},{10,11... | collective-permute-start | bytes 737288 | tf_op jit(solution)/shard_map/ppermute | solution.py:24
  41.4 8.0 %collective-permute-done.16.refs_1_ = bf16[160,768]{1,0:T(8,128)(2,1)S(1)} collective-permute-done((bf16[160,768]{1,0:T(8,128)(2,1)}, bf16[160,768]{1,0:T(8,128)(2,1)S(1)}, u32[]{:S(2)}, u32[]{:S(2)}) %collective-permute-start.16) | collective-permute-done | bytes 245792 | tf_op jit(solution)/shard_map/ppermute | solution.py:24
  50.7 3.3 %shard_map.306 = (bf16[512,768]{1,0:T(8,128)(2,1)}, bf16[768,576]{1,0:T(8,128)(2,1)}, bf16[512,192]{1,0:T(8,128)(2,1)}, bf16[512,384]{1,0:T(8,128)(2,1)}, f32[8,128]{1,0:T(8,128)}) custom-call(s32[2]{0:T(128)} %pad_add_fusion.where, bf16[144,768]{1,0:T(8,128)(2,1)} %get-tuple-element.95.x0, bf16[144,768]{1,0:T(8,128)(2,1)} %copy-done.29, ...), custom_call_target="tpu_custom_call" | custom-call | flops 452984832 | bytes 4182024 | tf_op jit(solution)/shard_map/pallas_call | solution.py:47
  58.5 4.0 %collective-permute-done.30.refs_3_ = bf16[96,768]{1,0:T(8,128)(2,1)S(1)} collective-permute-done((bf16[96,768]{1,0:T(8,128)(2,1)S(1)}, bf16[96,768]{1,0:T(8,128)(2,1)S(1)}, u32[]{:S(2)}, u32[]{:S(2)}) %collective-permute-start.30) | collective-permute-done | bytes 147488 | tf_op jit(solution)/shard_map/ppermute | solution.py:24
  73.8 7.7 %shard_map.307 = (bf16[512,192]{1,0:T(8,128)(2,1)}, bf16[3,1024,512]{2,1,0:T(8,128)(2,1)}) custom-call(bf16[512,192]{1,0:T(8,128)(2,1)} %get-tuple-element.97.queries, f32[1,512]{1,0:T(1,128)} %bitcast.15, bf16[1024,384]{1,0:T(8,128)(2,1)} %copy-done, f32[8,128]{1,0:T(8,128)} %pad_maximum_fusion.1.seg_key), custom_call_target="tpu_custom_call" | custom-call | flops 402653184 | bytes 4194304 | tf_op jit(solution)/shard_map/pallas_call | solution.py:258
  88.2 3.4 %shard_map.310.w_outer = bf16[1536,768]{1,0:T(8,128)(2,1)} custom-call(s32[2]{0:T(128)} %pad_add_fusion.where, bf16[768,768]{1,0:T(8,128)(2,1)} %wu.3, bf16[96,768]{1,0:T(8,128)(2,1)} %copy-done.34, bf16[96,768]{1,0:T(8,128)(2,1)} %copy-done.33, bf16[96,768]{1,0:T(8,128)(2,1)} %copy-done.37, bf16[96,768]{1,0:T(8,128)(2,1)} %copy-done.39, ...), custom_call_target="tpu_custom_call" | custom-call | bytes 5308424 | tf_op jit(solution)/shard_map/pallas_call | solution.py:47
  93.1 4.8 %shard_map.309 = (bf16[768,768]{1,0:T(8,128)(2,1)}, bf16[768,1536]{1,0:T(8,128)(2,1)}, f32[8,768]{1,0:T(8,128)}, f32[1,1536]{1,0:T(1,128)}) custom-call(s32[2]{0:T(128)} %pad_add_fusion.where, bf16[192,768]{1,0:T(8,128)(2,1)} %wo.3, bf16[192,3072]{1,0:T(8,128)(2,1)} %wi.3, bf16[16,768]{1,0:T(8,128)(2,1)} %reshape.41.vectors, bf16[160,768]{1,0:T(8,128)(2,1)} %copy-done.16, ...), custom_call_target="tpu_custom_call" | custom-call | bytes 8017928 | tf_op jit(solution)/shard_map/pallas_call | solution.py:47
  98.6 6.9 %shard_map.311 = (bf16[256,768]{1,0:T(8,128)(2,1)}, bf16[256,768]{1,0:T(8,128)(2,1)}, f32[256,768]{1,0:T(8,128)}, f32[256,1]{1,0:T(8,128)}, bf16[256,768]{1,0:T(...) custom-call(s32[2]{0:T(128)} %pad_add_fusion.where, bf16[256,192]{1,0:T(8,128)(2,1)} %copy-done.6, ...), custom_call_target="tpu_custom_call" | custom-call | flops 1509949440 | bytes 11435016 | tf_op jit(solution)/shard_map/pallas_call | solution.py:47
  107.6 13.0 %collective-permute-done.40.cot_far = bf16[128,768]{1,0:T(8,128)(2,1)S(1)} collective-permute-done((bf16[128,768]{1,0:T(8,128)(2,1)S(1)}, bf16[128,768]{1,0:T(8,128)(2,1)S(1)}, u32[]{:S(2)}, u32[]{:S(2)}) %collective-permute-start.40) | collective-permute-done | bytes 196640 | tf_op jit(solution)/shard_map/ppermute | solution.py:24
  121.4 6.5 %shard_map.312 = (bf16[1,128,768]{2,1,0:T(8,128)(2,1)}, f32[256,768]{1,0:T(8,128)}, bf16[256,768]{1,0:T(8,128)(2,1)}, bf16[256,1536]{1,0:T(8,128)(2,1)}, bf16[25...) custom-call(s32[2]{0:T(128)} %pad_add_fusion.where, bf16[256,768]{1,0:T(8,128)(2,1)} %get-tuple-element.108.part_own, ...), custom_call_target="tpu_custom_call" | custom-call | flops 1207959552 | bytes 10868744 | tf_op jit(solution)/shard_map/pallas_call | solution.py:47
  128.6 3.7 %shard_map.333 = (bf16[4,2,96,768]{3,2,1,0:T(8,128)(2,1)}, bf16[4,2,96,768]{3,2,1,0:T(8,128)(2,1)}) custom-call(s32[2]{0:T(128)} %pad_add_fusion.where, bf16[256,1536]{1,0:T(8,128)(2,1)} %get-tuple-element.163.left, bf16[256,768]{1,0:T(8,128)(2,1)} %get-tuple-element.164.right), custom_call_target="tpu_custom_call" | custom-call | flops 603979776 | bytes 3538952 | tf_op jit(solution)/shard_map/pallas_call | solution.py:47
  132.2 3.6 %shard_map.327 = (bf16[4,2,48,1536]{3,2,1,0:T(8,128)(2,1)}, bf16[4,2,48,1536]{3,2,1,0:T(8,128)(2,1)}) custom-call(s32[2]{0:T(128)} %pad_add_fusion.where, bf16[256,768]{1,0:T(8,128)(2,1)} %get-tuple-element.152.left, bf16[256,1536]{1,0:T(8,128)(2,1)} %get-tuple-element.153.right), custom_call_target="tpu_custom_call" | custom-call | flops 603979776 | bytes 3538952 | tf_op jit(solution)/shard_map/pallas_call | solution.py:47
  138.6 3.6 %shard_map.313 = (f32[128,768]{1,0:T(8,128)}, bf16[256,768]{1,0:T(8,128)(2,1)}, bf16[256,192]{1,0:T(8,128)(2,1)}, bf16[256,192]{1,0:T(8,128)(2,1)}, f32[8,768]{1,0:T(8,128)}) custom-call(s32[2]{0:T(128)} %pad_add_fusion.where, f32[256,768]{1,0:T(8,128)} %get-tuple-element.112.grad_summed, bf16[256,768]{1,0:T(8,128)(2,1)} %get-tuple-element.113.part_own, ...), custom_call_target="tpu_custom_call" | custom-call | flops 150994944 | bytes 4572168 | tf_op jit(solution)/shard_map/pallas_call | solution.py:47
  143.9 3.6 %collective-permute-done.42 = bf16[256,192]{1,0:T(8,128)(2,1)S(1)} collective-permute-done((bf16[256,192]{1,0:T(8,128)(2,1)}, bf16[256,192]{1,0:T(8,128)(2,1)S(1)}, u32[]{:S(2)}, u32[]{:S(2)}) %collective-permute-start.42) | collective-permute-done | bytes 98336 | tf_op jit(solution)/shard_map/ppermute | solution.py:24
  149.1 9.4 %shard_map.314 = (bf16[512,192]{1,0:T(8,128)(2,1)}, f32[1024,384]{1,0:T(8,128)}) custom-call(bf16[512,192]{1,0:T(8,128)(2,1)} %get-tuple-element.97.queries, bf16[1024,384]{1,0:T(8,128)(2,1)} %copy-done, bf16[512,192]{1,0:T(8,128)(2,1)} %pad_maximum_fusion.grad_context, bf16[3,1024,512]{2,1,0:T(8,128)(2,1)} %get-tuple-element.117.probs), custom_call_target="tpu_custom_call" | custom-call | flops 805306368 | bytes 6291456 | tf_op jit(solution)/shard_map/pallas_call | solution.py:285
  162.5 3.4 %shard_map.315 = (bf16[512,576]{1,0:T(8,128)(2,1)}, f32[128,768]{1,0:T(8,128)}, bf16[128,768]{1,0:T(8,128)(2,1)}, bf16[128,768]{1,0:T(8,128)(2,1)}, bf16[128,768]{1,0:T(8,128)(2,1)}) custom-call(s32[2]{0:T(128)} %pad_add_fusion.where, bf16[512,192]{1,0:T(8,128)(2,1)} %get-tuple-element.118.grad_queries, f32[512,384]{1,0:T(8,128)} %slice.43.grad_kv, ...), custom_call_target="tpu_custom_call" | custom-call | flops 452984832 | bytes 4227080 | tf_op jit(solution)/shard_map/pallas_call | solution.py:47
  166.0 3.2 %shard_map.316 = (bf16[4,112,576]{2,1,0:T(8,128)(2,1)}, bf16[4,112,576]{2,1,0:T(8,128)(2,1)}) custom-call(s32[2]{0:T(128)} %pad_add_fusion.where, bf16[512,768]{1,0:T(8,128)(2,1)} %get-tuple-element.101.rows_in, bf16[512,576]{1,0:T(8,128)(2,1)} %get-tuple-element.126.grad_qkv), custom_call_target="tpu_custom_call" | custom-call | flops 452984832 | bytes 2408456 | tf_op jit(solution)/shard_map/pallas_call | solution.py:47
  170.7 2.8 shard_map.334
  175.1 2.6 shard_map.321
  178.7 2.8 %shard_map.328 = (bf16[4,48,1536]{2,1,0:T(8,128)(2,1)}, bf16[4,48,1536]{2,1,0:T(8,128)(2,1)}) custom-call(s32[2]{0:T(128)} %pad_add_fusion.where, bf16[4,2,48,1536]{3,2,1,0:T(8,128)(2,1)} %get-tuple-element.154.kept, bf16[4,2,48,1536]{3,2,1,0:T(8,128)(2,1)} %copy-done.1), custom_call_target="tpu_custom_call" | custom-call | bytes 3538952 | tf_op jit(solution)/shard_map/pallas_call | solution.py:47
  194.9 10.9 %collective-permute-done.58.received = bf16[4,64,384]{2,1,0:T(8,128)(2,1)S(1)} collective-permute-done((bf16[4,64,384]{2,1,0:T(8,128)(2,1)}, bf16[4,64,384]{2,1,0:T(8,128)(2,1)S(1)}, u32[]{:S(2)}, u32[]{:S(2)}) %collective-permute-start.58) | collective-permute-done | bytes 196640 | tf_op jit(solution)/shard_map/ppermute | solution.py:24
  219.4 2.5 collective-permute-done.60.received
  221.9 2.8 %collective-permute-start.49 = (bf16[112,576]{1,0:T(8,128)(2,1)}, bf16[112,576]{1,0:T(8,128)(2,1)S(1)}, u32[]{:S(2)}, u32[]{:S(2)}) collective-permute-start(bf16[112,576]{1,0:T(8,128)(2,1)} %get-tuple-element.132), channel_id=1, source_target_pairs={{0,2},{1,3},{2,0},{3,1},{4,6},{5,7},{6,4},{7,5},{8,10},{9,11},{10,... | collective-permute-start | bytes 387080 | tf_op jit(solution)/shard_map/ppermute | solution.py:24
  240.3 2.4 collective-permute-start.71
  263.9 2.8 %shard_map.320 = (f32[192,768]{1,0:T(8,128)}, f32[192,768]{1,0:T(8,128)}, f32[192,768]{1,0:T(8,128)}, f32[8,192]{1,0:T(8,128)}) custom-call(s32[2]{0:T(128)} %pad_add_fusion.where, bf16[112,576]{1,0:T(8,128)(2,1)} %shard_map.319.refs_0_, bf16[112,576]{1,0:T(8,128)(2,1)} %copy-done.71, bf16[112,576]{1,0:T(8,128)(2,1)} %copy-done.70, ...), custom_call_target="tpu_custom_call" | custom-call | bytes 2807816 | tf_op jit(solution)/shard_map/pallas_call | solution.py:47
  270.7 2.9 %shard_map.338 = f32[768,768]{1,0:T(8,128)} custom-call(s32[2]{0:T(128)} %pad_add_fusion.where, bf16[96,768]{1,0:T(8,128)(2,1)} %shard_map.337.refs_0_, bf16[96,768]{1,0:T(8,128)(2,1)} %copy-done.50, bf16[96,768]{1,0:T(8,128)(2,1)} %copy-done.49, bf16[96,768]{1,0:T(8,128)(2,1)} %copy-done.48, bf16[96,768]{1,0:T(8,128)(2,1)} %copy-done.47, ...), custom_call_target="tpu_custom_call" | custom-call | bytes 3538952 | tf_op jit(solution)/shard_map/pallas_call | solution.py:47
  275.1 3.0 %shard_map.332 = f32[192,3072]{1,0:T(8,128)} custom-call(s32[2]{0:T(128)} %pad_add_fusion.where, bf16[48,1536]{1,0:T(8,128)(2,1)} %shard_map.331.refs_0_, bf16[48,1536]{1,0:T(8,128)(2,1)} %copy-done.53, bf16[48,1536]{1,0:T(8,128)(2,1)} %copy-done.52, bf16[48,1536]{1,0:T(8,128)(2,1)} %copy-done.51, bf16[48,1536]{1,0:T(8,128)(2,1)} %copy-done.56, ...), custom_call_target="tpu_custom_call" | custom-call | bytes 3538952 | tf_op jit(solution)/shard_map/pallas_call | solution.py:47
  (389 shorter events, 129.2 us)
Async XLA Ops:
  9.2 26.7 %collective-permute-start.28 = (bf16[96,768]{1,0:T(8,128)(2,1)}, bf16[96,768]{1,0:T(8,128)(2,1)S(1)}, u32[]{:S(2)}, u32[]{:S(2)}) collective-permute-start(bf16[96,768]{1,0:T(8,128)(2,1)} %get-tuple-element.107), channel_id=1, source_target_pairs={{0,2},{1,3},{2,0},{3,1},{4,6},{5,7},{6,4},{7,5},{8,10},{9,11},{10,... | collective-permute-start | bytes 442376 | tf_op jit(solution)/shard_map/ppermute | solution.py:24
  17.5 15.4 %collective-permute-start.4 = (bf16[112,576]{1,0:T(8,128)(2,1)}, bf16[112,576]{1,0:T(8,128)(2,1)S(1)}, u32[]{:S(2)}, u32[]{:S(2)}) collective-permute-start(bf16[112,576]{1,0:T(8,128)(2,1)} %get-tuple-element.96.refs_0_), channel_id=1, source_target_pairs={{0,2},{1,3},{2,0},{3,1},{4,6},{5,7},{6,4},{7,5},{8,10},{9,11},{10,... | collective-permute-start | bytes 387080 | tf_op jit(solution)/shard_map/ppermute | solution.py:24
  19.2 15.3 %collective-permute-start.3 = (bf16[112,576]{1,0:T(8,128)(2,1)}, bf16[112,576]{1,0:T(8,128)(2,1)S(1)}, u32[]{:S(2)}, u32[]{:S(2)}) collective-permute-start(bf16[112,576]{1,0:T(8,128)(2,1)} %get-tuple-element.96.refs_0_), channel_id=1, source_target_pairs={{0,1},{1,0},{2,3},{3,2},{4,5},{5,4},{6,7},{7,6},{8,9},{9,8},{10,11... | collective-permute-start | bytes 387080 | tf_op jit(solution)/shard_map/ppermute | solution.py:24
  20.5 19.5 %collective-permute-start.2 = (bf16[144,768]{1,0:T(8,128)(2,1)}, bf16[144,768]{1,0:T(8,128)(2,1)S(1)}, u32[]{:S(2)}, u32[]{:S(2)}) collective-permute-start(bf16[144,768]{1,0:T(8,128)(2,1)} %get-tuple-element.95.x0), channel_id=1, source_target_pairs={{0,24},{4,28},{8,16},{12,20},{16,8},{20,12},{24,0},{28,4},{1,25},{... | collective-permute-start | bytes 663560 | tf_op jit(solution)/shard_map/ppermute | solution.py:24
  35.9 13.4 %collective-permute-start.16 = (bf16[160,768]{1,0:T(8,128)(2,1)}, bf16[160,768]{1,0:T(8,128)(2,1)S(1)}, u32[]{:S(2)}, u32[]{:S(2)}) collective-permute-start(bf16[160,768]{1,0:T(8,128)(2,1)} %get-tuple-element.102), channel_id=1, source_target_pairs={{0,2},{1,3},{2,0},{3,1},{4,6},{5,7},{6,4},{7,5},{8,10},{9,11},{10,... | collective-permute-start | bytes 737288 | tf_op jit(solution)/shard_map/ppermute | solution.py:24
  36.0 18.7 %collective-permute-start.15 = (bf16[160,768]{1,0:T(8,128)(2,1)}, bf16[160,768]{1,0:T(8,128)(2,1)S(1)}, u32[]{:S(2)}, u32[]{:S(2)}) collective-permute-start(bf16[160,768]{1,0:T(8,128)(2,1)} %get-tuple-element.102), channel_id=1, source_target_pairs={{0,1},{1,0},{2,3},{3,2},{4,5},{5,4},{6,7},{7,6},{8,9},{9,8},{10,11... | collective-permute-start | bytes 737288 | tf_op jit(solution)/shard_map/ppermute | solution.py:24
  57.4 13.4 %collective-permute-start.10 = (bf16[512,384]{1,0:T(8,128)(2,1)}, bf16[512,384]{1,0:T(8,128)(2,1)S(1)}, u32[]{:S(2)}, u32[]{:S(2)}) collective-permute-start(bf16[512,384]{1,0:T(8,128)(2,1)} %get-tuple-element.99), channel_id=1, source_target_pairs={{0,4},{4,0},{8,12},{12,8},{16,20},{20,16},{24,28},{28,24},{1,5},{5... | collective-permute-start | bytes 1179656 | tf_op jit(solution)/shard_map/ppermute | solution.py:24
  67.7 13.9 %collective-permute-start.21 = (bf16[160,768]{1,0:T(8,128)(2,1)S(1)}, bf16[160,768]{1,0:T(8,128)(2,1)S(1)}, u32[]{:S(2)}, u32[]{:S(2)}) collective-permute-start(bf16[160,768]{1,0:T(8,128)(2,1)S(1)} %collective-permute-done.15.refs_0_), channel_id=1, source_target_pairs={{0,4},{4,0},{8,12},{12,8},{16,20},{20,16},{24,28},{28,24},{1,5},{5... | collective-permute-start | bytes 737288 | tf_op jit(solution)/shard_map/ppermute | solution.py:24
  69.2 12.9 %collective-permute-start.18 = (bf16[160,768]{1,0:T(8,128)(2,1)S(1)}, bf16[160,768]{1,0:T(8,128)(2,1)S(1)}, u32[]{:S(2)}, u32[]{:S(2)}) collective-permute-start(bf16[160,768]{1,0:T(8,128)(2,1)S(1)} %collective-permute-done.15.refs_0_), channel_id=1, source_target_pairs={{0,16},{4,20},{8,24},{12,28},{16,0},{20,4},{24,8},{28,12},{1,17},{... | collective-permute-start | bytes 737288 | tf_op jit(solution)/shard_map/ppermute | solution.py:24
  70.8 12.7 %collective-permute-start.20 = (bf16[160,768]{1,0:T(8,128)(2,1)S(1)}, bf16[160,768]{1,0:T(8,128)(2,1)S(1)}, u32[]{:S(2)}, u32[]{:S(2)}) collective-permute-start(bf16[160,768]{1,0:T(8,128)(2,1)S(1)} %collective-permute-done.17.refs_2_), channel_id=1, source_target_pairs={{0,16},{4,20},{8,24},{12,28},{16,0},{20,4},{24,8},{28,12},{1,17},{... | collective-permute-start | bytes 737288 | tf_op jit(solution)/shard_map/ppermute | solution.py:24
  72.0 14.6 %collective-permute-start.23 = (bf16[160,768]{1,0:T(8,128)(2,1)S(1)}, bf16[160,768]{1,0:T(8,128)(2,1)S(1)}, u32[]{:S(2)}, u32[]{:S(2)}) collective-permute-start(bf16[160,768]{1,0:T(8,128)(2,1)S(1)} %collective-permute-done.17.refs_2_), channel_id=1, source_target_pairs={{0,4},{4,0},{8,12},{12,8},{16,20},{20,16},{24,28},{28,24},{1,5},{5... | collective-permute-start | bytes 737288 | tf_op jit(solution)/shard_map/ppermute | solution.py:24
  73.8 12.5 %collective-permute-start.25 = (bf16[160,768]{1,0:T(8,128)(2,1)S(1)}, bf16[160,768]{1,0:T(8,128)(2,1)S(1)}, u32[]{:S(2)}, u32[]{:S(2)}) collective-permute-start(bf16[160,768]{1,0:T(8,128)(2,1)S(1)} %collective-permute-done.19.refs_4_), channel_id=1, source_target_pairs={{0,4},{4,0},{8,12},{12,8},{16,20},{20,16},{24,28},{28,24},{1,5},{5... | collective-permute-start | bytes 737288 | tf_op jit(solution)/shard_map/ppermute | solution.py:24
  84.6 13.3 %collective-permute-start.14 = (bf16[256,192]{1,0:T(8,128)(2,1)S(1)}, bf16[256,192]{1,0:T(8,128)(2,1)S(1)}, u32[]{:S(2)}, u32[]{:S(2)}) collective-permute-start(bf16[256,192]{1,0:T(8,128)(2,1)S(1)} %get-tuple-element.173), channel_id=1, source_target_pairs={{0,24},{4,28},{8,16},{12,20},{16,8},{20,12},{24,0},{28,4},{1,25},{... | collective-permute-start | bytes 294920 | tf_op jit(solution)/shard_map/ppermute | solution.py:24
  86.3 11.6 %collective-permute-start.13 = (bf16[256,192]{1,0:T(8,128)(2,1)S(1)}, bf16[256,192]{1,0:T(8,128)(2,1)S(1)}, u32[]{:S(2)}, u32[]{:S(2)}) collective-permute-start(bf16[256,192]{1,0:T(8,128)(2,1)S(1)} %get-tuple-element.173), channel_id=1, source_target_pairs={{0,16},{4,20},{8,24},{12,28},{16,0},{20,4},{24,8},{28,12},{1,17},{... | collective-permute-start | bytes 294920 | tf_op jit(solution)/shard_map/ppermute | solution.py:24
  86.6 11.3 %collective-permute-start.12 = (bf16[256,192]{1,0:T(8,128)(2,1)S(1)}, bf16[256,192]{1,0:T(8,128)(2,1)S(1)}, u32[]{:S(2)}, u32[]{:S(2)}) collective-permute-start(bf16[256,192]{1,0:T(8,128)(2,1)S(1)} %get-tuple-element.174.c0), channel_id=1, source_target_pairs={{0,8},{4,12},{8,0},{12,4},{16,24},{20,28},{24,16},{28,20},{1,9},{5... | collective-permute-start | bytes 294920 | tf_op jit(solution)/shard_map/ppermute | solution.py:24
  105.5 15.1 %collective-permute-start.39 = (bf16[256,768]{1,0:T(8,128)(2,1)}, bf16[256,768]{1,0:T(8,128)(2,1)S(1)}, u32[]{:S(2)}, u32[]{:S(2)}) collective-permute-start(bf16[256,768]{1,0:T(8,128)(2,1)} %get-tuple-element.108.part_own), channel_id=1, source_target_pairs={{0,8},{4,12},{8,0},{12,4},{16,24},{20,28},{24,16},{28,20},{1,9},{5... | collective-permute-start | bytes 1179656 | tf_op jit(solution)/shard_map/ppermute | solution.py:24
  106.1 14.5 %collective-permute-start.40 = (bf16[128,768]{1,0:T(8,128)(2,1)S(1)}, bf16[128,768]{1,0:T(8,128)(2,1)S(1)}, u32[]{:S(2)}, u32[]{:S(2)}) collective-permute-start(bf16[128,768]{1,0:T(8,128)(2,1)S(1)} %bitcast.14), channel_id=1, source_target_pairs={{0,8},{4,12},{8,0},{12,4},{16,24},{20,28},{24,16},{28,20},{1,9},{5... | collective-permute-start | bytes 589832 | tf_op jit(solution)/shard_map/ppermute | solution.py:24
  132.2 37.5 %collective-permute-start.79 = (bf16[4,2,96,768]{3,2,1,0:T(8,128)(2,1)}, bf16[4,2,96,768]{3,2,1,0:T(8,128)(2,1)S(1)}, u32[]{:S(2)}, u32[]{:S(2)}) collective-permute-start(bf16[4,2,96,768]{3,2,1,0:T(8,128)(2,1)} %get-tuple-element.166), channel_id=1, source_target_pairs={{0,4},{4,0},{8,12},{12,8},{16,20},{20,16},{24,28},{28,24},{1,5},{5... | collective-permute-start | bytes 3538952 | tf_op jit(solution)/shard_map/ppermute | solution.py:24
  135.8 41.9 %collective-permute-start.68 = (bf16[4,2,48,1536]{3,2,1,0:T(8,128)(2,1)}, bf16[4,2,48,1536]{3,2,1,0:T(8,128)(2,1)S(1)}, u32[]{:S(2)}, u32[]{:S(2)}) collective-permute-start(bf16[4,2,48,1536]{3,2,1,0:T(8,128)(2,1)} %get-tuple-element.155), channel_id=1, source_target_pairs={{0,4},{4,0},{8,12},{12,8},{16,20},{20,16},{24,28},{28,24},{1,5},{5... | collective-permute-start | bytes 3538952 | tf_op jit(solution)/shard_map/ppermute | solution.py:24
  169.2 17.7 %collective-permute-start.47 = (bf16[4,112,576]{2,1,0:T(8,128)(2,1)}, bf16[4,112,576]{2,1,0:T(8,128)(2,1)S(1)}, u32[]{:S(2)}, u32[]{:S(2)}) collective-permute-start(bf16[4,112,576]{2,1,0:T(8,128)(2,1)} %get-tuple-element.128), channel_id=1, source_target_pairs={{0,4},{4,0},{8,12},{12,8},{16,20},{20,16},{24,28},{28,24},{1,5},{5... | collective-permute-start | bytes 1548296 | tf_op jit(solution)/shard_map/ppermute | solution.py:24
  173.5 17.6 %collective-permute-start.80 = (bf16[4,96,768]{2,1,0:T(8,128)(2,1)}, bf16[4,96,768]{2,1,0:T(8,128)(2,1)S(1)}, u32[]{:S(2)}, u32[]{:S(2)}) collective-permute-start(bf16[4,96,768]{2,1,0:T(8,128)(2,1)} %get-tuple-element.168), channel_id=1, source_target_pairs={{0,16},{4,20},{8,24},{12,28},{16,0},{20,4},{24,8},{28,12},{1,17},{... | collective-permute-start | bytes 1769480 | tf_op jit(solution)/shard_map/ppermute | solution.py:24
  181.5 29.4 %collective-permute-start.69 = (bf16[4,48,1536]{2,1,0:T(8,128)(2,1)}, bf16[4,48,1536]{2,1,0:T(8,128)(2,1)S(1)}, u32[]{:S(2)}, u32[]{:S(2)}) collective-permute-start(bf16[4,48,1536]{2,1,0:T(8,128)(2,1)} %get-tuple-element.157), channel_id=1, source_target_pairs={{0,16},{4,20},{8,24},{12,28},{16,0},{20,4},{24,8},{28,12},{1,17},{... | collective-permute-start | bytes 1769480 | tf_op jit(solution)/shard_map/ppermute | solution.py:24
  184.6 21.2 %collective-permute-start.58 = (bf16[4,64,384]{2,1,0:T(8,128)(2,1)}, bf16[4,64,384]{2,1,0:T(8,128)(2,1)S(1)}, u32[]{:S(2)}, u32[]{:S(2)}) collective-permute-start(bf16[4,64,384]{2,1,0:T(8,128)(2,1)} %get-tuple-element.145), channel_id=1, source_target_pairs={{0,16},{4,20},{8,24},{12,28},{16,0},{20,4},{24,8},{28,12},{1,17},{... | collective-permute-start | bytes 589832 | tf_op jit(solution)/shard_map/ppermute | solution.py:24
  186.3 23.3 %collective-permute-start.44 = (bf16[128,768]{1,0:T(8,128)(2,1)S(1)}, bf16[128,768]{1,0:T(8,128)(2,1)S(1)}, u32[]{:S(2)}, u32[]{:S(2)}) collective-permute-start(bf16[128,768]{1,0:T(8,128)(2,1)S(1)} %copy-done.93), channel_id=1, source_target_pairs={{0,8},{4,12},{8,0},{12,4},{16,24},{20,28},{24,16},{28,20},{1,9},{5... | collective-permute-start | bytes 589832 | tf_op jit(solution)/shard_map/ppermute | solution.py:24
  189.9 26.6 %collective-permute-start.48 = (bf16[2,112,576]{2,1,0:T(8,128)(2,1)}, bf16[2,112,576]{2,1,0:T(8,128)(2,1)S(1)}, u32[]{:S(2)}, u32[]{:S(2)}) collective-permute-start(bf16[2,112,576]{2,1,0:T(8,128)(2,1)} %get-tuple-element.130), channel_id=1, source_target_pairs={{0,1},{1,0},{2,3},{3,2},{4,5},{5,4},{6,7},{7,6},{8,9},{9,8},{10,11... | collective-permute-start | bytes 774152 | tf_op jit(solution)/shard_map/ppermute | solution.py:24
  194.0 34.6 %collective-permute-start.81 = (bf16[2,96,768]{2,1,0:T(8,128)(2,1)}, bf16[2,96,768]{2,1,0:T(8,128)(2,1)S(1)}, u32[]{:S(2)}, u32[]{:S(2)}) collective-permute-start(bf16[2,96,768]{2,1,0:T(8,128)(2,1)} %get-tuple-element.170), channel_id=1, source_target_pairs={{0,1},{1,0},{2,3},{3,2},{4,5},{5,4},{6,7},{7,6},{8,9},{9,8},{10,11... | collective-permute-start | bytes 884744 | tf_op jit(solution)/shard_map/ppermute | solution.py:24
  209.5 16.6 %collective-permute-start.45 = (bf16[128,768]{1,0:T(8,128)(2,1)S(1)}, bf16[128,768]{1,0:T(8,128)(2,1)S(1)}, u32[]{:S(2)}, u32[]{:S(2)}) collective-permute-start(bf16[128,768]{1,0:T(8,128)(2,1)S(1)} %copy-done.92), channel_id=1, source_target_pairs={{0,16},{4,20},{8,24},{12,28},{16,0},{20,4},{24,8},{28,12},{1,17},{... | collective-permute-start | bytes 589832 | tf_op jit(solution)/shard_map/ppermute | solution.py:24
  211.0 15.2 %collective-permute-start.46 = (bf16[128,768]{1,0:T(8,128)(2,1)S(1)}, bf16[128,768]{1,0:T(8,128)(2,1)S(1)}, u32[]{:S(2)}, u32[]{:S(2)}) collective-permute-start(bf16[128,768]{1,0:T(8,128)(2,1)S(1)} %copy-done.91), channel_id=1, source_target_pairs={{0,24},{4,28},{8,16},{12,20},{16,8},{20,12},{24,0},{28,4},{1,25},{... | collective-permute-start | bytes 589832 | tf_op jit(solution)/shard_map/ppermute | solution.py:24
  214.0 23.8 %collective-permute-start.70 = (bf16[2,48,1536]{2,1,0:T(8,128)(2,1)}, bf16[2,48,1536]{2,1,0:T(8,128)(2,1)S(1)}, u32[]{:S(2)}, u32[]{:S(2)}) collective-permute-start(bf16[2,48,1536]{2,1,0:T(8,128)(2,1)} %get-tuple-element.159), channel_id=1, source_target_pairs={{0,1},{1,0},{2,3},{3,2},{4,5},{5,4},{6,7},{7,6},{8,9},{9,8},{10,11... | collective-permute-start | bytes 884744 | tf_op jit(solution)/shard_map/ppermute | solution.py:24
  231.9 12.7 %collective-permute-start.82 = (bf16[96,768]{1,0:T(8,128)(2,1)}, bf16[96,768]{1,0:T(8,128)(2,1)S(1)}, u32[]{:S(2)}, u32[]{:S(2)}) collective-permute-start(bf16[96,768]{1,0:T(8,128)(2,1)} %get-tuple-element.172), channel_id=1, source_target_pairs={{0,2},{1,3},{2,0},{3,1},{4,6},{5,7},{6,4},{7,5},{8,10},{9,11},{10,... | collective-permute-start | bytes 442376 | tf_op jit(solution)/shard_map/ppermute | solution.py:24
  240.3 11.6 %collective-permute-start.71 = (bf16[48,1536]{1,0:T(8,128)(2,1)}, bf16[48,1536]{1,0:T(8,128)(2,1)S(1)}, u32[]{:S(2)}, u32[]{:S(2)}) collective-permute-start(bf16[48,1536]{1,0:T(8,128)(2,1)} %get-tuple-element.161), channel_id=1, source_target_pairs={{0,2},{1,3},{2,0},{3,1},{4,6},{5,7},{6,4},{7,5},{8,10},{9,11},{10,... | collective-permute-start | bytes 442376 | tf_op jit(solution)/shard_map/ppermute | solution.py:24
  249.2 12.0 %collective-permute-start.85 = (bf16[96,768]{1,0:T(8,128)(2,1)}, bf16[96,768]{1,0:T(8,128)(2,1)S(1)}, u32[]{:S(2)}, u32[]{:S(2)}) collective-permute-start(bf16[96,768]{1,0:T(8,128)(2,1)} %shard_map.337.refs_0_), channel_id=1, source_target_pairs={{0,24},{4,28},{8,16},{12,20},{16,8},{20,12},{24,0},{28,4},{1,25},{... | collective-permute-start | bytes 442376 | tf_op jit(solution)/shard_map/ppermute | solution.py:24
  (152 other events, 1363.3 us)

commit v2 on v1

v2 whole, which is shorter than its diff:
```python
import functools

import jax
import jax.numpy as jnp
from jax import lax
from jax.experimental import pallas as pl
from jax.experimental.pallas import tpu as pltpu
from jax.sharding import PartitionSpec as P

HEAD_DIM = 64
NEGATIVE = -1000000000.0
EPSILON = 1e-12
LOW = jnp.bfloat16
WIDE = jnp.float32

CORE, SIDE, ROW = 1, 2, 4
TEAM = 8
CHIPS = 4
VMEM_BYTES = 56 << 20


def partner(block, axis, bit):
    devices = range(lax.axis_size(axis))
    return lax.ppermute(block, axis, [(i, i ^ bit) for i in devices])


def dot(left, right):
    return jnp.dot(left, right, preferred_element_type=WIDE)


def dot_rt(left, right):
    return lax.dot_general(left, right, (((1,), (1,)), ((), ())), preferred_element_type=WIDE)


def dot_lt(left, right):
    return lax.dot_general(left, right, (((0,), (0,)), ((), ())), preferred_element_type=WIDE)


def shape(dims, dtype=LOW):
    return jax.ShapeDtypeStruct(tuple(dims), dtype)


def kernel(body, outs, *args, scratch=(), room=8, last=(), after=(), loads=0):
    spec = pl.BlockSpec(memory_space=pltpu.VMEM)
    off = pl.BlockSpec(memory_space=pl.ANY)
    place = pltpu.HBM if loads else pltpu.VMEM
    args = tuple(pltpu.with_memory_space_constraint(a, place) for a in args)
    waits = len(after)

    def step(*refs):
        body(*refs[waits:])

    sems = [pltpu.SemaphoreType.DMA((loads,))] if loads else []
    return pl.pallas_call(
        step,
        out_shape=[
            o if n in last else pltpu.VMEM(o.shape, o.dtype) for n, o in enumerate(outs)
        ],
        in_specs=[off] * waits + [off if loads else spec] * len(args),
        out_specs=[spec] * len(outs),
        scratch_shapes=list(scratch) + sems,
        compiler_params=pltpu.CompilerParams(vmem_limit_bytes=room << 20),
        cost_estimate=pl.CostEstimate(flops=1, bytes_accessed=1, transcendentals=0),
    )(*after, *args)


def load(sems, *pairs):
    copies = [
        pltpu.make_async_copy(source, target, sems.at[n])
        for n, (source, target) in enumerate(pairs)
    ]
    for copy in copies:
        copy.start()
    return copies


def places():
    index, place = lax.axis_index("ctx"), lax.axis_index("fsdp")
    core, side, row = index & 1, (index >> 1) & 1, (index >> 2) & 1
    return core, side, row, (index >> 1) & 3, place


def rows_from(start, count):
    return pl.ds(pl.multiple_of(start, 16), count)


def normalized(values):
    center = values - jnp.mean(values, -1, keepdims=True)
    inverse = lax.rsqrt(jnp.mean(center * center, -1, keepdims=True) + EPSILON)
    return center * inverse, inverse


def norm_back(grad, unit, inverse, gain):
    scaled = grad * gain
    return inverse * (
        scaled
        - jnp.mean(scaled, -1, keepdims=True)
        - unit * jnp.mean(scaled * unit, -1, keepdims=True)
    )


def lines_of(*vectors):
    rows = [v[...].astype(WIDE).reshape(1, v.shape[0]) for v in vectors]
    return jnp.concatenate(rows + [jnp.zeros((16 - len(rows), rows[0].shape[1]), WIDE)])


def prepare_tokens(x, seg, own, line, sems):
    tokens, width = x.shape[1:]
    for copy in load(sems, (seg, line), (x.at[0], own.at[pl.ds(0, tokens)])):
        copy.wait()
    seg_row = jnp.broadcast_to(line[...].astype(WIDE), (16, tokens)).astype(LOW)
    own[tokens:, :tokens] = seg_row
    own[tokens:, tokens:] = jnp.zeros((16, width - tokens), LOW)


def prepare_weights(wq, wk, wv, wo, wi, wu, *refs):
    vectors, first, (blocks, block), lines, sems = (
        refs[:9],
        refs[9],
        refs[10:12],
        refs[12:21],
        refs[21],
    )
    core, _, _, chip, _ = places()
    part, width = wq.shape
    half = part // 2
    rows = rows_from(core * half, half)
    pairs = [(w.at[rows], blocks.at[j]) for j, w in enumerate((wq, wk, wv))]
    pairs += [(wi.at[rows], block), (wo.at[rows], first.at[pl.ds(half, half)])]
    rows = rows_from((2 * chip + core) * half, half)
    pairs += [(wu.at[rows], first.at[pl.ds(3 * half, half)])]
    for copy in load(sems, *pairs, *zip(vectors, lines)):
        copy.wait()
    six, bias_inner, biases = lines_of(*lines[:6]), lines_of(lines[6]), lines_of(*lines[7:])
    for p in range(CHIPS):

        @pl.when(chip == p)
        def _():
            span = slice(p * part, (p + 1) * part)
            for j in range(3):
                first[:half, j * part : (j + 1) * part] = blocks[j, :, span]
            for k in range(4):
                start = k * width + p * part
                first[2 * half : 3 * half, k * part : (k + 1) * part] = block[
                    :, start : start + part
                ]
            small = [six[:6], bias_inner[:1, span], biases[:2], jnp.zeros((half - 9, part), WIDE)]
            first[:half, 3 * part :] = jnp.concatenate(small).astype(LOW)


def first_rows(block, out):
    out[...] = block[: out.shape[0]]


def passed(block, out):
    out[...] = block[...]


def sort_pieces(own, near, far, farthest, projections, others, sent):
    half = farthest.shape[0]
    for r, piece in enumerate((own, near, far, farthest)):
        projections[r] = piece[:half]
    for r, piece in enumerate((own, near, far)):
        others[r] = piece[half:]
    sent[...] = far[half:]


def assemble(own, own_last, other, other_last, *weights):
    core, _, _, _, place = places()
    half = weights[0].shape[0] // 8
    for c, (pieces, last) in enumerate(((own, own_last), (other, other_last))):
        for r in range(4):
            piece = last if r == 3 else pieces.at[r]
            base = rows_from((2 * (place ^ r) + (core ^ c)) * half, half)
            for m, weight in enumerate(weights):
                weight[base] = piece[m * half : (m + 1) * half]


def project(seen, *refs):
    pieces, outs = refs[:2], refs[2:]
    rows_in, w_qkv, queries, keys_values, segs, vec, b_inner, stage = outs
    core, _, _, chip, place = places()
    width = seen.shape[2]
    tokens = rows_in.shape[0] // CHIPS
    part, half = width // 4, width // 8
    for s in range(CHIPS):
        x = seen.at[chip ^ s]
        rows_in[s * tokens : (s + 1) * tokens] = x[:tokens]
        segs[s : s + 1] = x[tokens : tokens + 1, :tokens].astype(WIDE)
    segs[CHIPS:] = jnp.zeros((8 - CHIPS, tokens), WIDE)
    for r in range(4):
        for c, piece in enumerate(pieces):
            base = rows_from((2 * (place ^ r) + (core ^ c)) * half, half)
            w_qkv[base] = piece[r, :, : 3 * part]
        stage[place ^ r] = pieces[0][r, :16, 3 * part :].astype(WIDE)
    for k in range(4):
        span = slice(k * part, (k + 1) * part)
        vec[:6, span] = stage[k, :6]
        b_inner[:, span] = stage[k, 6:7]
    vec[6:] = jnp.zeros((2, width), WIDE)
    bias = stage[chip]
    out = dot(rows_in[...], w_qkv[...])
    scale = HEAD_DIM ** (-0.5)
    queries[...] = ((out[:, :part] + bias[7:8]).astype(LOW).astype(WIDE) * scale).astype(LOW)
    keys_values[:, :part] = out[:, part : 2 * part].astype(LOW)
    keys_values[:, part:] = (out[:, 2 * part :] + bias[8:9]).astype(LOW)


def attend(queries, seg_query, keys_values, seg_key, context, probs):
    part = queries.shape[1]
    seg_columns = seg_key[...].T
    seg_row = seg_query[...]
    allowed = jnp.concatenate(
        [seg_columns[:, b : b + 1] == seg_row for b in range(seg_key.shape[0])]
    )
    for h in range(part // HEAD_DIM):
        keys = keys_values[:, h * HEAD_DIM : (h + 1) * HEAD_DIM]
        values = keys_values[:, part + h * HEAD_DIM : part + (h + 1) * HEAD_DIM]
        scores = dot_rt(keys, queries[:, h * HEAD_DIM : (h + 1) * HEAD_DIM])
        scores = jnp.where(allowed, scores, NEGATIVE)
        weights = jnp.exp(scores - jnp.max(scores, 0, keepdims=True))
        weights = (weights * (1.0 / jnp.sum(weights, 0, keepdims=True))).astype(LOW)
        probs[h] = weights
        out = dot_lt(values, weights)
        context[:, h * HEAD_DIM : (h + 1) * HEAD_DIM] = out.T.astype(LOW)


def attend_back(queries, keys_values, grad_context, probs, grad_queries, grad_keys_values):
    part = queries.shape[1]
    scale = HEAD_DIM ** (-0.5)
    for h in range(part // HEAD_DIM):
        span = slice(h * HEAD_DIM, (h + 1) * HEAD_DIM)
        span_v = slice(part + h * HEAD_DIM, part + (h + 1) * HEAD_DIM)
        keys, values = keys_values[:, span], keys_values[:, span_v]
        grads = grad_context[:, span]
        soft = probs[h]
        grad_keys_values[:, span_v] += dot(soft, grads)
        grad_probs = dot_rt(values, grads)
        wide = soft.astype(WIDE)
        delta = jnp.sum(wide * grad_probs, 0, keepdims=True)
        grad_scores = (wide * (grad_probs - delta)).astype(LOW)
        grad_queries[:, span] = (dot_lt(keys, grad_scores) * scale).T.astype(LOW)
        grad_keys_values[:, span] += dot(grad_scores, queries[:, span])


def attend_all(queries, kv_own, kv_far, seg_own, seg_far, context, probs, *scratch):
    keys_values, seg_key, seg_query = scratch
    count = kv_own.shape[0]
    tokens = seg_own.shape[1]
    keys_values[:count] = kv_own[...]
    keys_values[count:] = kv_far[...]
    seg_key[:CHIPS] = seg_own[:CHIPS]
    seg_key[CHIPS:] = seg_far[:CHIPS]
    for s in range(CHIPS):
        seg_query[:, s * tokens : (s + 1) * tokens] = seg_own[s : s + 1]
    attend(queries, seg_query, keys_values, seg_key, context, probs)


def context_back(g0, g1, g2, g3, w_output, grad_low, grad_context):
    _, _, _, chip, _ = places()
    tokens, part = g0.shape[0], grad_context.shape[1]
    for s, block in enumerate((g0, g1, g2, g3)):
        grad_low[s * tokens : (s + 1) * tokens] = block[...]
    grad_context[...] = dot_rt(grad_low[...], w_output[rows_from(chip * part, part)]).astype(LOW)


def attend_back_all(queries, kv_own, kv_far, g0, g1, g2, g3, w_output, probs, *refs):
    grad_low, grad_queries, grad_own, grad_far, keys_values, grad_context, total = refs
    count = kv_own.shape[0]
    keys_values[:count] = kv_own[...]
    keys_values[count:] = kv_far[...]
    context_back(g0, g1, g2, g3, w_output, grad_low, grad_context)
    total[...] = jnp.zeros(total.shape, WIDE)
    attend_back(queries, keys_values, grad_context, probs, grad_queries, total)
    grad_own[...] = total[:count]
    grad_far[...] = total[count:].astype(LOW)


def attend_back_block(queries, keys_values, grads, probs, grad_queries, grad_keys_values):
    @pl.when(pl.program_id(0) == 0)
    def _():
        grad_keys_values[...] = jnp.zeros(grad_keys_values.shape, WIDE)

    attend_back(queries, keys_values, grads, probs, grad_queries, grad_keys_values)


def attention_block(queries, keys_values):
    return min(queries.shape[0], 128 * max(1, 2048 // keys_values.shape[0]))


def whole(array):
    return pl.BlockSpec(array.shape, lambda i: (0,) * array.ndim)


def attention(queries, seg_query, keys_values, seg_key):
    count, part = queries.shape
    keys = keys_values.shape[0]
    heads = part // HEAD_DIM
    block = attention_block(queries, keys_values)
    return pl.pallas_call(
        attend,
        grid=(count // block,),
        in_specs=[
            pl.BlockSpec((block, part), lambda i: (i, 0)),
            pl.BlockSpec((1, block), lambda i: (0, i)),
            whole(keys_values),
            whole(seg_key),
        ],
        out_specs=[
            pl.BlockSpec((block, part), lambda i: (i, 0)),
            pl.BlockSpec((heads, keys, block), lambda i: (0, 0, i)),
        ],
        out_shape=[shape((count, part)), shape((heads, keys, count))],
        compiler_params=pltpu.CompilerParams(vmem_limit_bytes=VMEM_BYTES),
    )(queries, seg_query, keys_values, seg_key)


def attention_back(queries, keys_values, grad_context, probs):
    count, part = queries.shape
    keys = keys_values.shape[0]
    block = attention_block(queries, keys_values)
    rows = pl.BlockSpec((block, part), lambda i: (i, 0))
    return pl.pallas_call(
        attend_back_block,
        grid=(count // block,),
        in_specs=[
            rows,
            whole(keys_values),
            rows,
            pl.BlockSpec((probs.shape[0], keys, block), lambda i: (0, 0, i)),
        ],
        out_specs=[rows, pl.BlockSpec((keys, 2 * part), lambda i: (0, 0))],
        out_shape=[shape((count, part)), shape((keys, 2 * part), WIDE)],
        compiler_params=pltpu.CompilerParams(vmem_limit_bytes=VMEM_BYTES),
    )(queries, keys_values, grad_context, probs)


def forward(c0, c1, c2, c3, rows_in, w_output, vec, w_inner, b_inner, w_outer, *outs):
    context_low, unit_one, inverse_one, normed_low, activated, slope = outs[:6]
    own, sent, stage = outs[6], outs[7:10], outs[10]
    _, _, _, chip, _ = places()
    count, part = c0.shape
    tokens = count // CHIPS
    for s, block in enumerate((c0, c1, c2, c3)):
        for t in range(CHIPS):
            stage[chip ^ s, t * tokens : (t + 1) * tokens] = block[
                (t ^ s) * tokens : ((t ^ s) + 1) * tokens
            ]
    for k in range(CHIPS):
        context_low[:, k * part : (k + 1) * part] = stage[k]
    residual = rows_in[...].astype(WIDE) + dot(context_low[...], w_output[...]) + vec[0:1]
    unit, inverse = normalized(residual)
    unit_one[...] = unit[:tokens]
    inverse_one[...] = inverse[:tokens]
    normed_low[...] = (unit * vec[1:2] + vec[2:3]).astype(LOW)
    inner_pre = dot(normed_low[...], w_inner[...]) + b_inner[...]
    cdf = 0.5 * (1.0 + lax.erf(inner_pre * (0.5**0.5)))
    activated[...] = (inner_pre * cdf).astype(LOW)
    slope[...] = cdf + inner_pre * jnp.exp(-0.5 * inner_pre * inner_pre) * 0.3989422804014327
    parted(dot(activated[...], w_outer[...]), own, sent)


def parted(values, own, sent):
    tokens = own.shape[0]
    own[...] = values[:tokens]
    for s, out in enumerate(sent):
        out[...] = values[(s + 1) * tokens : (s + 2) * tokens].astype(LOW)


def total_of(own, blocks):
    total = own[...]
    for block in blocks:
        total = total + block[...].astype(WIDE)
    return total


def backward_first(own, s1, s2, s3, unit_one, vec, cot, result, grad_summed, grad_outer, sums):
    summed = unit_one[...] * vec[1:2] + vec[2:3] + vec[3:4] + total_of(own, (s1, s2, s3))
    unit, inverse = normalized(summed)
    result[0] = (unit * vec[4:5] + vec[5:6]).astype(LOW)
    c = cot[0].astype(WIDE)
    grad = norm_back(c, unit, inverse, vec[4:5])
    grad_summed[...] = grad
    grad_outer[...] = grad.astype(LOW)
    sums[0:1] = jnp.sum(grad_outer[...].astype(WIDE), 0, keepdims=True)
    sums[1:2] = jnp.sum(c * unit, 0, keepdims=True)
    sums[2:3] = jnp.sum(c, 0, keepdims=True)
    sums[3:] = jnp.zeros((5, sums.shape[1]), WIDE)


def backward_second(g0, g1, g2, g3, slope, w_outer, w_inner, grad_outer, grad_inner, sums, *outs):
    tokens = g0.shape[0]
    for s, block in enumerate((g0, g1, g2, g3)):
        grad_outer[s * tokens : (s + 1) * tokens] = block[...]
    grad_inner[...] = (dot_rt(grad_outer[...], w_outer[...]) * slope[...]).astype(LOW)
    parted(dot_rt(grad_inner[...], w_inner[...]), outs[0], outs[1:])
    sums[...] = jnp.sum(grad_inner[...].astype(WIDE), 0, keepdims=True)


def weight_grads(activated, grad_outer, normed_low, grad_inner, keep, send, stage):
    core, _, _, _, place = places()
    half = keep.shape[1] // 2
    for m, (left, right) in enumerate(((activated, grad_outer), (normed_low, grad_inner))):
        stage[...] = dot_lt(left[...], right[...]).astype(LOW)
        for r in range(4):
            for c, out in enumerate((keep, send)):
                start = (2 * (place ^ r) + (core ^ c)) * half
                out[r, m * half : (m + 1) * half] = stage[rows_from(start, half)]


def norm_backward(grad_summed, own, s1, s2, s3, unit_one, inverse_one, vec, grad_own, grad_low, sums):
    grad = grad_summed[...] + total_of(own, (s1, s2, s3))
    unit = unit_one[...]
    branch = norm_back(grad, unit, inverse_one[...], vec[1:2])
    grad_own[...] = branch
    grad_low[...] = branch.astype(LOW)
    sums[0:1] = jnp.sum(grad_low[...].astype(WIDE), 0, keepdims=True)
    sums[1:2] = jnp.sum(grad * unit, 0, keepdims=True)
    sums[2:3] = jnp.sum(grad, 0, keepdims=True)
    sums[3:] = jnp.zeros((5, sums.shape[1]), WIDE)


def output_grads(context_low, grad_low, out):
    _, _, _, chip, _ = places()
    part = out.shape[1]
    for p in range(CHIPS):

        @pl.when(chip == p)
        def _():
            block = grad_low[:, p * part : (p + 1) * part]
            out[...] = dot_lt(context_low[...], block).astype(LOW)


def projection_grads(
    rows_in, grad_queries, grad_kv, grad_kv_far, grad_o, sums_one, sums_two, sums_inner, *outs
):
    grad_qkv, keep, send, stage = outs
    core, _, _, _, place = places()
    part = grad_queries.shape[1]
    width = 4 * part
    grad_qkv[:, :part] = grad_queries[...]
    grad_qkv[:, part:] = (grad_kv[...] + grad_kv_far[...].astype(WIDE)).astype(LOW)
    stage[:, : 3 * part] = dot_lt(rows_in[...], grad_qkv[...]).astype(LOW)
    stage[:, 3 * part :] = grad_o[...]
    half = part // 2
    total = jnp.sum(grad_qkv[...].astype(WIDE), 0, keepdims=True)
    for k in range(4):
        span = slice(k * part, (k + 1) * part)
        small = jnp.concatenate(
            [
                sums_one[:3, span],
                sums_two[:3, span],
                sums_inner[:, span],
                total[:, :part],
                total[:, 2 * part :],
                jnp.zeros((7, part), WIDE),
            ]
        )
        small = jnp.concatenate([small, jnp.zeros((16, width - part), WIDE)], 1).astype(LOW)
        for c, out in enumerate((keep, send)):
            out[place ^ k, half:] = small
            out[place ^ k, :half] = stage[rows_from(k * part + (core ^ c) * half, half)]


def input_grads(grad_qkv, w_qkv, grad_residual, own, s1, s2, s3):
    tokens = own.shape[0]
    grads = dot_rt(grad_qkv[...], w_qkv[...])
    parted(grads, own, (s1, s2, s3))
    own[...] += grad_residual[...]


def add_tokens(own, s1, s2, s3, out):
    out[0] = total_of(own, (s1, s2, s3)).astype(LOW)


def add_near(kept, received, keep, send):
    total = kept[...].astype(WIDE) + received[...].astype(WIDE)
    for r in range(2):
        keep[r] = total[2 * r].astype(LOW)
        send[r] = total[2 * r + 1].astype(LOW)


def add_near_both(kept, received, *outs):
    half = outs[0].shape[1]
    for m in range(2):
        rows = pl.ds(m * half, half)
        add_near(kept.at[:, rows], received.at[:, rows], *outs[2 * m : 2 * m + 2])


def add_far(kept, received, keep, send):
    total = kept[...].astype(WIDE) + received[...].astype(WIDE)
    keep[...] = total[0].astype(LOW)
    send[...] = total[1].astype(LOW)


def add_far_passing(kept, received, other, keep, send, out):
    add_far(kept, received, keep, send)
    out[...] = other[...]


def add_last(kept, received, out):
    out[...] = (kept[...].astype(WIDE) + received[...].astype(WIDE)).astype(LOW)


def unpack_mlp(*refs):
    pieces, blocks, (outer, inner, stage) = refs[:8], refs[8:16], refs[16:]
    core, _, _, chip, _ = places()
    half, width = pieces[0].shape
    part = 2 * half
    for i, (piece, block) in enumerate(zip(pieces, blocks)):
        far, c = chip ^ (i % 4), core ^ (i // 4)
        outer[rows_from((2 * far + c) * half, half)] = piece[...].astype(WIDE)
        stage[c, far] = block[...]
    for c in range(2):
        for p in range(CHIPS):
            for k in range(4):
                start = k * width + p * part
                inner[c * half : (c + 1) * half, start : start + part] = stage[
                    c, p, :, k * part : (k + 1) * part
                ].astype(WIDE)


def unpack_rest(*refs):
    pieces, mats, vectors, (b_query, b_value, b_inner, stage, small) = (
        refs[:8],
        refs[8:12],
        refs[12:18],
        refs[18:],
    )
    core, _, _, chip, place = places()
    part = mats[0].shape[0]
    half = part // 2
    for i, piece in enumerate(pieces):
        far = chip ^ (i % 4)
        stage[core ^ (i // 4), far] = piece[:half]
        if i < 4:
            small[far] = piece[half:, :part].astype(WIDE)
    for c in range(2):
        for k in range(CHIPS):
            for j, out in enumerate(mats):
                out[c * half : (c + 1) * half, k * part : (k + 1) * part] = stage[
                    c, k, :, j * part : (j + 1) * part
                ].astype(WIDE)
    total = small[0] + small[1] + small[2] + small[3]
    for i, out in enumerate(vectors):
        out[...] = total[i]
    biases = small[place]
    b_query[...] = biases[7]
    b_value[...] = biases[8]
    for p in range(CHIPS):
        b_inner[p * part : (p + 1) * part] = small[p][6]


def per_device(
    inputs,
    segments,
    query_weight,
    query_bias,
    key_weight,
    value_weight,
    value_bias,
    output_weight,
    output_bias,
    first_gain,
    first_shift,
    inner_weight,
    inner_bias,
    outer_weight,
    outer_bias,
    second_gain,
    second_shift,
    cotangent,
):
    groups = lax.axis_size("ctx") // TEAM
    lines = [[m + TEAM * g for g in range(groups)] for m in range(TEAM)]
    tokens, width = inputs.shape[1:]
    part = query_weight.shape[0]
    hidden = outer_weight.shape[0]
    count, half = CHIPS * tokens, part // 2
    heads = part // HEAD_DIM

    def chips(block):
        return [partner(block, "ctx", s << 1) for s in (1, 2, 3)]

    def exchanged(blocks):
        return [partner(block, "ctx", (s + 1) << 1) for s, block in enumerate(blocks)]

    def joined(block):
        return partner(block, "ctx", CORE)

    (own,) = kernel(
        prepare_tokens,
        [shape((tokens + 16, width))],
        inputs,
        segments,
        scratch=[pltpu.VMEM((1, tokens), jnp.int32)],
        loads=2,
    )
    teams = [[c + TEAM * g + 2 * n for n in range(CHIPS)] for g in range(groups) for c in range(2)]
    seen = lax.all_gather(own, "ctx", axis_index_groups=teams)
    (first,) = kernel(
        prepare_weights,
        [shape((4 * half, width))],
        query_weight,
        key_weight,
        value_weight,
        output_weight,
        inner_weight,
        outer_weight,
        output_bias,
        first_gain,
        first_shift,
        outer_bias,
        second_gain,
        second_shift,
        inner_bias,
        query_bias,
        value_bias,
        scratch=[
            pltpu.VMEM((3, half, width), LOW),
            pltpu.VMEM((half, 4 * width), LOW),
            *[pltpu.VMEM((part,), LOW)] * 6,
            pltpu.VMEM((hidden,), LOW),
            *[pltpu.VMEM((part,), LOW)] * 2,
        ],
        loads=15,
    )
    (mine,) = kernel(first_rows, [shape((half, width))], first, after=(seen,))
    line = [first, partner(first, "fsdp", 1), partner(first, "fsdp", 2), partner(mine, "fsdp", 3)]
    projections, others, sent = kernel(
        sort_pieces,
        [shape((4, half, width)), shape((3, 3 * half, width)), shape((3 * half, width))],
        *line,
    )
    last = partner(sent, "fsdp", 1)

    rows_in, w_qkv, queries, kv_own, segs, vec, b_inner = kernel(
        project,
        [
            shape((count, width)),
            shape((width, 3 * part)),
            shape((count, part)),
            shape((count, 2 * part)),
            shape((8, tokens), WIDE),
            shape((8, width), WIDE),
            shape((1, width), WIDE),
        ],
        seen,
        projections,
        joined(projections),
        scratch=[pltpu.VMEM((4, 16, part), WIDE)],
    )
    kv_far, seg_far = partner(kv_own, "ctx", CORE), partner(segs, "ctx", CORE)
    if groups == 1:
        context, probs = kernel(
            attend_all,
            [shape((count, part)), shape((heads, 2 * count, count))],
            queries,
            kv_own,
            kv_far,
            segs,
            seg_far,
            scratch=[
                pltpu.VMEM((2 * count, 2 * part), LOW),
                pltpu.VMEM((2 * CHIPS, tokens), WIDE),
                pltpu.VMEM((1, count), WIDE),
            ],
            room=24,
        )
    else:
        kv = jnp.concatenate([kv_own, kv_far])
        seg_key = jnp.concatenate([segs[:CHIPS], seg_far[:CHIPS]])
        kv = lax.all_gather(kv, "ctx", axis=0, tiled=True, axis_index_groups=lines)
        seg_key = lax.all_gather(seg_key, "ctx", axis=0, tiled=True, axis_index_groups=lines)
        context, probs = attention(queries, segs[:CHIPS].reshape(1, count), kv, seg_key)

    contexts = [context] + chips(context)
    (last,) = kernel(passed, [shape(last.shape)], last, after=(context,))
    w_output, w_inner, w_outer = kernel(
        assemble, [shape((width, width))] * 3, others, last, joined(others), joined(last)
    )
    context_low, unit_one, inverse_one, normed_low, activated, slope, *outer_sent = kernel(
        forward,
        [
            shape((count, width)),
            shape((tokens, width), WIDE),
            shape((tokens, 1), WIDE),
            shape((count, width)),
            shape((count, width)),
            shape((count, width), WIDE),
            shape((tokens, width), WIDE),
        ]
        + [shape((tokens, width))] * 3,
        *contexts,
        rows_in,
        w_output,
        vec,
        w_inner,
        b_inner,
        w_outer,
        scratch=[pltpu.VMEM((CHIPS, count, part), LOW)],
        room=16,
    )
    result, grad_summed, grad_outer, sums_one = kernel(
        backward_first,
        [
            shape((1, tokens, width)),
            shape((tokens, width), WIDE),
            shape((tokens, width)),
            shape((8, width), WIDE),
        ],
        outer_sent[0],
        *exchanged(outer_sent[1:]),
        unit_one,
        vec,
        cotangent,
        last=(0,),
    )
    grad_outer, grad_inner, sums_inner, inner_own, *inner_sent = kernel(
        backward_second,
        [
            shape((count, width)),
            shape((count, width)),
            shape((1, width), WIDE),
            shape((tokens, width), WIDE),
        ]
        + [shape((tokens, width))] * 3,
        grad_outer,
        *chips(grad_outer),
        slope,
        w_outer,
        w_inner,
        room=12,
    )

    inner_far = exchanged(inner_sent)

    def near_sum(kept, sent):
        received = partner(sent, "ctx", CORE)
        return kernel(add_near, [shape((2,) + kept.shape[1:])] * 2, kept, received)

    def far_sum(kept, sent, after=()):
        received = partner(sent, "fsdp", 1)
        return kernel(add_far, [shape(kept.shape[1:])] * 2, kept, received, after=after)

    def last_sum(kept, sent, after=()):
        received = partner(sent, "fsdp", 2)
        (total,) = kernel(add_last, [shape(kept.shape)], kept, received, after=after)
        if groups > 1:
            total = lax.psum(total.astype(WIDE), "ctx", axis_index_groups=lines).astype(LOW)
        return total

    kept, sent = kernel(
        weight_grads,
        [shape((4, 2 * half, width))] * 2,
        activated,
        grad_outer,
        normed_low,
        grad_inner,
        scratch=[pltpu.VMEM((width, width), LOW)],
        room=12,
    )
    outer_kept, outer_sent, inner_kept, inner_sent = mlp_near = kernel(
        add_near_both, [shape((2, half, width))] * 4, kept, partner(sent, "ctx", CORE)
    )
    outer_kept, outer_sent, inner_sent = kernel(
        add_far_passing,
        [shape((half, width))] * 2 + [shape((2, half, width))],
        outer_kept,
        partner(outer_sent, "fsdp", 1),
        inner_sent,
    )
    outer_total = last_sum(outer_kept, outer_sent)
    mlp_far = far_sum(inner_kept, inner_sent)
    grad_residual, grad_low, sums_two = kernel(
        norm_backward,
        [shape((tokens, width), WIDE), shape((tokens, width)), shape((8, width), WIDE)],
        grad_summed,
        inner_own,
        *inner_far,
        unit_one,
        inverse_one,
        vec,
        after=tuple(mlp_near),
    )
    grads_low = [grad_low] + chips(grad_low)
    if groups == 1:
        grad_low, grad_queries, grad_kv, grad_kv_sent = kernel(
            attend_back_all,
            [
                shape((count, width)),
                shape((count, part)),
                shape((count, 2 * part), WIDE),
                shape((count, 2 * part)),
            ],
            queries,
            kv_own,
            kv_far,
            *grads_low,
            w_output,
            probs,
            scratch=[
                pltpu.VMEM((2 * count, 2 * part), LOW),
                pltpu.VMEM((count, part), LOW),
                pltpu.VMEM((2 * count, 2 * part), WIDE),
            ],
            room=24,
            after=(outer_total, *mlp_far),
        )
    else:
        grad_low, grad_context = kernel(
            context_back, [shape((count, width)), shape((count, part))], *grads_low, w_output
        )
        grad_queries, grad_kv = attention_back(queries, kv, grad_context, probs)
        grad_kv = grad_kv.reshape(groups, 2, count, 2 * part).transpose(1, 0, 2, 3)
        grad_kv = lax.psum_scatter(
            grad_kv.reshape(2, groups * count, 2 * part),
            "ctx",
            scatter_dimension=1,
            tiled=True,
            axis_index_groups=lines,
        )
        grad_kv, grad_kv_sent = grad_kv[0], grad_kv[1].astype(LOW)
    grad_kv_far = partner(grad_kv_sent, "ctx", CORE)
    (grad_o,) = kernel(output_grads, [shape((width, part))], context_low, grad_low)
    inner_total = last_sum(*mlp_far)
    cut = shape((4, half + 16, width))
    grad_qkv, rest_kept, rest_sent = kernel(
        projection_grads,
        [shape((count, 3 * part)), cut, cut],
        rows_in,
        grad_queries,
        grad_kv,
        grad_kv_far,
        grad_o,
        sums_one,
        sums_two,
        sums_inner,
        scratch=[pltpu.VMEM((width, width), LOW)],
    )
    rest_near = near_sum(rest_kept, rest_sent)
    input_own, *input_sent = kernel(
        input_grads,
        [shape((tokens, width), WIDE)] + [shape((tokens, width))] * 3,
        grad_qkv,
        w_qkv,
        grad_residual,
        after=tuple(rest_near),
    )
    input_far = exchanged(input_sent)

    outer_chips = [outer_total] + chips(outer_total)
    inner_chips = [inner_total] + chips(inner_total)
    rest_total = last_sum(
        *far_sum(*rest_near, after=(inner_total,)),
        after=(*outer_chips[1:], *inner_chips[1:], *input_far),
    )
    rest_chips = [rest_total] + chips(rest_total)
    (grad_input,) = kernel(
        add_tokens,
        [shape((1, tokens, width))],
        input_own,
        *input_far,
        last=(0,),
        after=(rest_total,),
    )
    g_outer, g_inner = kernel(
        unpack_mlp,
        [shape((hidden, width), WIDE), shape((part, 4 * hidden), WIDE)],
        *outer_chips,
        *map(joined, outer_chips),
        *inner_chips,
        *map(joined, inner_chips),
        last=(0, 1),
        scratch=[pltpu.VMEM((2, CHIPS, half, width), LOW)],
        room=12,
        after=(rest_total,),
    )
    g_query, g_key, g_value, g_output, *vec, g_b_query, g_b_value, g_b_inner = kernel(
        unpack_rest,
        [shape((part, width), WIDE)] * 4
        + [shape((part,), WIDE)] * 8
        + [shape((width,), WIDE)],
        *rest_chips,
        *map(joined, rest_chips),
        last=range(13),
        scratch=[
            pltpu.VMEM((2, CHIPS, half, width), LOW),
            pltpu.VMEM((CHIPS, 16, part), WIDE),
        ],
        room=12,
    )
    return (
        result,
        grad_input,
        g_query,
        g_b_query,
        g_key,
        g_value,
        g_b_value,
        g_output,
        vec[3],
        vec[4],
        vec[5],
        g_inner,
        g_b_inner,
        g_outer,
        vec[0],
        vec[1],
        vec[2],
    )


def solution(mesh):
    rows, cuts, whole = P("fsdp", "ctx", None), P("fsdp", None), P("fsdp")
    params = (cuts, whole, cuts, cuts, whole, cuts, whole, whole, whole)
    params += (cuts, whole, cuts, whole, whole, whole)
    return jax.shard_map(
        per_device,
        mesh=mesh,
        in_specs=(rows, P("fsdp", "ctx")) + params + (rows,),
        out_specs=(rows, rows) + params,
        check_vma=False,
    )
```

time: 279 us -> 186 us (0.67)
  Pallas kernels: 107 us -> 29.5 us
  local copies, waits for them, and re-layouts: 28.2 us -> 0.01 us
  waiting for transfers between devices: 57.6 us -> 85.2 us
  starting transfers between devices: 78.9 us -> 58.2 us
  blocking collectives: 0 us -> 11.8 us
  other arithmetic: 4.95 us -> 0 us
    pallas_call x34 -> x28, Pallas kernels: 107 us -> 29.5 us  [kernel(): pl.pallas_call(step, out_shape=[o if n in last else pltpu.VMEM(o.shape, o...]
    ppermute x90 -> x57, waiting for transfers between devices: 57.6 us -> 85.2 us  [partner(): return lax.ppermute(block, axis, [(i, i ^ bit) for i in devices])]
    ppermute x90 -> x57, starting transfers between devices: 78.9 us -> 58.2 us  [partner(): return lax.ppermute(block, axis, [(i, i ^ bit) for i in devices])]
    unnamed x189 -> x2, local copies, waits for them, and re-layouts: 14.2 us -> 0.01 us
    all_gather x0 -> x1, blocking collectives: none -> 11.8 us  [per_device(): seen = lax.all_gather(own, 'ctx', axis_index_groups=teams)]
    slice x6 -> x0, local copies, waits for them, and re-layouts: 7.84 us -> none  [the longest x1 2.06 us: per_device(): grad_kv[:count]]
    concatenate x2 -> x0, local copies, waits for them, and re-layouts: 4.83 us -> none  [the longest x1 4.77 us: per_device(): jnp.concatenate([output_bias, first_gain, first_shift, outer_bias, second...]
  transfers between devices with their start and end apart: 90 -> 57, of which waited for: 17 -> 24; matrix products, arithmetic and copies ran while one was open for 5% -> 0% of each run, Pallas kernels for 32% -> 6%
where the time goes in v2:
time: 186 us
  waiting for transfers between devices  85.2 us (46%)
  starting transfers between devices  58.2 us (31%)
  Pallas kernels  29.5 us (16%)
  blocking collectives  11.8 us (6%)
    ppermute x57, waiting for transfers between devices, partner(): return lax.ppermute(block, axis, [(i, i ^ bit) for i in devices])  85.2 us
    ppermute x57, starting transfers between devices, partner(): return lax.ppermute(block, axis, [(i, i ^ bit) for i in devices])  58.2 us
    pallas_call x28, Pallas kernels, kernel(): pl.pallas_call(step, out_shape=[o if n in last else pltpu.VMEM(o.shape, o...  29.5 us
    all_gather x1, blocking collectives, per_device(): seen = lax.all_gather(own, 'ctx', axis_index_groups=teams)  11.8 us
  transfers between devices with their start and end apart: 57, of which 24 were waited for; matrix products, arithmetic and copies ran while one was open for 0% of the time, Pallas kernels for 6%

profile of v2, /device:TPU:0, one launch (start us, length us, event | category | flops | bytes accessed | tf_op | source)
XLA Modules:
  0.0 185.8 jit_solution(16243341772816179961)
XLA Ops:
  2.3 4.1 %collective-permute-start.1 = (bf16[384,768]{1,0:T(8,128)(2,1)S(1)}, bf16[384,768]{1,0:T(8,128)(2,1)S(1)}, u32[]{:S(2)}, u32[]{:S(2)}) collective-permute-start(bf16[384,768]{1,0:T(8,128)(2,1)S(1)} %shard_map.306.refs_1_.refs_0_), channel_id=1, source_target_pairs={{0,2},{1,3},{2,0},{3,1},{4,6},{5,7},{6,4},{7,5},{8,10},{9,11},{10,... | collective-permute-start | bytes 1769480 | tf_op jit(solution)/shard_map/ppermute | solution.py:24
  9.0 11.8 %all-gather = bf16[576,768]{1,0:T(8,128)(2,1)S(1)} all-gather(bf16[144,768]{1,0:T(8,128)(2,1)S(1)} %shard_map.305), channel_id=2, replica_groups={{0,8,16,24},{4,12,20,28},{1,9,17,25},{5,13,21,29},{2,10,18,26},{6,14,22..., dimensions={0}, use_global_device_ids=true | all-gather | bytes 1105920 | tf_op jit(solution)/shard_map/all_gather | solution.py:600
  21.1 15.7 %collective-permute-done.2.refs_3_ = bf16[96,768]{1,0:T(8,128)(2,1)S(1)} collective-permute-done((bf16[96,768]{1,0:T(8,128)(2,1)S(1)}, bf16[96,768]{1,0:T(8,128)(2,1)S(1)}, u32[]{:S(2)}, u32[]{:S(2)}) %collective-permute-start.2) | collective-permute-done | bytes 147488 | tf_op jit(solution)/shard_map/ppermute | solution.py:24
  37.5 2.7 %collective-permute-start.9 = (bf16[288,768]{1,0:T(8,128)(2,1)S(1)}, bf16[288,768]{1,0:T(8,128)(2,1)S(1)}, u32[]{:S(2)}, u32[]{:S(2)}) collective-permute-start(bf16[288,768]{1,0:T(8,128)(2,1)S(1)} %get-tuple-element.104), channel_id=1, source_target_pairs={{0,1},{1,0},{2,3},{3,2},{4,5},{5,4},{6,7},{7,6},{8,9},{9,8},{10,11... | collective-permute-start | bytes 1327112 | tf_op jit(solution)/shard_map/ppermute | solution.py:24
  43.0 3.8 %shard_map.310 = (bf16[512,192]{1,0:T(8,128)(2,1)S(1)}, bf16[3,1024,512]{2,1,0:T(8,128)(2,1)S(1)}) custom-call(bf16[512,192]{1,0:T(8,128)(2,1)S(1)} %get-tuple-element.98.refs_0_.refs_3_, bf16[512,384]{1,0:T(8,128)(2,1)S(1)} %get-tuple-element.99.refs_1_.refs_4_, bf16[512,384]{1,0:T(8,128)(2,1)S(1)} %collective-permute-done.4.refs_2_.refs_5_, ...), custom_call_target="tpu_custom_call" | custom-call | flops 1 | bytes 1 | tf_op jit(solution)/shard_map/pallas_call | solution.py:54
  46.7 3.9 %collective-permute-done.9.refs_1_ = bf16[288,768]{1,0:T(8,128)(2,1)S(1)} collective-permute-done((bf16[288,768]{1,0:T(8,128)(2,1)S(1)}, bf16[288,768]{1,0:T(8,128)(2,1)S(1)}, u32[]{:S(2)}, u32[]{:S(2)}) %collective-permute-start.9) | collective-permute-done | bytes 442400 | tf_op jit(solution)/shard_map/ppermute | solution.py:24
  50.7 2.5 %collective-permute-start.8 = (bf16[512,192]{1,0:T(8,128)(2,1)S(1)}, bf16[512,192]{1,0:T(8,128)(2,1)S(1)}, u32[]{:S(2)}, u32[]{:S(2)}) collective-permute-start(bf16[512,192]{1,0:T(8,128)(2,1)S(1)} %get-tuple-element.101.refs_0_), channel_id=1, source_target_pairs={{0,24},{4,28},{8,16},{12,20},{16,8},{20,12},{24,0},{28,4},{1,25},{... | collective-permute-start | bytes 589832 | tf_op jit(solution)/shard_map/ppermute | solution.py:24
  54.5 6.3 %collective-permute-done.8.refs_3_ = bf16[512,192]{1,0:T(8,128)(2,1)S(1)} collective-permute-done((bf16[512,192]{1,0:T(8,128)(2,1)S(1)}, bf16[512,192]{1,0:T(8,128)(2,1)S(1)}, u32[]{:S(2)}, u32[]{:S(2)}) %collective-permute-start.8) | collective-permute-done | bytes 196640 | tf_op jit(solution)/shard_map/ppermute | solution.py:24
  60.8 5.1 %collective-permute-done.7.refs_2_ = bf16[512,192]{1,0:T(8,128)(2,1)S(1)} collective-permute-done((bf16[512,192]{1,0:T(8,128)(2,1)S(1)}, bf16[512,192]{1,0:T(8,128)(2,1)S(1)}, u32[]{:S(2)}, u32[]{:S(2)}) %collective-permute-start.7) | collective-permute-done | bytes 196640 | tf_op jit(solution)/shard_map/ppermute | solution.py:24
  66.0 3.1 %shard_map.313 = (bf16[512,768]{1,0:T(8,128)(2,1)S(1)}, f32[128,768]{1,0:T(8,128)S(1)}, f32[128,1]{1,0:T(8,128)S(1)}, bf16[512,768]{1,0:T(8,128)(2,1)S(1)}, bf16...) custom-call(bf16[512,192]{1,0:T(8,128)(2,1)S(1)} %get-tuple-element., ...), custom_call_target="tpu_custom_call" | custom-call | flops 1 | bytes 1 | tf_op jit(solution)/shard_map/pallas_call | solution.py:54
  72.7 4.3 %collective-permute-done.12.refs_1_ = bf16[128,768]{1,0:T(8,128)(2,1)S(1)} collective-permute-done((bf16[128,768]{1,0:T(8,128)(2,1)S(1)}, bf16[128,768]{1,0:T(8,128)(2,1)S(1)}, u32[]{:S(2)}, u32[]{:S(2)}) %collective-permute-start.12) | collective-permute-done | bytes 196640 | tf_op jit(solution)/shard_map/ppermute | solution.py:24
  77.0 4.4 %collective-permute-done.13.refs_2_ = bf16[128,768]{1,0:T(8,128)(2,1)S(1)} collective-permute-done((bf16[128,768]{1,0:T(8,128)(2,1)S(1)}, bf16[128,768]{1,0:T(8,128)(2,1)S(1)}, u32[]{:S(2)}, u32[]{:S(2)}) %collective-permute-start.13) | collective-permute-done | bytes 196640 | tf_op jit(solution)/shard_map/ppermute | solution.py:24
  86.0 5.3 %collective-permute-done.17.refs_3_ = bf16[128,768]{1,0:T(8,128)(2,1)S(1)} collective-permute-done((bf16[128,768]{1,0:T(8,128)(2,1)S(1)}, bf16[128,768]{1,0:T(8,128)(2,1)S(1)}, u32[]{:S(2)}, u32[]{:S(2)}) %collective-permute-start.17) | collective-permute-done | bytes 196640 | tf_op jit(solution)/shard_map/ppermute | solution.py:24
  91.2 2.1 %collective-permute-done.16.refs_2_ = bf16[128,768]{1,0:T(8,128)(2,1)S(1)} collective-permute-done((bf16[128,768]{1,0:T(8,128)(2,1)S(1)}, bf16[128,768]{1,0:T(8,128)(2,1)S(1)}, u32[]{:S(2)}, u32[]{:S(2)}) %collective-permute-start.16) | collective-permute-done | bytes 196640 | tf_op jit(solution)/shard_map/ppermute | solution.py:24
  96.6 2.8 %collective-permute-done.18.refs_1_ = bf16[4,192,768]{2,1,0:T(8,128)(2,1)S(1)} collective-permute-done((bf16[4,192,768]{2,1,0:T(8,128)(2,1)S(1)}, bf16[4,192,768]{2,1,0:T(8,128)(2,1)S(1)}, u32[]{:S(2)}, u32[]{:S(2)}) %collective-permute-start.18) | collective-permute-done | bytes 1179680 | tf_op jit(solution)/shard_map/ppermute | solution.py:24
  99.7 1.8 collective-permute-start.19
  105.0 3.8 %collective-permute-done.19.refs_1_ = bf16[2,96,768]{2,1,0:T(8,128)(2,1)S(1)} collective-permute-done((bf16[2,96,768]{2,1,0:T(8,128)(2,1)S(1)}, bf16[2,96,768]{2,1,0:T(8,128)(2,1)S(1)}, u32[]{:S(2)}, u32[]{:S(2)}) %collective-permute-start.19) | collective-permute-done | bytes 294944 | tf_op jit(solution)/shard_map/ppermute | solution.py:24
  108.9 1.8 collective-permute-start.24
  110.7 1.8 collective-permute-done.30.refs_7_
  116.5 2.3 %collective-permute-start.20 = (bf16[96,768]{1,0:T(8,128)(2,1)S(1)}, bf16[96,768]{1,0:T(8,128)(2,1)S(1)}, u32[]{:S(2)}, u32[]{:S(2)}) collective-permute-start(bf16[96,768]{1,0:T(8,128)(2,1)S(1)} %get-tuple-element.128), channel_id=1, source_target_pairs={{0,2},{1,3},{2,0},{3,1},{4,6},{5,7},{6,4},{7,5},{8,10},{9,11},{10,... | collective-permute-start | bytes 442376 | tf_op jit(solution)/shard_map/ppermute | solution.py:24
  118.7 5.9 %collective-permute-done.20.refs_1_ = bf16[96,768]{1,0:T(8,128)(2,1)S(1)} collective-permute-done((bf16[96,768]{1,0:T(8,128)(2,1)S(1)}, bf16[96,768]{1,0:T(8,128)(2,1)S(1)}, u32[]{:S(2)}, u32[]{:S(2)}) %collective-permute-start.20) | collective-permute-done | bytes 147488 | tf_op jit(solution)/shard_map/ppermute | solution.py:24
  124.8 5.4 %shard_map.323 = (bf16[512,768]{1,0:T(8,128)(2,1)S(1)}, bf16[512,192]{1,0:T(8,128)(2,1)S(1)}, f32[512,384]{1,0:T(8,128)S(1)}, bf16[512,384]{1,0:T(8,128)(2,1)S(1)}) custom-call(bf16[96,768]{1,0:T(8,128)(2,1)S(1)} %shard_map.319.refs_0_.refs_1_, bf16[96,768]{1,0:T(8,128)(2,1)S(1)} %get-tuple-element.131.refs_0_.refs_1_, ...), custom_call_target="tpu_custom_call" | custom-call | flops 1 | bytes 1 | tf_op jit(solution)/shard_map/pallas_call | solution.py:54
  133.4 2.0 %collective-permute-done.36.refs_1_ = bf16[4,112,768]{2,1,0:T(8,128)(2,1)S(1)} collective-permute-done((bf16[4,112,768]{2,1,0:T(8,128)(2,1)S(1)}, bf16[4,112,768]{2,1,0:T(8,128)(2,1)S(1)}, u32[]{:S(2)}, u32[]{:S(2)}) %collective-permute-start.36) | collective-permute-done | bytes 688160 | tf_op jit(solution)/shard_map/ppermute | solution.py:24
  135.8 3.4 %collective-permute-start.25 = (bf16[96,768]{1,0:T(8,128)(2,1)S(1)}, bf16[96,768]{1,0:T(8,128)(2,1)S(1)}, u32[]{:S(2)}, u32[]{:S(2)}) collective-permute-start(bf16[96,768]{1,0:T(8,128)(2,1)S(1)} %get-tuple-element.132.refs_2_), channel_id=1, source_target_pairs={{0,2},{1,3},{2,0},{3,1},{4,6},{5,7},{6,4},{7,5},{8,10},{9,11},{10,... | collective-permute-start | bytes 442376 | tf_op jit(solution)/shard_map/ppermute | solution.py:24
  142.7 4.0 %collective-permute-done.25.refs_1_ = bf16[96,768]{1,0:T(8,128)(2,1)S(1)} collective-permute-done((bf16[96,768]{1,0:T(8,128)(2,1)S(1)}, bf16[96,768]{1,0:T(8,128)(2,1)S(1)}, u32[]{:S(2)}, u32[]{:S(2)}) %collective-permute-start.25) | collective-permute-done | bytes 147488 | tf_op jit(solution)/shard_map/ppermute | solution.py:24
  153.6 2.1 %collective-permute-start.39 = (bf16[128,768]{1,0:T(8,128)(2,1)S(1)}, bf16[128,768]{1,0:T(8,128)(2,1)S(1)}, u32[]{:S(2)}, u32[]{:S(2)}) collective-permute-start(bf16[128,768]{1,0:T(8,128)(2,1)S(1)} %get-tuple-element.158), channel_id=1, source_target_pairs={{0,24},{4,28},{8,16},{12,20},{16,8},{20,12},{24,0},{28,4},{1,25},{... | collective-permute-start | bytes 589832 | tf_op jit(solution)/shard_map/ppermute | solution.py:24
  156.8 3.4 %collective-permute-start.41 = (bf16[112,768]{1,0:T(8,128)(2,1)S(1)}, bf16[112,768]{1,0:T(8,128)(2,1)S(1)}, u32[]{:S(2)}, u32[]{:S(2)}) collective-permute-start(bf16[112,768]{1,0:T(8,128)(2,1)S(1)} %get-tuple-element.160), channel_id=1, source_target_pairs={{0,2},{1,3},{2,0},{3,1},{4,6},{5,7},{6,4},{7,5},{8,10},{9,11},{10,... | collective-permute-start | bytes 516104 | tf_op jit(solution)/shard_map/ppermute | solution.py:24
  160.3 4.1 %collective-permute-done.26.refs_3_.refs_10_ = bf16[96,768]{1,0:T(8,128)(2,1)S(1)} collective-permute-done((bf16[96,768]{1,0:T(8,128)(2,1)S(1)}, bf16[96,768]{1,0:T(8,128)(2,1)S(1)}, u32[]{:S(2)}, u32[]{:S(2)}) %collective-permute-start.26) | collective-permute-done | bytes 147488 | tf_op jit(solution)/shard_map/ppermute | solution.py:24
  165.4 2.4 %collective-permute-done.41.refs_10_ = bf16[112,768]{1,0:T(8,128)(2,1)S(1)} collective-permute-done((bf16[112,768]{1,0:T(8,128)(2,1)S(1)}, bf16[112,768]{1,0:T(8,128)(2,1)S(1)}, u32[]{:S(2)}, u32[]{:S(2)}) %collective-permute-start.41) | collective-permute-done | bytes 172064 | tf_op jit(solution)/shard_map/ppermute | solution.py:24
  173.0 3.1 %collective-permute-done.44.refs_3_ = bf16[112,768]{1,0:T(8,128)(2,1)S(1)} collective-permute-done((bf16[112,768]{1,0:T(8,128)(2,1)S(1)}, bf16[112,768]{1,0:T(8,128)(2,1)S(1)}, u32[]{:S(2)}, u32[]{:S(2)}) %collective-permute-start.44) | collective-permute-done | bytes 172064 | tf_op jit(solution)/shard_map/ppermute | solution.py:24
  176.1 3.3 %collective-permute-done.43.refs_2_ = bf16[112,768]{1,0:T(8,128)(2,1)S(1)} collective-permute-done((bf16[112,768]{1,0:T(8,128)(2,1)S(1)}, bf16[112,768]{1,0:T(8,128)(2,1)S(1)}, u32[]{:S(2)}, u32[]{:S(2)}) %collective-permute-start.43) | collective-permute-done | bytes 172064 | tf_op jit(solution)/shard_map/ppermute | solution.py:24
  181.2 2.6 %shard_map.332 = (f32[768,768]{1,0:T(8,128)}, f32[192,3072]{1,0:T(8,128)}) custom-call(bf16[112,768]{1,0:T(8,128)(2,1)S(1)} %shard_map.329.refs_0_, bf16[96,768]{1,0:T(8,128)(2,1)S(1)} %shard_map.319.refs_0_.refs_1_, bf16[96,768]{1,0:T(8,128)(2,1)S(1)} %collective-permute-done.21.refs_0_.refs_2_, ...), custom_call_target="tpu_custom_call" | custom-call | flops 1 | bytes 1 | tf_op jit(solution)/shard_map/pallas_call | solution.py:54
  (113 shorter events, 53.6 us)
Async XLA Ops:
  2.3 34.4 %collective-permute-start.1 = (bf16[384,768]{1,0:T(8,128)(2,1)S(1)}, bf16[384,768]{1,0:T(8,128)(2,1)S(1)}, u32[]{:S(2)}, u32[]{:S(2)}) collective-permute-start(bf16[384,768]{1,0:T(8,128)(2,1)S(1)} %shard_map.306.refs_1_.refs_0_), channel_id=1, source_target_pairs={{0,2},{1,3},{2,0},{3,1},{4,6},{5,7},{6,4},{7,5},{8,10},{9,11},{10,... | collective-permute-start | bytes 1769480 | tf_op jit(solution)/shard_map/ppermute | solution.py:24
  6.4 30.3 %collective-permute-start = (bf16[384,768]{1,0:T(8,128)(2,1)S(1)}, bf16[384,768]{1,0:T(8,128)(2,1)S(1)}, u32[]{:S(2)}, u32[]{:S(2)}) collective-permute-start(bf16[384,768]{1,0:T(8,128)(2,1)S(1)} %shard_map.306.refs_1_.refs_0_), channel_id=1, source_target_pairs={{0,1},{1,0},{2,3},{3,2},{4,5},{5,4},{6,7},{7,6},{8,9},{9,8},{10,11... | collective-permute-start | bytes 1769480 | tf_op jit(solution)/shard_map/ppermute | solution.py:24
  20.8 15.9 %collective-permute-start.2 = (bf16[96,768]{1,0:T(8,128)(2,1)S(1)}, bf16[96,768]{1,0:T(8,128)(2,1)S(1)}, u32[]{:S(2)}, u32[]{:S(2)}) collective-permute-start(bf16[96,768]{1,0:T(8,128)(2,1)S(1)} %shard_map.307), channel_id=1, source_target_pairs={{0,3},{1,2},{2,1},{3,0},{4,7},{5,6},{6,5},{7,4},{8,11},{9,10},{10,... | collective-permute-start | bytes 442376 | tf_op jit(solution)/shard_map/ppermute | solution.py:24
  37.0 17.2 %collective-permute-start.10 = (bf16[3,288,768]{2,1,0:T(8,128)(2,1)S(1)}, bf16[3,288,768]{2,1,0:T(8,128)(2,1)S(1)}, u32[]{:S(2)}, u32[]{:S(2)}) collective-permute-start(bf16[3,288,768]{2,1,0:T(8,128)(2,1)S(1)} %get-tuple-element.103.refs_0_), channel_id=1, source_target_pairs={{0,4},{4,0},{8,12},{12,8},{16,20},{20,16},{24,28},{28,24},{1,5},{5... | collective-permute-start | bytes 3981320 | tf_op jit(solution)/shard_map/ppermute | solution.py:24
  37.5 13.1 %collective-permute-start.9 = (bf16[288,768]{1,0:T(8,128)(2,1)S(1)}, bf16[288,768]{1,0:T(8,128)(2,1)S(1)}, u32[]{:S(2)}, u32[]{:S(2)}) collective-permute-start(bf16[288,768]{1,0:T(8,128)(2,1)S(1)} %get-tuple-element.104), channel_id=1, source_target_pairs={{0,1},{1,0},{2,3},{3,2},{4,5},{5,4},{6,7},{7,6},{8,9},{9,8},{10,11... | collective-permute-start | bytes 1327112 | tf_op jit(solution)/shard_map/ppermute | solution.py:24
  50.7 10.1 %collective-permute-start.8 = (bf16[512,192]{1,0:T(8,128)(2,1)S(1)}, bf16[512,192]{1,0:T(8,128)(2,1)S(1)}, u32[]{:S(2)}, u32[]{:S(2)}) collective-permute-start(bf16[512,192]{1,0:T(8,128)(2,1)S(1)} %get-tuple-element.101.refs_0_), channel_id=1, source_target_pairs={{0,24},{4,28},{8,16},{12,20},{16,8},{20,12},{24,0},{28,4},{1,25},{... | collective-permute-start | bytes 589832 | tf_op jit(solution)/shard_map/ppermute | solution.py:24
  53.3 12.7 %collective-permute-start.7 = (bf16[512,192]{1,0:T(8,128)(2,1)S(1)}, bf16[512,192]{1,0:T(8,128)(2,1)S(1)}, u32[]{:S(2)}, u32[]{:S(2)}) collective-permute-start(bf16[512,192]{1,0:T(8,128)(2,1)S(1)} %get-tuple-element.101.refs_0_), channel_id=1, source_target_pairs={{0,16},{4,20},{8,24},{12,28},{16,0},{20,4},{24,8},{28,12},{1,17},{... | collective-permute-start | bytes 589832 | tf_op jit(solution)/shard_map/ppermute | solution.py:24
  53.7 12.3 %collective-permute-start.6 = (bf16[512,192]{1,0:T(8,128)(2,1)S(1)}, bf16[512,192]{1,0:T(8,128)(2,1)S(1)}, u32[]{:S(2)}, u32[]{:S(2)}) collective-permute-start(bf16[512,192]{1,0:T(8,128)(2,1)S(1)} %get-tuple-element.101.refs_0_), channel_id=1, source_target_pairs={{0,8},{4,12},{8,0},{12,4},{16,24},{20,28},{24,16},{28,20},{1,9},{5... | collective-permute-start | bytes 589832 | tf_op jit(solution)/shard_map/ppermute | solution.py:24
  70.7 10.7 %collective-permute-start.13 = (bf16[128,768]{1,0:T(8,128)(2,1)S(1)}, bf16[128,768]{1,0:T(8,128)(2,1)S(1)}, u32[]{:S(2)}, u32[]{:S(2)}) collective-permute-start(bf16[128,768]{1,0:T(8,128)(2,1)S(1)} %get-tuple-element.112), channel_id=1, source_target_pairs={{0,16},{4,20},{8,24},{12,28},{16,0},{20,4},{24,8},{28,12},{1,17},{... | collective-permute-start | bytes 589832 | tf_op jit(solution)/shard_map/ppermute | solution.py:24
  71.4 10.0 %collective-permute-start.14 = (bf16[128,768]{1,0:T(8,128)(2,1)S(1)}, bf16[128,768]{1,0:T(8,128)(2,1)S(1)}, u32[]{:S(2)}, u32[]{:S(2)}) collective-permute-start(bf16[128,768]{1,0:T(8,128)(2,1)S(1)} %get-tuple-element.113), channel_id=1, source_target_pairs={{0,24},{4,28},{8,16},{12,20},{16,8},{20,12},{24,0},{28,4},{1,25},{... | collective-permute-start | bytes 589832 | tf_op jit(solution)/shard_map/ppermute | solution.py:24
  82.5 8.7 %collective-permute-start.17 = (bf16[128,768]{1,0:T(8,128)(2,1)S(1)}, bf16[128,768]{1,0:T(8,128)(2,1)S(1)}, u32[]{:S(2)}, u32[]{:S(2)}) collective-permute-start(bf16[128,768]{1,0:T(8,128)(2,1)S(1)} %get-tuple-element.117.refs_0_), channel_id=1, source_target_pairs={{0,24},{4,28},{8,16},{12,20},{16,8},{20,12},{24,0},{28,4},{1,25},{... | collective-permute-start | bytes 589832 | tf_op jit(solution)/shard_map/ppermute | solution.py:24
  83.9 9.4 %collective-permute-start.16 = (bf16[128,768]{1,0:T(8,128)(2,1)S(1)}, bf16[128,768]{1,0:T(8,128)(2,1)S(1)}, u32[]{:S(2)}, u32[]{:S(2)}) collective-permute-start(bf16[128,768]{1,0:T(8,128)(2,1)S(1)} %get-tuple-element.117.refs_0_), channel_id=1, source_target_pairs={{0,16},{4,20},{8,24},{12,28},{16,0},{20,4},{24,8},{28,12},{1,17},{... | collective-permute-start | bytes 589832 | tf_op jit(solution)/shard_map/ppermute | solution.py:24
  84.4 8.9 %collective-permute-start.15 = (bf16[128,768]{1,0:T(8,128)(2,1)S(1)}, bf16[128,768]{1,0:T(8,128)(2,1)S(1)}, u32[]{:S(2)}, u32[]{:S(2)}) collective-permute-start(bf16[128,768]{1,0:T(8,128)(2,1)S(1)} %get-tuple-element.117.refs_0_), channel_id=1, source_target_pairs={{0,8},{4,12},{8,0},{12,4},{16,24},{20,28},{24,16},{28,20},{1,9},{5... | collective-permute-start | bytes 589832 | tf_op jit(solution)/shard_map/ppermute | solution.py:24
  99.7 9.1 %collective-permute-start.19 = (bf16[2,96,768]{2,1,0:T(8,128)(2,1)S(1)}, bf16[2,96,768]{2,1,0:T(8,128)(2,1)S(1)}, u32[]{:S(2)}, u32[]{:S(2)}) collective-permute-start(bf16[2,96,768]{2,1,0:T(8,128)(2,1)S(1)} %get-tuple-element.125.refs_1_), channel_id=1, source_target_pairs={{0,1},{1,0},{2,3},{3,2},{4,5},{5,4},{6,7},{7,6},{8,9},{9,8},{10,11... | collective-permute-start | bytes 884744 | tf_op jit(solution)/shard_map/ppermute | solution.py:24
  101.5 9.2 %collective-permute-start.29 = (bf16[128,768]{1,0:T(8,128)(2,1)S(1)}, bf16[128,768]{1,0:T(8,128)(2,1)S(1)}, u32[]{:S(2)}, u32[]{:S(2)}) collective-permute-start(bf16[128,768]{1,0:T(8,128)(2,1)S(1)} %get-tuple-element.135), channel_id=1, source_target_pairs={{0,8},{4,12},{8,0},{12,4},{16,24},{20,28},{24,16},{28,20},{1,9},{5... | collective-permute-start | bytes 589832 | tf_op jit(solution)/shard_map/ppermute | solution.py:24
  101.9 10.6 %collective-permute-start.30 = (bf16[128,768]{1,0:T(8,128)(2,1)S(1)}, bf16[128,768]{1,0:T(8,128)(2,1)S(1)}, u32[]{:S(2)}, u32[]{:S(2)}) collective-permute-start(bf16[128,768]{1,0:T(8,128)(2,1)S(1)} %get-tuple-element.136), channel_id=1, source_target_pairs={{0,16},{4,20},{8,24},{12,28},{16,0},{20,4},{24,8},{28,12},{1,17},{... | collective-permute-start | bytes 589832 | tf_op jit(solution)/shard_map/ppermute | solution.py:24
  103.4 9.1 %collective-permute-start.31 = (bf16[128,768]{1,0:T(8,128)(2,1)S(1)}, bf16[128,768]{1,0:T(8,128)(2,1)S(1)}, u32[]{:S(2)}, u32[]{:S(2)}) collective-permute-start(bf16[128,768]{1,0:T(8,128)(2,1)S(1)} %get-tuple-element.137), channel_id=1, source_target_pairs={{0,24},{4,28},{8,16},{12,20},{16,8},{20,12},{24,0},{28,4},{1,25},{... | collective-permute-start | bytes 589832 | tf_op jit(solution)/shard_map/ppermute | solution.py:24
  108.9 15.8 %collective-permute-start.24 = (bf16[2,96,768]{2,1,0:T(8,128)(2,1)S(1)}, bf16[2,96,768]{2,1,0:T(8,128)(2,1)S(1)}, u32[]{:S(2)}, u32[]{:S(2)}) collective-permute-start(bf16[2,96,768]{2,1,0:T(8,128)(2,1)S(1)} %get-tuple-element.130), channel_id=1, source_target_pairs={{0,1},{1,0},{2,3},{3,2},{4,5},{5,4},{6,7},{7,6},{8,9},{9,8},{10,11... | collective-permute-start | bytes 884744 | tf_op jit(solution)/shard_map/ppermute | solution.py:24
  112.9 11.8 %collective-permute-start.34 = (bf16[128,768]{1,0:T(8,128)(2,1)S(1)}, bf16[128,768]{1,0:T(8,128)(2,1)S(1)}, u32[]{:S(2)}, u32[]{:S(2)}) collective-permute-start(bf16[128,768]{1,0:T(8,128)(2,1)S(1)} %get-tuple-element.139.refs_6_), channel_id=1, source_target_pairs={{0,24},{4,28},{8,16},{12,20},{16,8},{20,12},{24,0},{28,4},{1,25},{... | collective-permute-start | bytes 589832 | tf_op jit(solution)/shard_map/ppermute | solution.py:24
  114.6 10.2 %collective-permute-start.33 = (bf16[128,768]{1,0:T(8,128)(2,1)S(1)}, bf16[128,768]{1,0:T(8,128)(2,1)S(1)}, u32[]{:S(2)}, u32[]{:S(2)}) collective-permute-start(bf16[128,768]{1,0:T(8,128)(2,1)S(1)} %get-tuple-element.139.refs_6_), channel_id=1, source_target_pairs={{0,16},{4,20},{8,24},{12,28},{16,0},{20,4},{24,8},{28,12},{1,17},{... | collective-permute-start | bytes 589832 | tf_op jit(solution)/shard_map/ppermute | solution.py:24
  116.0 8.7 %collective-permute-start.32 = (bf16[128,768]{1,0:T(8,128)(2,1)S(1)}, bf16[128,768]{1,0:T(8,128)(2,1)S(1)}, u32[]{:S(2)}, u32[]{:S(2)}) collective-permute-start(bf16[128,768]{1,0:T(8,128)(2,1)S(1)} %get-tuple-element.139.refs_6_), channel_id=1, source_target_pairs={{0,8},{4,12},{8,0},{12,4},{16,24},{20,28},{24,16},{28,20},{1,9},{5... | collective-permute-start | bytes 589832 | tf_op jit(solution)/shard_map/ppermute | solution.py:24
  135.6 20.1 %collective-permute-start.40 = (bf16[2,112,768]{2,1,0:T(8,128)(2,1)S(1)}, bf16[2,112,768]{2,1,0:T(8,128)(2,1)S(1)}, u32[]{:S(2)}, u32[]{:S(2)}) collective-permute-start(bf16[2,112,768]{2,1,0:T(8,128)(2,1)S(1)} %get-tuple-element.152.refs_1_), channel_id=1, source_target_pairs={{0,1},{1,0},{2,3},{3,2},{4,5},{5,4},{6,7},{7,6},{8,9},{9,8},{10,11... | collective-permute-start | bytes 1032200 | tf_op jit(solution)/shard_map/ppermute | solution.py:24
  135.8 10.9 %collective-permute-start.25 = (bf16[96,768]{1,0:T(8,128)(2,1)S(1)}, bf16[96,768]{1,0:T(8,128)(2,1)S(1)}, u32[]{:S(2)}, u32[]{:S(2)}) collective-permute-start(bf16[96,768]{1,0:T(8,128)(2,1)S(1)} %get-tuple-element.132.refs_2_), channel_id=1, source_target_pairs={{0,2},{1,3},{2,0},{3,1},{4,6},{5,7},{6,4},{7,5},{8,10},{9,11},{10,... | collective-permute-start | bytes 442376 | tf_op jit(solution)/shard_map/ppermute | solution.py:24
  139.2 9.1 %collective-permute-start.23 = (bf16[96,768]{1,0:T(8,128)(2,1)S(1)}, bf16[96,768]{1,0:T(8,128)(2,1)S(1)}, u32[]{:S(2)}, u32[]{:S(2)}) collective-permute-start(bf16[96,768]{1,0:T(8,128)(2,1)S(1)} %shard_map.319.refs_0_.refs_1_), channel_id=1, source_target_pairs={{0,24},{4,28},{8,16},{12,20},{16,8},{20,12},{24,0},{28,4},{1,25},{... | collective-permute-start | bytes 442376 | tf_op jit(solution)/shard_map/ppermute | solution.py:24
  140.5 9.8 %collective-permute-start.22 = (bf16[96,768]{1,0:T(8,128)(2,1)S(1)}, bf16[96,768]{1,0:T(8,128)(2,1)S(1)}, u32[]{:S(2)}, u32[]{:S(2)}) collective-permute-start(bf16[96,768]{1,0:T(8,128)(2,1)S(1)} %shard_map.319.refs_0_.refs_1_), channel_id=1, source_target_pairs={{0,16},{4,20},{8,24},{12,28},{16,0},{20,4},{24,8},{28,12},{1,17},{... | collective-permute-start | bytes 442376 | tf_op jit(solution)/shard_map/ppermute | solution.py:24
  141.9 9.3 %collective-permute-start.21 = (bf16[96,768]{1,0:T(8,128)(2,1)S(1)}, bf16[96,768]{1,0:T(8,128)(2,1)S(1)}, u32[]{:S(2)}, u32[]{:S(2)}) collective-permute-start(bf16[96,768]{1,0:T(8,128)(2,1)S(1)} %shard_map.319.refs_0_.refs_1_), channel_id=1, source_target_pairs={{0,8},{4,12},{8,0},{12,4},{16,24},{20,28},{24,16},{28,20},{1,9},{5... | collective-permute-start | bytes 442376 | tf_op jit(solution)/shard_map/ppermute | solution.py:24
  150.3 14.1 %collective-permute-start.37 = (bf16[128,768]{1,0:T(8,128)(2,1)S(1)}, bf16[128,768]{1,0:T(8,128)(2,1)S(1)}, u32[]{:S(2)}, u32[]{:S(2)}) collective-permute-start(bf16[128,768]{1,0:T(8,128)(2,1)S(1)} %get-tuple-element.156), channel_id=1, source_target_pairs={{0,8},{4,12},{8,0},{12,4},{16,24},{20,28},{24,16},{28,20},{1,9},{5... | collective-permute-start | bytes 589832 | tf_op jit(solution)/shard_map/ppermute | solution.py:24
  151.2 13.7 %collective-permute-start.38 = (bf16[128,768]{1,0:T(8,128)(2,1)S(1)}, bf16[128,768]{1,0:T(8,128)(2,1)S(1)}, u32[]{:S(2)}, u32[]{:S(2)}) collective-permute-start(bf16[128,768]{1,0:T(8,128)(2,1)S(1)} %get-tuple-element.157), channel_id=1, source_target_pairs={{0,16},{4,20},{8,24},{12,28},{16,0},{20,4},{24,8},{28,12},{1,17},{... | collective-permute-start | bytes 589832 | tf_op jit(solution)/shard_map/ppermute | solution.py:24
  153.6 11.3 %collective-permute-start.39 = (bf16[128,768]{1,0:T(8,128)(2,1)S(1)}, bf16[128,768]{1,0:T(8,128)(2,1)S(1)}, u32[]{:S(2)}, u32[]{:S(2)}) collective-permute-start(bf16[128,768]{1,0:T(8,128)(2,1)S(1)} %get-tuple-element.158), channel_id=1, source_target_pairs={{0,24},{4,28},{8,16},{12,20},{16,8},{20,12},{24,0},{28,4},{1,25},{... | collective-permute-start | bytes 589832 | tf_op jit(solution)/shard_map/ppermute | solution.py:24
  156.8 11.0 %collective-permute-start.41 = (bf16[112,768]{1,0:T(8,128)(2,1)S(1)}, bf16[112,768]{1,0:T(8,128)(2,1)S(1)}, u32[]{:S(2)}, u32[]{:S(2)}) collective-permute-start(bf16[112,768]{1,0:T(8,128)(2,1)S(1)} %get-tuple-element.160), channel_id=1, source_target_pairs={{0,2},{1,3},{2,0},{3,1},{4,6},{5,7},{6,4},{7,5},{8,10},{9,11},{10,... | collective-permute-start | bytes 516104 | tf_op jit(solution)/shard_map/ppermute | solution.py:24
  169.5 9.8 %collective-permute-start.43 = (bf16[112,768]{1,0:T(8,128)(2,1)S(1)}, bf16[112,768]{1,0:T(8,128)(2,1)S(1)}, u32[]{:S(2)}, u32[]{:S(2)}) collective-permute-start(bf16[112,768]{1,0:T(8,128)(2,1)S(1)} %shard_map.329.refs_0_), channel_id=1, source_target_pairs={{0,16},{4,20},{8,24},{12,28},{16,0},{20,4},{24,8},{28,12},{1,17},{... | collective-permute-start | bytes 516104 | tf_op jit(solution)/shard_map/ppermute | solution.py:24
  172.8 11.0 %collective-permute-start.45 = (bf16[112,768]{1,0:T(8,128)(2,1)S(1)}, bf16[112,768]{1,0:T(8,128)(2,1)S(1)}, u32[]{:S(2)}, u32[]{:S(2)}) collective-permute-start(bf16[112,768]{1,0:T(8,128)(2,1)S(1)} %shard_map.329.refs_0_), channel_id=1, source_target_pairs={{0,4},{4,0},{8,12},{12,8},{16,20},{20,16},{24,28},{28,24},{1,5},{5... | collective-permute-start | bytes 516104 | tf_op jit(solution)/shard_map/ppermute | solution.py:24
  (26 other events, 142.1 us)

commit v3 on v2

--- a/solution.py
+++ b/solution.py
@@ -156,6 +156,12 @@
     out[...] = block[...]
 
 
+def split_rows(block, *outs):
+    n = outs[0].shape[0]
+    for m, out in enumerate(outs):
+        out[...] = block[m * n : (m + 1) * n]
+
+
 def sort_pieces(own, near, far, farthest, projections, others, sent):
     half = farthest.shape[0]
     for r, piece in enumerate((own, near, far, farthest)):
@@ -165,15 +171,20 @@
     sent[...] = far[half:]
 
 
-def assemble(own, own_last, other, other_last, *weights):
+def assemble(*refs):
+    own, own_last, other, other_last, weights = refs[0], refs[1:4], refs[4], refs[5:8], refs[8:]
     core, _, _, _, place = places()
     half = weights[0].shape[0] // 8
     for c, (pieces, last) in enumerate(((own, own_last), (other, other_last))):
         for r in range(4):
-            piece = last if r == 3 else pieces.at[r]
             base = rows_from((2 * (place ^ r) + (core ^ c)) * half, half)
             for m, weight in enumerate(weights):
-                weight[base] = piece[m * half : (m + 1) * half]
+                weight[base] = last[m][...] if r == 3 else pieces[r, m * half : (m + 1) * half]
+
+
+def stack(own, near, far, farthest, out):
+    for r, piece in enumerate((own, near, far, farthest)):
+        out[r] = piece[...]
 
 
 def project(seen, *refs):
@@ -243,8 +254,14 @@
         grad_keys_values[:, span] += dot(grad_scores, queries[:, span])
 
 
+def beside(rows, out):
+    tokens, part = out.shape[0], rows.shape[1]
+    for t in range(CHIPS):
+        out[:, t * part : (t + 1) * part] = rows[t * tokens : (t + 1) * tokens]
+
+
 def attend_all(queries, kv_own, kv_far, seg_own, seg_far, context, probs, *scratch):
-    keys_values, seg_key, seg_query = scratch
+    keys_values, seg_key, seg_query, rows = scratch
     count = kv_own.shape[0]
     tokens = seg_own.shape[1]
     keys_values[:count] = kv_own[...]
@@ -253,7 +270,8 @@
     seg_key[CHIPS:] = seg_far[:CHIPS]
     for s in range(CHIPS):
         seg_query[:, s * tokens : (s + 1) * tokens] = seg_own[s : s + 1]
-    attend(queries, seg_query, keys_values, seg_key, context, probs)
+    attend(queries, seg_query, keys_values, seg_key, rows, probs)
+    beside(rows, context)
 
 
 def context_back(g0, g1, g2, g3, w_output, grad_low, grad_context):
@@ -265,7 +283,7 @@
 
 
 def attend_back_all(queries, kv_own, kv_far, g0, g1, g2, g3, w_output, probs, *refs):
-    grad_low, grad_queries, grad_own, grad_far, keys_values, grad_context, total = refs
+    grad_low, grad_queries, grad_own, *grad_far, keys_values, grad_context, total = refs
     count = kv_own.shape[0]
     keys_values[:count] = kv_own[...]
     keys_values[count:] = kv_far[...]
@@ -273,7 +291,9 @@
     total[...] = jnp.zeros(total.shape, WIDE)
     attend_back(queries, keys_values, grad_context, probs, grad_queries, total)
     grad_own[...] = total[:count]
-    grad_far[...] = total[count:].astype(LOW)
+    tokens = count // CHIPS
+    for t, out in enumerate(grad_far):
+        out[...] = total[count + t * tokens : count + (t + 1) * tokens].astype(LOW)
 
 
 def attend_back_block(queries, keys_values, grads, probs, grad_queries, grad_keys_values):
@@ -339,12 +359,11 @@
     context_low, unit_one, inverse_one, normed_low, activated, slope = outs[:6]
     own, sent, stage = outs[6], outs[7:10], outs[10]
     _, _, _, chip, _ = places()
-    count, part = c0.shape
-    tokens = count // CHIPS
+    tokens, part = c0.shape[0], c0.shape[1] // CHIPS
     for s, block in enumerate((c0, c1, c2, c3)):
         for t in range(CHIPS):
             stage[chip ^ s, t * tokens : (t + 1) * tokens] = block[
-                (t ^ s) * tokens : ((t ^ s) + 1) * tokens
+                :, (t ^ s) * part : ((t ^ s) + 1) * part
             ]
     for k in range(CHIPS):
         context_low[:, k * part : (k + 1) * part] = stage[k]
@@ -388,24 +407,30 @@
     sums[3:] = jnp.zeros((5, sums.shape[1]), WIDE)
 
 
-def backward_second(g0, g1, g2, g3, slope, w_outer, w_inner, grad_outer, grad_inner, sums, *outs):
-    tokens = g0.shape[0]
-    for s, block in enumerate((g0, g1, g2, g3)):
-        grad_outer[s * tokens : (s + 1) * tokens] = block[...]
-    grad_inner[...] = (dot_rt(grad_outer[...], w_outer[...]) * slope[...]).astype(LOW)
+def backward_second(g0, g1, g2, g3, slope, w_outer, w_inner, grad_inner, sums, *outs):
+    grad_outer = jnp.concatenate([g0[...], g1[...], g2[...], g3[...]])
+    grad_inner[...] = (dot_rt(grad_outer, w_outer[...]) * slope[...]).astype(LOW)
     parted(dot_rt(grad_inner[...], w_inner[...]), outs[0], outs[1:])
     sums[...] = jnp.sum(grad_inner[...].astype(WIDE), 0, keepdims=True)
 
 
-def weight_grads(activated, grad_outer, normed_low, grad_inner, keep, send, stage):
+def cut_rows(stage, keep, sent):
     core, _, _, _, place = places()
-    half = keep.shape[1] // 2
-    for m, (left, right) in enumerate(((activated, grad_outer), (normed_low, grad_inner))):
-        stage[...] = dot_lt(left[...], right[...]).astype(LOW)
-        for r in range(4):
-            for c, out in enumerate((keep, send)):
-                start = (2 * (place ^ r) + (core ^ c)) * half
-                out[r, m * half : (m + 1) * half] = stage[rows_from(start, half)]
+    half = keep.shape[1]
+    for r in range(4):
+        for c, out in enumerate((keep.at[r], sent[r])):
+            out[...] = stage[rows_from((2 * (place ^ r) + (core ^ c)) * half, half)]
+
+
+def outer_grads(activated, g0, g1, g2, g3, keep, send, stage):
+    grad_outer = jnp.concatenate([g0[...], g1[...], g2[...], g3[...]])
+    stage[...] = dot_lt(activated[...], grad_outer).astype(LOW)
+    cut_rows(stage, keep, [send.at[r] for r in range(4)])
+
+
+def inner_grads(normed_low, grad_inner, keep, s0, s1, s2, s3, stage):
+    stage[...] = dot_lt(normed_low[...], grad_inner[...]).astype(LOW)
+    cut_rows(stage, keep, (s0, s1, s2, s3))
 
 
 def norm_backward(grad_summed, own, s1, s2, s3, unit_one, inverse_one, vec, grad_own, grad_low, sums):
@@ -431,15 +456,15 @@
             out[...] = dot_lt(context_low[...], block).astype(LOW)
 
 
-def projection_grads(
-    rows_in, grad_queries, grad_kv, grad_kv_far, grad_o, sums_one, sums_two, sums_inner, *outs
-):
+def projection_grads(rows_in, grad_queries, grad_kv, f0, f1, f2, f3, grad_o, *refs):
+    (sums_one, sums_two, sums_inner), outs = refs[:3], refs[3:]
     grad_qkv, keep, send, stage = outs
     core, _, _, _, place = places()
     part = grad_queries.shape[1]
     width = 4 * part
     grad_qkv[:, :part] = grad_queries[...]
-    grad_qkv[:, part:] = (grad_kv[...] + grad_kv_far[...].astype(WIDE)).astype(LOW)
+    far = jnp.concatenate([f0[...], f1[...], f2[...], f3[...]]).astype(WIDE)
+    grad_qkv[:, part:] = (grad_kv[...] + far).astype(LOW)
     stage[:, : 3 * part] = dot_lt(rows_in[...], grad_qkv[...]).astype(LOW)
     stage[:, 3 * part :] = grad_o[...]
     half = part // 2
@@ -469,7 +494,8 @@
     own[...] += grad_residual[...]
 
 
-def add_tokens(own, s1, s2, s3, out):
+def add_tokens(own, s1, s2, s3, out, done):
+    done[...] = jnp.zeros(done.shape, WIDE)
     out[0] = total_of(own, (s1, s2, s3)).astype(LOW)
 
 
@@ -480,11 +506,10 @@
         send[r] = total[2 * r + 1].astype(LOW)
 
 
-def add_near_both(kept, received, *outs):
-    half = outs[0].shape[1]
-    for m in range(2):
-        rows = pl.ds(m * half, half)
-        add_near(kept.at[:, rows], received.at[:, rows], *outs[2 * m : 2 * m + 2])
+def add_near_parts(kept, r0, r1, r2, r3, keep, send):
+    for r, received in enumerate((r0, r1, r2, r3)):
+        out = (keep, send)[r % 2]
+        out[r // 2] = (kept[r].astype(WIDE) + received[...].astype(WIDE)).astype(LOW)
 
 
 def add_far(kept, received, keep, send):
@@ -502,15 +527,21 @@
     out[...] = (kept[...].astype(WIDE) + received[...].astype(WIDE)).astype(LOW)
 
 
-def unpack_mlp(*refs):
-    pieces, blocks, (outer, inner, stage) = refs[:8], refs[8:16], refs[16:]
+def add_beside(other, kept, received, out):
+    half = kept.shape[0]
+    out[:half] = other[...]
+    add_last(kept, received, out.at[half:])
+
+
+def unpack_mlp(own, other, outer, inner, done, stage):
     core, _, _, chip, _ = places()
-    half, width = pieces[0].shape
+    half, width = own.shape[1] // 2, own.shape[2]
     part = 2 * half
-    for i, (piece, block) in enumerate(zip(pieces, blocks)):
-        far, c = chip ^ (i % 4), core ^ (i // 4)
-        outer[rows_from((2 * far + c) * half, half)] = piece[...].astype(WIDE)
-        stage[c, far] = block[...]
+    for s in range(CHIPS):
+        for m, blocks in enumerate((own, other)):
+            far, c = chip ^ s, core ^ m
+            outer[rows_from((2 * far + c) * half, half)] = blocks[s, :half].astype(WIDE)
+            stage[c, far] = blocks[s, half:]
     for c in range(2):
         for p in range(CHIPS):
             for k in range(4):
@@ -518,23 +549,23 @@
                 inner[c * half : (c + 1) * half, start : start + part] = stage[
                     c, p, :, k * part : (k + 1) * part
                 ].astype(WIDE)
+    done[...] = jnp.zeros(done.shape, WIDE)
 
 
 def unpack_rest(*refs):
     pieces, mats, vectors, (b_query, b_value, b_inner, stage, small) = (
-        refs[:8],
-        refs[8:12],
-        refs[12:18],
-        refs[18:],
+        refs[:2],
+        refs[2:6],
+        refs[6:12],
+        refs[12:],
     )
     core, _, _, chip, place = places()
     part = mats[0].shape[0]
     half = part // 2
-    for i, piece in enumerate(pieces):
-        far = chip ^ (i % 4)
-        stage[core ^ (i // 4), far] = piece[:half]
-        if i < 4:
-            small[far] = piece[half:, :part].astype(WIDE)
+    for s in range(CHIPS):
+        for m, blocks in enumerate(pieces):
+            stage[core ^ m, s] = blocks[s, :half]
+        small[s] = pieces[0][s, half:, :part].astype(WIDE)
     for c in range(2):
         for k in range(CHIPS):
             for j, out in enumerate(mats):
@@ -654,7 +685,7 @@
     if groups == 1:
         context, probs = kernel(
             attend_all,
-            [shape((count, part)), shape((heads, 2 * count, count))],
+            [shape((tokens, width)), shape((heads, 2 * count, count))],
             queries,
             kv_own,
             kv_far,
@@ -664,6 +695,7 @@
                 pltpu.VMEM((2 * count, 2 * part), LOW),
                 pltpu.VMEM((2 * CHIPS, tokens), WIDE),
                 pltpu.VMEM((1, count), WIDE),
+                pltpu.VMEM((count, part), LOW),
             ],
             room=24,
         )
@@ -672,12 +704,15 @@
         seg_key = jnp.concatenate([segs[:CHIPS], seg_far[:CHIPS]])
         kv = lax.all_gather(kv, "ctx", axis=0, tiled=True, axis_index_groups=lines)
         seg_key = lax.all_gather(seg_key, "ctx", axis=0, tiled=True, axis_index_groups=lines)
-        context, probs = attention(queries, segs[:CHIPS].reshape(1, count), kv, seg_key)
+        rows, probs = attention(queries, segs[:CHIPS].reshape(1, count), kv, seg_key)
+        (context,) = kernel(beside, [shape((tokens, width))], rows)
 
     contexts = [context] + chips(context)
-    (last,) = kernel(passed, [shape(last.shape)], last, after=(context,))
+    last = kernel(
+        split_rows, [shape((half, width))] * 3, last, after=(context,)
+    )
     w_output, w_inner, w_outer = kernel(
-        assemble, [shape((width, width))] * 3, others, last, joined(others), joined(last)
+        assemble, [shape((width, width))] * 3, others, *last, joined(others), *map(joined, last)
     )
     context_low, unit_one, inverse_one, normed_low, activated, slope, *outer_sent = kernel(
         forward,
@@ -716,23 +751,24 @@
         cotangent,
         last=(0,),
     )
-    grad_outer, grad_inner, sums_inner, inner_own, *inner_sent = kernel(
+    grads_outer = [grad_outer] + chips(grad_outer)
+    outer_kept, outer_sent = kernel(
+        outer_grads,
+        [shape((4, half, width))] * 2,
+        activated,
+        *grads_outer,
+        scratch=[pltpu.VMEM((width, width), LOW)],
+    )
+    grad_inner, sums_inner, inner_own, *inner_sent = kernel(
         backward_second,
-        [
-            shape((count, width)),
-            shape((count, width)),
-            shape((1, width), WIDE),
-            shape((tokens, width), WIDE),
-        ]
+        [shape((count, width)), shape((1, width), WIDE), shape((tokens, width), WIDE)]
         + [shape((tokens, width))] * 3,
-        grad_outer,
-        *chips(grad_outer),
+        *grads_outer,
         slope,
         w_outer,
         w_inner,
         room=12,
     )
-
     inner_far = exchanged(inner_sent)
 
     def near_sum(kept, sent):
@@ -750,19 +786,20 @@
             total = lax.psum(total.astype(WIDE), "ctx", axis_index_groups=lines).astype(LOW)
         return total
 
-    kept, sent = kernel(
-        weight_grads,
-        [shape((4, 2 * half, width))] * 2,
-        activated,
-        grad_outer,
+    inner_kept, *inner_sent = kernel(
+        inner_grads,
+        [shape((4, half, width))] + [shape((half, width))] * 4,
         normed_low,
         grad_inner,
         scratch=[pltpu.VMEM((width, width), LOW)],
-        room=12,
-    )
-    outer_kept, outer_sent, inner_kept, inner_sent = mlp_near = kernel(
-        add_near_both, [shape((2, half, width))] * 4, kept, partner(sent, "ctx", CORE)
-    )
+    )
+    inner_kept, inner_sent = kernel(
+        add_near_parts,
+        [shape((2, half, width))] * 2,
+        inner_kept,
+        *(partner(block, "ctx", CORE) for block in inner_sent),
+    )
+    outer_kept, outer_sent = near_sum(outer_kept, outer_sent)
     outer_kept, outer_sent, inner_sent = kernel(
         add_far_passing,
         [shape((half, width))] * 2 + [shape((2, half, width))],
@@ -770,8 +807,8 @@
         partner(outer_sent, "fsdp", 1),
         inner_sent,
     )
+    inner_far_sum = far_sum(inner_kept, inner_sent)
     outer_total = last_sum(outer_kept, outer_sent)
-    mlp_far = far_sum(inner_kept, inner_sent)
     grad_residual, grad_low, sums_two = kernel(
         norm_backward,
         [shape((tokens, width), WIDE), shape((tokens, width)), shape((8, width), WIDE)],
@@ -781,18 +818,17 @@
         unit_one,
         inverse_one,
         vec,
-        after=tuple(mlp_near),
     )
     grads_low = [grad_low] + chips(grad_low)
     if groups == 1:
-        grad_low, grad_queries, grad_kv, grad_kv_sent = kernel(
+        grad_low, grad_queries, grad_kv, *grad_kv_sent = kernel(
             attend_back_all,
             [
                 shape((count, width)),
                 shape((count, part)),
                 shape((count, 2 * part), WIDE),
-                shape((count, 2 * part)),
-            ],
+            ]
+            + [shape((tokens, 2 * part))] * CHIPS,
             queries,
             kv_own,
             kv_far,
@@ -805,7 +841,7 @@
                 pltpu.VMEM((2 * count, 2 * part), WIDE),
             ],
             room=24,
-            after=(outer_total, *mlp_far),
+            after=(outer_kept,),
         )
     else:
         grad_low, grad_context = kernel(
@@ -820,10 +856,9 @@
             tiled=True,
             axis_index_groups=lines,
         )
-        grad_kv, grad_kv_sent = grad_kv[0], grad_kv[1].astype(LOW)
-    grad_kv_far = partner(grad_kv_sent, "ctx", CORE)
+        grad_kv, grad_kv_sent = grad_kv[0], jnp.split(grad_kv[1].astype(LOW), CHIPS)
+    grad_kv_far = [joined(block) for block in grad_kv_sent]
     (grad_o,) = kernel(output_grads, [shape((width, part))], context_low, grad_low)
-    inner_total = last_sum(*mlp_far)
     cut = shape((4, half + 16, width))
     grad_qkv, rest_kept, rest_sent = kernel(
         projection_grads,
@@ -831,12 +866,13 @@
         rows_in,
         grad_queries,
         grad_kv,
-        grad_kv_far,
+        *grad_kv_far,
         grad_o,
         sums_one,
         sums_two,
         sums_inner,
         scratch=[pltpu.VMEM((width, width), LOW)],
+        after=(outer_total, inner_far_sum[0]),
     )
     rest_near = near_sum(rest_kept, rest_sent)
     input_own, *input_sent = kernel(
@@ -849,40 +885,50 @@
     )
     input_far = exchanged(input_sent)
 
-    outer_chips = [outer_total] + chips(outer_total)
-    inner_chips = [inner_total] + chips(inner_total)
-    rest_total = last_sum(
-        *far_sum(*rest_near, after=(inner_total,)),
-        after=(*outer_chips[1:], *inner_chips[1:], *input_far),
-    )
-    rest_chips = [rest_total] + chips(rest_total)
-    (grad_input,) = kernel(
+    def shared(total, after=()):
+        (found,) = kernel(stack, [shape((CHIPS,) + total.shape)], total, *chips(total), after=after)
+        return found, joined(found)
+
+    rest_far = far_sum(*rest_near)
+    (mlp_total,) = kernel(
+        add_beside,
+        [shape((2 * half, width))],
+        outer_total,
+        inner_far_sum[0],
+        partner(inner_far_sum[1], "fsdp", 2),
+        after=(*input_far, rest_far[0]),
+    )
+    rest_total = last_sum(*rest_far)
+    rest_all = lax.all_gather(rest_total, "ctx", axis_index_groups=teams)
+    mlp_blocks = shared(mlp_total, after=(rest_all,))
+    grad_input, done_input = kernel(
         add_tokens,
-        [shape((1, tokens, width))],
+        [shape((1, tokens, width)), shape((8, 128), WIDE)],
         input_own,
         *input_far,
         last=(0,),
         after=(rest_total,),
     )
-    g_outer, g_inner = kernel(
+    g_outer, g_inner, done_mlp = kernel(
         unpack_mlp,
-        [shape((hidden, width), WIDE), shape((part, 4 * hidden), WIDE)],
-        *outer_chips,
-        *map(joined, outer_chips),
-        *inner_chips,
-        *map(joined, inner_chips),
+        [
+            shape((hidden, width), WIDE),
+            shape((part, 4 * hidden), WIDE),
+            shape((8, 128), WIDE),
+        ],
+        *mlp_blocks,
         last=(0, 1),
         scratch=[pltpu.VMEM((2, CHIPS, half, width), LOW)],
         room=12,
-        after=(rest_total,),
+        after=(rest_all,),
     )
     g_query, g_key, g_value, g_output, *vec, g_b_query, g_b_value, g_b_inner = kernel(
         unpack_rest,
         [shape((part, width), WIDE)] * 4
         + [shape((part,), WIDE)] * 8
         + [shape((width,), WIDE)],
-        *rest_chips,
-        *map(joined, rest_chips),
+        rest_all,
+        joined(rest_all),
         last=range(13),
         scratch=[
             pltpu.VMEM((2, CHIPS, half, width), LOW),

time: 186 us -> 174 us (0.935)
  waiting for transfers between devices: 85.2 us -> 70.9 us
  blocking collectives: 11.8 us -> 25.6 us
  starting transfers between devices: 58.2 us -> 46.6 us
    ppermute x57 -> x50, waiting for transfers between devices: 85.2 us -> 70.9 us  [partner(): return lax.ppermute(block, axis, [(i, i ^ bit) for i in devices])]
    all_gather x0 -> x1, blocking collectives: none -> 13.7 us  [per_device(): rest_all = lax.all_gather(rest_total, 'ctx', axis_index_groups=teams)]
    ppermute x57 -> x50, starting transfers between devices: 58.2 us -> 46.6 us  [partner(): return lax.ppermute(block, axis, [(i, i ^ bit) for i in devices])]
    pallas_call x28 -> x31, Pallas kernels: 29.5 us -> 30 us  [kernel(): pl.pallas_call(step, out_shape=[o if n in last else pltpu.VMEM(o.shape, o...]
  transfers between devices with their start and end apart: 57 -> 50, of which waited for: 24 -> 22; matrix products, arithmetic and copies ran while one was open for 0% -> 0% of each run, Pallas kernels for 6% -> 11%
where the time goes in v3:
time: 174 us
  waiting for transfers between devices  70.9 us (41%)
  starting transfers between devices  46.6 us (27%)
  Pallas kernels  30 us (17%)
  blocking collectives  25.6 us (15%)
    ppermute x50, waiting for transfers between devices, partner(): return lax.ppermute(block, axis, [(i, i ^ bit) for i in devices])  70.9 us
    ppermute x50, starting transfers between devices, partner(): return lax.ppermute(block, axis, [(i, i ^ bit) for i in devices])  46.6 us
    pallas_call x31, Pallas kernels, kernel(): pl.pallas_call(step, out_shape=[o if n in last else pltpu.VMEM(o.shape, o...  30 us
    all_gather x1, blocking collectives, per_device(): rest_all = lax.all_gather(rest_total, 'ctx', axis_index_groups=teams)  13.7 us
    all_gather x1, blocking collectives, per_device(): seen = lax.all_gather(own, 'ctx', axis_index_groups=teams)  11.8 us
  transfers between devices with their start and end apart: 50, of which 22 were waited for; matrix products, arithmetic and copies ran while one was open for 0% of the time, Pallas kernels for 11%

profile of v3, /device:TPU:0, one launch (start us, length us, event | category | flops | bytes accessed | tf_op | source)
XLA Modules:
  0.0 174.1 jit_solution(3886349238482544862)
XLA Ops:
  0.7 1.7 shard_map.306.refs_1_.refs_0_
  2.3 3.1 %collective-permute-start = (bf16[384,768]{1,0:T(8,128)(2,1)S(1)}, bf16[384,768]{1,0:T(8,128)(2,1)S(1)}, u32[]{:S(2)}, u32[]{:S(2)}) collective-permute-start(bf16[384,768]{1,0:T(8,128)(2,1)S(1)} %shard_map.306.refs_1_.refs_0_), channel_id=1, source_target_pairs={{0,1},{1,0},{2,3},{3,2},{4,5},{5,4},{6,7},{7,6},{8,9},{9,8},{10,11... | collective-permute-start | bytes 1769480 | tf_op jit(solution)/shard_map/ppermute | solution.py:24
  5.4 2.6 %collective-permute-start.1 = (bf16[384,768]{1,0:T(8,128)(2,1)S(1)}, bf16[384,768]{1,0:T(8,128)(2,1)S(1)}, u32[]{:S(2)}, u32[]{:S(2)}) collective-permute-start(bf16[384,768]{1,0:T(8,128)(2,1)S(1)} %shard_map.306.refs_1_.refs_0_), channel_id=1, source_target_pairs={{0,2},{1,3},{2,0},{3,1},{4,6},{5,7},{6,4},{7,5},{8,10},{9,11},{10,... | collective-permute-start | bytes 1769480 | tf_op jit(solution)/shard_map/ppermute | solution.py:24
  9.0 11.8 %all-gather = bf16[576,768]{1,0:T(8,128)(2,1)S(1)} all-gather(bf16[144,768]{1,0:T(8,128)(2,1)S(1)} %shard_map.305), channel_id=2, replica_groups={{0,8,16,24},{4,12,20,28},{1,9,17,25},{5,13,21,29},{2,10,18,26},{6,14,22..., dimensions={0}, use_global_device_ids=true | all-gather | bytes 1105920 | tf_op jit(solution)/shard_map/all_gather | solution.py:631
  21.1 15.7 %collective-permute-done.2.refs_3_ = bf16[96,768]{1,0:T(8,128)(2,1)S(1)} collective-permute-done((bf16[96,768]{1,0:T(8,128)(2,1)S(1)}, bf16[96,768]{1,0:T(8,128)(2,1)S(1)}, u32[]{:S(2)}, u32[]{:S(2)}) %collective-permute-start.2) | collective-permute-done | bytes 147488 | tf_op jit(solution)/shard_map/ppermute | solution.py:24
  38.2 3.2 %collective-permute-start.9 = (bf16[288,768]{1,0:T(8,128)(2,1)S(1)}, bf16[288,768]{1,0:T(8,128)(2,1)S(1)}, u32[]{:S(2)}, u32[]{:S(2)}) collective-permute-start(bf16[288,768]{1,0:T(8,128)(2,1)S(1)} %get-tuple-element.115), channel_id=1, source_target_pairs={{0,1},{1,0},{2,3},{3,2},{4,5},{5,4},{6,7},{7,6},{8,9},{9,8},{10,11... | collective-permute-start | bytes 1327112 | tf_op jit(solution)/shard_map/ppermute | solution.py:24
  44.2 3.9 %shard_map.310 = (bf16[128,768]{1,0:T(8,128)(2,1)S(1)}, bf16[3,1024,512]{2,1,0:T(8,128)(2,1)S(1)}) custom-call(bf16[512,192]{1,0:T(8,128)(2,1)S(1)} %get-tuple-element.109.refs_0_.refs_1_, bf16[512,384]{1,0:T(8,128)(2,1)S(1)} %get-tuple-element.110.refs_1_.refs_2_, bf16[512,384]{1,0:T(8,128)(2,1)S(1)} %collective-permute-done.4.refs_2_.refs_3_, ...), custom_call_target="tpu_custom_call" | custom-call | flops 1 | bytes 1 | tf_op jit(solution)/shard_map/pallas_call | solution.py:54
  48.1 3.7 %collective-permute-done.9.refs_1_ = bf16[288,768]{1,0:T(8,128)(2,1)S(1)} collective-permute-done((bf16[288,768]{1,0:T(8,128)(2,1)S(1)}, bf16[288,768]{1,0:T(8,128)(2,1)S(1)}, u32[]{:S(2)}, u32[]{:S(2)}) %collective-permute-start.9) | collective-permute-done | bytes 442400 | tf_op jit(solution)/shard_map/ppermute | solution.py:24
  57.6 2.6 %collective-permute-done.6.refs_1_ = bf16[128,768]{1,0:T(8,128)(2,1)S(1)} collective-permute-done((bf16[128,768]{1,0:T(8,128)(2,1)S(1)}, bf16[128,768]{1,0:T(8,128)(2,1)S(1)}, u32[]{:S(2)}, u32[]{:S(2)}) %collective-permute-start.6) | collective-permute-done | bytes 196640 | tf_op jit(solution)/shard_map/ppermute | solution.py:24
  60.2 4.6 %collective-permute-done.7.refs_2_ = bf16[128,768]{1,0:T(8,128)(2,1)S(1)} collective-permute-done((bf16[128,768]{1,0:T(8,128)(2,1)S(1)}, bf16[128,768]{1,0:T(8,128)(2,1)S(1)}, u32[]{:S(2)}, u32[]{:S(2)}) %collective-permute-start.7) | collective-permute-done | bytes 196640 | tf_op jit(solution)/shard_map/ppermute | solution.py:24
  64.8 3.2 %shard_map.313 = (bf16[512,768]{1,0:T(8,128)(2,1)S(1)}, f32[128,768]{1,0:T(8,128)S(1)}, f32[128,1]{1,0:T(8,128)S(1)}, bf16[512,768]{1,0:T(8,128)(2,1)S(1)}, bf16...) custom-call(bf16[128,768]{1,0:T(8,128)(2,1)S(1)} %get-tuple-element., ...), custom_call_target="tpu_custom_call" | custom-call | flops 1 | bytes 1 | tf_op jit(solution)/shard_map/pallas_call | solution.py:54
  71.5 4.1 %collective-permute-done.14.refs_1_ = bf16[128,768]{1,0:T(8,128)(2,1)S(1)} collective-permute-done((bf16[128,768]{1,0:T(8,128)(2,1)S(1)}, bf16[128,768]{1,0:T(8,128)(2,1)S(1)}, u32[]{:S(2)}, u32[]{:S(2)}) %collective-permute-start.14) | collective-permute-done | bytes 196640 | tf_op jit(solution)/shard_map/ppermute | solution.py:24
  75.7 3.6 %collective-permute-done.15.refs_2_ = bf16[128,768]{1,0:T(8,128)(2,1)S(1)} collective-permute-done((bf16[128,768]{1,0:T(8,128)(2,1)S(1)}, bf16[128,768]{1,0:T(8,128)(2,1)S(1)}, u32[]{:S(2)}, u32[]{:S(2)}) %collective-permute-start.15) | collective-permute-done | bytes 196640 | tf_op jit(solution)/shard_map/ppermute | solution.py:24
  80.9 1.5 collective-permute-start.18
  83.8 2.9 %collective-permute-done.17.refs_2_.refs_1_ = bf16[128,768]{1,0:T(8,128)(2,1)S(1)} collective-permute-done((bf16[128,768]{1,0:T(8,128)(2,1)S(1)}, bf16[128,768]{1,0:T(8,128)(2,1)S(1)}, u32[]{:S(2)}, u32[]{:S(2)}) %collective-permute-start.17) | collective-permute-done | bytes 196640 | tf_op jit(solution)/shard_map/ppermute | solution.py:24
  86.7 3.3 %collective-permute-done.18.refs_3_.refs_2_ = bf16[128,768]{1,0:T(8,128)(2,1)S(1)} collective-permute-done((bf16[128,768]{1,0:T(8,128)(2,1)S(1)}, bf16[128,768]{1,0:T(8,128)(2,1)S(1)}, u32[]{:S(2)}, u32[]{:S(2)}) %collective-permute-start.18) | collective-permute-done | bytes 196640 | tf_op jit(solution)/shard_map/ppermute | solution.py:24
  90.9 1.6 shard_map.317
  94.3 1.8 %collective-permute-start.30 = (bf16[128,768]{1,0:T(8,128)(2,1)S(1)}, bf16[128,768]{1,0:T(8,128)(2,1)S(1)}, u32[]{:S(2)}, u32[]{:S(2)}) collective-permute-start(bf16[128,768]{1,0:T(8,128)(2,1)S(1)} %get-tuple-element.154), channel_id=1, source_target_pairs={{0,24},{4,28},{8,16},{12,20},{16,8},{20,12},{24,0},{28,4},{1,25},{... | collective-permute-start | bytes 589832 | tf_op jit(solution)/shard_map/ppermute | solution.py:24
  96.4 1.8 %collective-permute-start.21 = (bf16[2,96,768]{2,1,0:T(8,128)(2,1)S(1)}, bf16[2,96,768]{2,1,0:T(8,128)(2,1)S(1)}, u32[]{:S(2)}, u32[]{:S(2)}) collective-permute-start(bf16[2,96,768]{2,1,0:T(8,128)(2,1)S(1)} %get-tuple-element.135), channel_id=1, source_target_pairs={{0,1},{1,0},{2,3},{3,2},{4,5},{5,4},{6,7},{7,6},{8,9},{9,8},{10,11... | collective-permute-start | bytes 884744 | tf_op jit(solution)/shard_map/ppermute | solution.py:24
  100.3 4.6 %collective-permute-done.29.refs_3_ = bf16[128,768]{1,0:T(8,128)(2,1)S(1)} collective-permute-done((bf16[128,768]{1,0:T(8,128)(2,1)S(1)}, bf16[128,768]{1,0:T(8,128)(2,1)S(1)}, u32[]{:S(2)}, u32[]{:S(2)}) %collective-permute-start.29) | collective-permute-done | bytes 196640 | tf_op jit(solution)/shard_map/ppermute | solution.py:24
  109.6 1.8 %collective-permute-start.27 = (bf16[2,96,768]{2,1,0:T(8,128)(2,1)S(1)}, bf16[2,96,768]{2,1,0:T(8,128)(2,1)S(1)}, u32[]{:S(2)}, u32[]{:S(2)}) collective-permute-start(bf16[2,96,768]{2,1,0:T(8,128)(2,1)S(1)} %get-tuple-element.148), channel_id=1, source_target_pairs={{0,1},{1,0},{2,3},{3,2},{4,5},{5,4},{6,7},{7,6},{8,9},{9,8},{10,11... | collective-permute-start | bytes 884744 | tf_op jit(solution)/shard_map/ppermute | solution.py:24
  113.6 3.9 %collective-permute-done.32.refs_6_ = bf16[128,768]{1,0:T(8,128)(2,1)S(1)} collective-permute-done((bf16[128,768]{1,0:T(8,128)(2,1)S(1)}, bf16[128,768]{1,0:T(8,128)(2,1)S(1)}, u32[]{:S(2)}, u32[]{:S(2)}) %collective-permute-start.32) | collective-permute-done | bytes 196640 | tf_op jit(solution)/shard_map/ppermute | solution.py:24
  117.5 5.4 %shard_map.324 = (bf16[512,768]{1,0:T(8,128)(2,1)S(1)}, bf16[512,192]{1,0:T(8,128)(2,1)S(1)}, f32[512,384]{1,0:T(8,128)S(1)}, bf16[128,384]{1,0:T(8,128)(2,1)S(1...) custom-call(bf16[96,768]{1,0:T(8,128)(2,1)S(1)} %get-tuple-element.145.refs_0_, ...), custom_call_target="tpu_custom_call" | custom-call | flops 1 | bytes 1 | tf_op jit(solution)/shard_map/pallas_call | solution.py:54
  126.6 1.8 %collective-permute-done.38.refs_1_ = bf16[4,112,768]{2,1,0:T(8,128)(2,1)S(1)} collective-permute-done((bf16[4,112,768]{2,1,0:T(8,128)(2,1)S(1)}, bf16[4,112,768]{2,1,0:T(8,128)(2,1)S(1)}, u32[]{:S(2)}, u32[]{:S(2)}) %collective-permute-start.38) | collective-permute-done | bytes 688160 | tf_op jit(solution)/shard_map/ppermute | solution.py:24
  128.6 1.8 %collective-permute-start.39 = (bf16[2,112,768]{2,1,0:T(8,128)(2,1)S(1)}, bf16[2,112,768]{2,1,0:T(8,128)(2,1)S(1)}, u32[]{:S(2)}, u32[]{:S(2)}) collective-permute-start(bf16[2,112,768]{2,1,0:T(8,128)(2,1)S(1)} %get-tuple-element.172.refs_1_), channel_id=1, source_target_pairs={{0,1},{1,0},{2,3},{3,2},{4,5},{5,4},{6,7},{7,6},{8,9},{9,8},{10,11... | collective-permute-start | bytes 1032200 | tf_op jit(solution)/shard_map/ppermute | solution.py:24
  133.0 1.7 collective-permute-start.43
  136.0 6.1 %collective-permute-done.39.refs_1_ = bf16[2,112,768]{2,1,0:T(8,128)(2,1)S(1)} collective-permute-done((bf16[2,112,768]{2,1,0:T(8,128)(2,1)S(1)}, bf16[2,112,768]{2,1,0:T(8,128)(2,1)S(1)}, u32[]{:S(2)}, u32[]{:S(2)}) %collective-permute-start.39) | collective-permute-done | bytes 344096 | tf_op jit(solution)/shard_map/ppermute | solution.py:24
  146.8 5.1 %collective-permute-done.40.refs_1_ = bf16[112,768]{1,0:T(8,128)(2,1)S(1)} collective-permute-done((bf16[112,768]{1,0:T(8,128)(2,1)S(1)}, bf16[112,768]{1,0:T(8,128)(2,1)S(1)}, u32[]{:S(2)}, u32[]{:S(2)}) %collective-permute-start.40) | collective-permute-done | bytes 172064 | tf_op jit(solution)/shard_map/ppermute | solution.py:24
  151.9 13.7 %all-gather.1 = bf16[448,768]{1,0:T(8,128)(2,1)S(1)} all-gather(bf16[112,768]{1,0:T(8,128)(2,1)S(1)} %shard_map.329.refs_0_), channel_id=3, replica_groups={{0,8,16,24},{4,12,20,28},{1,9,17,25},{5,13,21,29},{2,10,18,26},{6,14,22..., dimensions={0}, use_global_device_ids=true | all-gather | bytes 860160 | tf_op jit(solution)/shard_map/all_gather | solution.py:902
  167.1 2.6 %collective-permute-done.44.refs_1_ = bf16[4,112,768]{2,1,0:T(8,128)(2,1)S(1)} collective-permute-done((bf16[4,112,768]{2,1,0:T(8,128)(2,1)S(1)}, bf16[4,112,768]{2,1,0:T(8,128)(2,1)S(1)}, u32[]{:S(2)}, u32[]{:S(2)}) %collective-permute-start.44) | collective-permute-done | bytes 688160 | tf_op jit(solution)/shard_map/ppermute | solution.py:24
  169.7 1.8 %shard_map.332 = (f32[192,768]{1,0:T(8,128)}, f32[192,768]{1,0:T(8,128)}, f32[192,768]{1,0:T(8,128)}, f32[192,768]{1,0:T(8,128)}, f32[192]{0:T(256)}, /*index=5*...) custom-call(bf16[4,112,768]{2,1,0:T(8,128)(2,1)S(1)} %bitcast.4, ...), custom_call_target="tpu_custom_call" | custom-call | flops 1 | bytes 1 | tf_op jit(solution)/shard_map/pallas_call | solution.py:54
  171.4 2.7 %shard_map.335 = (f32[768,768]{1,0:T(8,128)}, f32[192,3072]{1,0:T(8,128)}, f32[8,128]{1,0:T(8,128)}) custom-call(bf16[4,112,768]{2,1,0:T(8,128)(2,1)S(1)} %bitcast.5, bf16[4,192,768]{2,1,0:T(8,128)(2,1)S(1)} %shard_map.334.refs_1_, bf16[4,192,768]{2,1,0:T(8,128)(2,1)S(1)} %collective-permute-done.49.refs_2_), custom_call_target="tpu_custom_call" | custom-call | flops 1 | bytes 1 | tf_op jit(solution)/shard_map/pallas_call | solution.py:54
  (103 shorter events, 43.5 us)
Async XLA Ops:
  2.3 34.5 %collective-permute-start = (bf16[384,768]{1,0:T(8,128)(2,1)S(1)}, bf16[384,768]{1,0:T(8,128)(2,1)S(1)}, u32[]{:S(2)}, u32[]{:S(2)}) collective-permute-start(bf16[384,768]{1,0:T(8,128)(2,1)S(1)} %shard_map.306.refs_1_.refs_0_), channel_id=1, source_target_pairs={{0,1},{1,0},{2,3},{3,2},{4,5},{5,4},{6,7},{7,6},{8,9},{9,8},{10,11... | collective-permute-start | bytes 1769480 | tf_op jit(solution)/shard_map/ppermute | solution.py:24
  5.4 32.0 %collective-permute-start.1 = (bf16[384,768]{1,0:T(8,128)(2,1)S(1)}, bf16[384,768]{1,0:T(8,128)(2,1)S(1)}, u32[]{:S(2)}, u32[]{:S(2)}) collective-permute-start(bf16[384,768]{1,0:T(8,128)(2,1)S(1)} %shard_map.306.refs_1_.refs_0_), channel_id=1, source_target_pairs={{0,2},{1,3},{2,0},{3,1},{4,6},{5,7},{6,4},{7,5},{8,10},{9,11},{10,... | collective-permute-start | bytes 1769480 | tf_op jit(solution)/shard_map/ppermute | solution.py:24
  20.8 16.0 %collective-permute-start.2 = (bf16[96,768]{1,0:T(8,128)(2,1)S(1)}, bf16[96,768]{1,0:T(8,128)(2,1)S(1)}, u32[]{:S(2)}, u32[]{:S(2)}) collective-permute-start(bf16[96,768]{1,0:T(8,128)(2,1)S(1)} %shard_map.307), channel_id=1, source_target_pairs={{0,3},{1,2},{2,1},{3,0},{4,7},{5,6},{6,5},{7,4},{8,11},{9,10},{10,... | collective-permute-start | bytes 442376 | tf_op jit(solution)/shard_map/ppermute | solution.py:24
  37.7 19.6 %collective-permute-start.10 = (bf16[3,288,768]{2,1,0:T(8,128)(2,1)S(1)}, bf16[3,288,768]{2,1,0:T(8,128)(2,1)S(1)}, u32[]{:S(2)}, u32[]{:S(2)}) collective-permute-start(bf16[3,288,768]{2,1,0:T(8,128)(2,1)S(1)} %get-tuple-element.114.refs_0_), channel_id=1, source_target_pairs={{0,4},{4,0},{8,12},{12,8},{16,20},{20,16},{24,28},{28,24},{1,5},{5... | collective-permute-start | bytes 3981320 | tf_op jit(solution)/shard_map/ppermute | solution.py:24
  38.2 13.6 %collective-permute-start.9 = (bf16[288,768]{1,0:T(8,128)(2,1)S(1)}, bf16[288,768]{1,0:T(8,128)(2,1)S(1)}, u32[]{:S(2)}, u32[]{:S(2)}) collective-permute-start(bf16[288,768]{1,0:T(8,128)(2,1)S(1)} %get-tuple-element.115), channel_id=1, source_target_pairs={{0,1},{1,0},{2,3},{3,2},{4,5},{5,4},{6,7},{7,6},{8,9},{9,8},{10,11... | collective-permute-start | bytes 1327112 | tf_op jit(solution)/shard_map/ppermute | solution.py:24
  52.4 7.8 %collective-permute-start.6 = (bf16[128,768]{1,0:T(8,128)(2,1)S(1)}, bf16[128,768]{1,0:T(8,128)(2,1)S(1)}, u32[]{:S(2)}, u32[]{:S(2)}) collective-permute-start(bf16[128,768]{1,0:T(8,128)(2,1)S(1)} %get-tuple-element.112.refs_0_), channel_id=1, source_target_pairs={{0,8},{4,12},{8,0},{12,4},{16,24},{20,28},{24,16},{28,20},{1,9},{5... | collective-permute-start | bytes 589832 | tf_op jit(solution)/shard_map/ppermute | solution.py:24
  53.9 10.8 %collective-permute-start.7 = (bf16[128,768]{1,0:T(8,128)(2,1)S(1)}, bf16[128,768]{1,0:T(8,128)(2,1)S(1)}, u32[]{:S(2)}, u32[]{:S(2)}) collective-permute-start(bf16[128,768]{1,0:T(8,128)(2,1)S(1)} %get-tuple-element.112.refs_0_), channel_id=1, source_target_pairs={{0,16},{4,20},{8,24},{12,28},{16,0},{20,4},{24,8},{28,12},{1,17},{... | collective-permute-start | bytes 589832 | tf_op jit(solution)/shard_map/ppermute | solution.py:24
  55.5 9.3 %collective-permute-start.8 = (bf16[128,768]{1,0:T(8,128)(2,1)S(1)}, bf16[128,768]{1,0:T(8,128)(2,1)S(1)}, u32[]{:S(2)}, u32[]{:S(2)}) collective-permute-start(bf16[128,768]{1,0:T(8,128)(2,1)S(1)} %get-tuple-element.112.refs_0_), channel_id=1, source_target_pairs={{0,24},{4,28},{8,16},{12,20},{16,8},{20,12},{24,0},{28,4},{1,25},{... | collective-permute-start | bytes 589832 | tf_op jit(solution)/shard_map/ppermute | solution.py:24
  68.0 7.7 %collective-permute-start.14 = (bf16[128,768]{1,0:T(8,128)(2,1)S(1)}, bf16[128,768]{1,0:T(8,128)(2,1)S(1)}, u32[]{:S(2)}, u32[]{:S(2)}) collective-permute-start(bf16[128,768]{1,0:T(8,128)(2,1)S(1)} %get-tuple-element.125), channel_id=1, source_target_pairs={{0,8},{4,12},{8,0},{12,4},{16,24},{20,28},{24,16},{28,20},{1,9},{5... | collective-permute-start | bytes 589832 | tf_op jit(solution)/shard_map/ppermute | solution.py:24
  69.3 10.0 %collective-permute-start.15 = (bf16[128,768]{1,0:T(8,128)(2,1)S(1)}, bf16[128,768]{1,0:T(8,128)(2,1)S(1)}, u32[]{:S(2)}, u32[]{:S(2)}) collective-permute-start(bf16[128,768]{1,0:T(8,128)(2,1)S(1)} %get-tuple-element.126), channel_id=1, source_target_pairs={{0,16},{4,20},{8,24},{12,28},{16,0},{20,4},{24,8},{28,12},{1,17},{... | collective-permute-start | bytes 589832 | tf_op jit(solution)/shard_map/ppermute | solution.py:24
  70.1 9.2 %collective-permute-start.16 = (bf16[128,768]{1,0:T(8,128)(2,1)S(1)}, bf16[128,768]{1,0:T(8,128)(2,1)S(1)}, u32[]{:S(2)}, u32[]{:S(2)}) collective-permute-start(bf16[128,768]{1,0:T(8,128)(2,1)S(1)} %get-tuple-element.127), channel_id=1, source_target_pairs={{0,24},{4,28},{8,16},{12,20},{16,8},{20,12},{24,0},{28,4},{1,25},{... | collective-permute-start | bytes 589832 | tf_op jit(solution)/shard_map/ppermute | solution.py:24
  80.9 9.0 %collective-permute-start.18 = (bf16[128,768]{1,0:T(8,128)(2,1)S(1)}, bf16[128,768]{1,0:T(8,128)(2,1)S(1)}, u32[]{:S(2)}, u32[]{:S(2)}) collective-permute-start(bf16[128,768]{1,0:T(8,128)(2,1)S(1)} %get-tuple-element.131.refs_1_.refs_0_), channel_id=1, source_target_pairs={{0,16},{4,20},{8,24},{12,28},{16,0},{20,4},{24,8},{28,12},{1,17},{... | collective-permute-start | bytes 589832 | tf_op jit(solution)/shard_map/ppermute | solution.py:24
  82.5 7.5 %collective-permute-start.19 = (bf16[128,768]{1,0:T(8,128)(2,1)S(1)}, bf16[128,768]{1,0:T(8,128)(2,1)S(1)}, u32[]{:S(2)}, u32[]{:S(2)}) collective-permute-start(bf16[128,768]{1,0:T(8,128)(2,1)S(1)} %get-tuple-element.131.refs_1_.refs_0_), channel_id=1, source_target_pairs={{0,24},{4,28},{8,16},{12,20},{16,8},{20,12},{24,0},{28,4},{1,25},{... | collective-permute-start | bytes 589832 | tf_op jit(solution)/shard_map/ppermute | solution.py:24
  92.5 7.8 %collective-permute-start.28 = (bf16[128,768]{1,0:T(8,128)(2,1)S(1)}, bf16[128,768]{1,0:T(8,128)(2,1)S(1)}, u32[]{:S(2)}, u32[]{:S(2)}) collective-permute-start(bf16[128,768]{1,0:T(8,128)(2,1)S(1)} %get-tuple-element.152), channel_id=1, source_target_pairs={{0,8},{4,12},{8,0},{12,4},{16,24},{20,28},{24,16},{28,20},{1,9},{5... | collective-permute-start | bytes 589832 | tf_op jit(solution)/shard_map/ppermute | solution.py:24
  93.7 11.2 %collective-permute-start.29 = (bf16[128,768]{1,0:T(8,128)(2,1)S(1)}, bf16[128,768]{1,0:T(8,128)(2,1)S(1)}, u32[]{:S(2)}, u32[]{:S(2)}) collective-permute-start(bf16[128,768]{1,0:T(8,128)(2,1)S(1)} %get-tuple-element.153), channel_id=1, source_target_pairs={{0,16},{4,20},{8,24},{12,28},{16,0},{20,4},{24,8},{28,12},{1,17},{... | collective-permute-start | bytes 589832 | tf_op jit(solution)/shard_map/ppermute | solution.py:24
  94.3 10.6 %collective-permute-start.30 = (bf16[128,768]{1,0:T(8,128)(2,1)S(1)}, bf16[128,768]{1,0:T(8,128)(2,1)S(1)}, u32[]{:S(2)}, u32[]{:S(2)}) collective-permute-start(bf16[128,768]{1,0:T(8,128)(2,1)S(1)} %get-tuple-element.154), channel_id=1, source_target_pairs={{0,24},{4,28},{8,16},{12,20},{16,8},{20,12},{24,0},{28,4},{1,25},{... | collective-permute-start | bytes 589832 | tf_op jit(solution)/shard_map/ppermute | solution.py:24
  96.4 13.1 %collective-permute-start.21 = (bf16[2,96,768]{2,1,0:T(8,128)(2,1)S(1)}, bf16[2,96,768]{2,1,0:T(8,128)(2,1)S(1)}, u32[]{:S(2)}, u32[]{:S(2)}) collective-permute-start(bf16[2,96,768]{2,1,0:T(8,128)(2,1)S(1)} %get-tuple-element.135), channel_id=1, source_target_pairs={{0,1},{1,0},{2,3},{3,2},{4,5},{5,4},{6,7},{7,6},{8,9},{9,8},{10,11... | collective-permute-start | bytes 884744 | tf_op jit(solution)/shard_map/ppermute | solution.py:24
  99.1 6.7 %collective-permute-start.22 = (bf16[96,768]{1,0:T(8,128)(2,1)S(1)}, bf16[96,768]{1,0:T(8,128)(2,1)S(1)}, u32[]{:S(2)}, u32[]{:S(2)}) collective-permute-start(bf16[96,768]{1,0:T(8,128)(2,1)S(1)} %get-tuple-element.140), channel_id=1, source_target_pairs={{0,4},{4,0},{8,12},{12,8},{16,20},{20,16},{24,28},{28,24},{1,5},{5... | collective-permute-start | bytes 442376 | tf_op jit(solution)/shard_map/ppermute | solution.py:24
  105.8 7.8 %collective-permute-start.31 = (bf16[128,768]{1,0:T(8,128)(2,1)S(1)}, bf16[128,768]{1,0:T(8,128)(2,1)S(1)}, u32[]{:S(2)}, u32[]{:S(2)}) collective-permute-start(bf16[128,768]{1,0:T(8,128)(2,1)S(1)} %get-tuple-element.156.refs_4_), channel_id=1, source_target_pairs={{0,8},{4,12},{8,0},{12,4},{16,24},{20,28},{24,16},{28,20},{1,9},{5... | collective-permute-start | bytes 589832 | tf_op jit(solution)/shard_map/ppermute | solution.py:24
  106.8 10.7 %collective-permute-start.32 = (bf16[128,768]{1,0:T(8,128)(2,1)S(1)}, bf16[128,768]{1,0:T(8,128)(2,1)S(1)}, u32[]{:S(2)}, u32[]{:S(2)}) collective-permute-start(bf16[128,768]{1,0:T(8,128)(2,1)S(1)} %get-tuple-element.156.refs_4_), channel_id=1, source_target_pairs={{0,16},{4,20},{8,24},{12,28},{16,0},{20,4},{24,8},{28,12},{1,17},{... | collective-permute-start | bytes 589832 | tf_op jit(solution)/shard_map/ppermute | solution.py:24
  108.0 9.6 %collective-permute-start.33 = (bf16[128,768]{1,0:T(8,128)(2,1)S(1)}, bf16[128,768]{1,0:T(8,128)(2,1)S(1)}, u32[]{:S(2)}, u32[]{:S(2)}) collective-permute-start(bf16[128,768]{1,0:T(8,128)(2,1)S(1)} %get-tuple-element.156.refs_4_), channel_id=1, source_target_pairs={{0,24},{4,28},{8,16},{12,20},{16,8},{20,12},{24,0},{28,4},{1,25},{... | collective-permute-start | bytes 589832 | tf_op jit(solution)/shard_map/ppermute | solution.py:24
  109.6 14.9 %collective-permute-start.27 = (bf16[2,96,768]{2,1,0:T(8,128)(2,1)S(1)}, bf16[2,96,768]{2,1,0:T(8,128)(2,1)S(1)}, u32[]{:S(2)}, u32[]{:S(2)}) collective-permute-start(bf16[2,96,768]{2,1,0:T(8,128)(2,1)S(1)} %get-tuple-element.148), channel_id=1, source_target_pairs={{0,1},{1,0},{2,3},{3,2},{4,5},{5,4},{6,7},{7,6},{8,9},{9,8},{10,11... | collective-permute-start | bytes 884744 | tf_op jit(solution)/shard_map/ppermute | solution.py:24
  111.4 12.1 %collective-permute-start.26 = (bf16[96,768]{1,0:T(8,128)(2,1)S(1)}, bf16[96,768]{1,0:T(8,128)(2,1)S(1)}, u32[]{:S(2)}, u32[]{:S(2)}) collective-permute-start(bf16[96,768]{1,0:T(8,128)(2,1)S(1)} %get-tuple-element.146), channel_id=1, source_target_pairs={{0,2},{1,3},{2,0},{3,1},{4,6},{5,7},{6,4},{7,5},{8,10},{9,11},{10,... | collective-permute-start | bytes 442376 | tf_op jit(solution)/shard_map/ppermute | solution.py:24
  128.6 13.6 %collective-permute-start.39 = (bf16[2,112,768]{2,1,0:T(8,128)(2,1)S(1)}, bf16[2,112,768]{2,1,0:T(8,128)(2,1)S(1)}, u32[]{:S(2)}, u32[]{:S(2)}) collective-permute-start(bf16[2,112,768]{2,1,0:T(8,128)(2,1)S(1)} %get-tuple-element.172.refs_1_), channel_id=1, source_target_pairs={{0,1},{1,0},{2,3},{3,2},{4,5},{5,4},{6,7},{7,6},{8,9},{9,8},{10,11... | collective-permute-start | bytes 1032200 | tf_op jit(solution)/shard_map/ppermute | solution.py:24
  131.2 11.2 %collective-permute-start.41 = (bf16[128,768]{1,0:T(8,128)(2,1)S(1)}, bf16[128,768]{1,0:T(8,128)(2,1)S(1)}, u32[]{:S(2)}, u32[]{:S(2)}) collective-permute-start(bf16[128,768]{1,0:T(8,128)(2,1)S(1)} %get-tuple-element.179), channel_id=1, source_target_pairs={{0,8},{4,12},{8,0},{12,4},{16,24},{20,28},{24,16},{28,20},{1,9},{5... | collective-permute-start | bytes 589832 | tf_op jit(solution)/shard_map/ppermute | solution.py:24
  132.4 10.8 %collective-permute-start.42 = (bf16[128,768]{1,0:T(8,128)(2,1)S(1)}, bf16[128,768]{1,0:T(8,128)(2,1)S(1)}, u32[]{:S(2)}, u32[]{:S(2)}) collective-permute-start(bf16[128,768]{1,0:T(8,128)(2,1)S(1)} %get-tuple-element.180), channel_id=1, source_target_pairs={{0,16},{4,20},{8,24},{12,28},{16,0},{20,4},{24,8},{28,12},{1,17},{... | collective-permute-start | bytes 589832 | tf_op jit(solution)/shard_map/ppermute | solution.py:24
  133.0 10.2 %collective-permute-start.43 = (bf16[128,768]{1,0:T(8,128)(2,1)S(1)}, bf16[128,768]{1,0:T(8,128)(2,1)S(1)}, u32[]{:S(2)}, u32[]{:S(2)}) collective-permute-start(bf16[128,768]{1,0:T(8,128)(2,1)S(1)} %get-tuple-element.181), channel_id=1, source_target_pairs={{0,24},{4,28},{8,16},{12,20},{16,8},{20,12},{24,0},{28,4},{1,25},{... | collective-permute-start | bytes 589832 | tf_op jit(solution)/shard_map/ppermute | solution.py:24
  134.8 7.7 %collective-permute-start.45 = (bf16[96,768]{1,0:T(8,128)(2,1)S(1)}, bf16[96,768]{1,0:T(8,128)(2,1)S(1)}, u32[]{:S(2)}, u32[]{:S(2)}) collective-permute-start(bf16[96,768]{1,0:T(8,128)(2,1)S(1)} %get-tuple-element.192), channel_id=1, source_target_pairs={{0,2},{1,3},{2,0},{3,1},{4,6},{5,7},{6,4},{7,5},{8,10},{9,11},{10,... | collective-permute-start | bytes 442376 | tf_op jit(solution)/shard_map/ppermute | solution.py:24
  142.2 9.7 %collective-permute-start.40 = (bf16[112,768]{1,0:T(8,128)(2,1)S(1)}, bf16[112,768]{1,0:T(8,128)(2,1)S(1)}, u32[]{:S(2)}, u32[]{:S(2)}) collective-permute-start(bf16[112,768]{1,0:T(8,128)(2,1)S(1)} %get-tuple-element.174), channel_id=1, source_target_pairs={{0,2},{1,3},{2,0},{3,1},{4,6},{5,7},{6,4},{7,5},{8,10},{9,11},{10,... | collective-permute-start | bytes 516104 | tf_op jit(solution)/shard_map/ppermute | solution.py:24
  143.2 22.4 %collective-permute-start.46 = (bf16[192,768]{1,0:T(8,128)(2,1)S(1)}, bf16[192,768]{1,0:T(8,128)(2,1)S(1)}, u32[]{:S(2)}, u32[]{:S(2)}) collective-permute-start(bf16[192,768]{1,0:T(8,128)(2,1)S(1)} %shard_map.333.refs_1_), channel_id=1, source_target_pairs={{0,8},{4,12},{8,0},{12,4},{16,24},{20,28},{24,16},{28,20},{1,9},{5... | collective-permute-start | bytes 884744 | tf_op jit(solution)/shard_map/ppermute | solution.py:24
  144.2 21.4 %collective-permute-start.47 = (bf16[192,768]{1,0:T(8,128)(2,1)S(1)}, bf16[192,768]{1,0:T(8,128)(2,1)S(1)}, u32[]{:S(2)}, u32[]{:S(2)}) collective-permute-start(bf16[192,768]{1,0:T(8,128)(2,1)S(1)} %shard_map.333.refs_1_), channel_id=1, source_target_pairs={{0,16},{4,20},{8,24},{12,28},{16,0},{20,4},{24,8},{28,12},{1,17},{... | collective-permute-start | bytes 884744 | tf_op jit(solution)/shard_map/ppermute | solution.py:24
  145.4 20.2 %collective-permute-start.48 = (bf16[192,768]{1,0:T(8,128)(2,1)S(1)}, bf16[192,768]{1,0:T(8,128)(2,1)S(1)}, u32[]{:S(2)}, u32[]{:S(2)}) collective-permute-start(bf16[192,768]{1,0:T(8,128)(2,1)S(1)} %shard_map.333.refs_1_), channel_id=1, source_target_pairs={{0,24},{4,28},{8,16},{12,20},{16,8},{20,12},{24,0},{28,4},{1,25},{... | collective-permute-start | bytes 884744 | tf_op jit(solution)/shard_map/ppermute | solution.py:24
  (19 other events, 74.1 us)

commit v4 on v3

--- a/solution.py
+++ b/solution.py
@@ -533,15 +533,22 @@
     add_last(kept, received, out.at[half:])
 
 
-def unpack_mlp(own, other, outer, inner, done, stage):
+def stack_halves(own, near, far, farthest, first, second):
+    half = first.shape[1]
+    for s, block in enumerate((own, near, far, farthest)):
+        first[s] = block[:half]
+        second[s] = block[half:]
+
+
+def unpack_mlp(outer_own, inner_own, outer_other, inner_other, outer, inner, done, stage):
     core, _, _, chip, _ = places()
-    half, width = own.shape[1] // 2, own.shape[2]
+    half, width = outer_own.shape[1:]
     part = 2 * half
     for s in range(CHIPS):
-        for m, blocks in enumerate((own, other)):
+        for m, (one, two) in enumerate(((outer_own, inner_own), (outer_other, inner_other))):
             far, c = chip ^ s, core ^ m
-            outer[rows_from((2 * far + c) * half, half)] = blocks[s, :half].astype(WIDE)
-            stage[c, far] = blocks[s, half:]
+            outer[rows_from((2 * far + c) * half, half)] = one[s].astype(WIDE)
+            stage[c, far] = two[s]
     for c in range(2):
         for p in range(CHIPS):
             for k in range(4):
@@ -885,10 +892,6 @@
     )
     input_far = exchanged(input_sent)
 
-    def shared(total, after=()):
-        (found,) = kernel(stack, [shape((CHIPS,) + total.shape)], total, *chips(total), after=after)
-        return found, joined(found)
-
     rest_far = far_sum(*rest_near)
     (mlp_total,) = kernel(
         add_beside,
@@ -900,7 +903,13 @@
     )
     rest_total = last_sum(*rest_far)
     rest_all = lax.all_gather(rest_total, "ctx", axis_index_groups=teams)
-    mlp_blocks = shared(mlp_total, after=(rest_all,))
+    mlp_blocks = kernel(
+        stack_halves,
+        [shape((CHIPS, half, width))] * 2,
+        mlp_total,
+        *chips(mlp_total),
+        after=(rest_all,),
+    )
     grad_input, done_input = kernel(
         add_tokens,
         [shape((1, tokens, width)), shape((8, 128), WIDE)],
@@ -917,6 +926,7 @@
             shape((8, 128), WIDE),
         ],
         *mlp_blocks,
+        *map(joined, mlp_blocks),
         last=(0, 1),
         scratch=[pltpu.VMEM((2, CHIPS, half, width), LOW)],
         room=12,

time: 174 us -> 172 us (0.989)
  waiting for transfers between devices: 70.9 us -> 69 us
    ppermute x50 -> x51, waiting for transfers between devices: 70.9 us -> 69 us  [partner(): return lax.ppermute(block, axis, [(i, i ^ bit) for i in devices])]
    ppermute x50 -> x51, starting transfers between devices: 46.6 us -> 46.7 us  [partner(): return lax.ppermute(block, axis, [(i, i ^ bit) for i in devices])]
  transfers between devices with their start and end apart: 50 -> 51, of which waited for: 22 -> 22; matrix products, arithmetic and copies ran while one was open for 0% -> 0% of each run, Pallas kernels for 11% -> 11%
where the time goes in v4:
time: 172 us
  waiting for transfers between devices  69 us (40%)
  starting transfers between devices  46.7 us (27%)
  Pallas kernels  30 us (17%)
  blocking collectives  25.6 us (15%)
    ppermute x51, waiting for transfers between devices, partner(): return lax.ppermute(block, axis, [(i, i ^ bit) for i in devices])  69 us
    ppermute x51, starting transfers between devices, partner(): return lax.ppermute(block, axis, [(i, i ^ bit) for i in devices])  46.7 us
    pallas_call x31, Pallas kernels, kernel(): pl.pallas_call(step, out_shape=[o if n in last else pltpu.VMEM(o.shape, o...  30 us
    all_gather x1, blocking collectives, per_device(): rest_all = lax.all_gather(rest_total, 'ctx', axis_index_groups=teams)  13.7 us
    all_gather x1, blocking collectives, per_device(): seen = lax.all_gather(own, 'ctx', axis_index_groups=teams)  11.8 us
  transfers between devices with their start and end apart: 51, of which 22 were waited for; matrix products, arithmetic and copies ran while one was open for 0% of the time, Pallas kernels for 11%

profile of v4, /device:TPU:0, one launch (start us, length us, event | category | flops | bytes accessed | tf_op | source)
XLA Modules:
  0.0 172.2 jit_solution(10837365617253936077)
XLA Ops:
  0.7 1.7 shard_map.306.refs_1_.refs_0_
  2.3 3.1 %collective-permute-start = (bf16[384,768]{1,0:T(8,128)(2,1)S(1)}, bf16[384,768]{1,0:T(8,128)(2,1)S(1)}, u32[]{:S(2)}, u32[]{:S(2)}) collective-permute-start(bf16[384,768]{1,0:T(8,128)(2,1)S(1)} %shard_map.306.refs_1_.refs_0_), channel_id=1, source_target_pairs={{0,1},{1,0},{2,3},{3,2},{4,5},{5,4},{6,7},{7,6},{8,9},{9,8},{10,11... | collective-permute-start | bytes 1769480 | tf_op jit(solution)/shard_map/ppermute | solution.py:24
  5.4 2.6 %collective-permute-start.1 = (bf16[384,768]{1,0:T(8,128)(2,1)S(1)}, bf16[384,768]{1,0:T(8,128)(2,1)S(1)}, u32[]{:S(2)}, u32[]{:S(2)}) collective-permute-start(bf16[384,768]{1,0:T(8,128)(2,1)S(1)} %shard_map.306.refs_1_.refs_0_), channel_id=1, source_target_pairs={{0,2},{1,3},{2,0},{3,1},{4,6},{5,7},{6,4},{7,5},{8,10},{9,11},{10,... | collective-permute-start | bytes 1769480 | tf_op jit(solution)/shard_map/ppermute | solution.py:24
  9.0 11.8 %all-gather = bf16[576,768]{1,0:T(8,128)(2,1)S(1)} all-gather(bf16[144,768]{1,0:T(8,128)(2,1)S(1)} %shard_map.305), channel_id=2, replica_groups={{0,8,16,24},{4,12,20,28},{1,9,17,25},{5,13,21,29},{2,10,18,26},{6,14,22..., dimensions={0}, use_global_device_ids=true | all-gather | bytes 1105920 | tf_op jit(solution)/shard_map/all_gather | solution.py:638
  21.1 15.7 %collective-permute-done.2.refs_3_ = bf16[96,768]{1,0:T(8,128)(2,1)S(1)} collective-permute-done((bf16[96,768]{1,0:T(8,128)(2,1)S(1)}, bf16[96,768]{1,0:T(8,128)(2,1)S(1)}, u32[]{:S(2)}, u32[]{:S(2)}) %collective-permute-start.2) | collective-permute-done | bytes 147488 | tf_op jit(solution)/shard_map/ppermute | solution.py:24
  38.2 3.2 %collective-permute-start.9 = (bf16[288,768]{1,0:T(8,128)(2,1)S(1)}, bf16[288,768]{1,0:T(8,128)(2,1)S(1)}, u32[]{:S(2)}, u32[]{:S(2)}) collective-permute-start(bf16[288,768]{1,0:T(8,128)(2,1)S(1)} %get-tuple-element.117), channel_id=1, source_target_pairs={{0,1},{1,0},{2,3},{3,2},{4,5},{5,4},{6,7},{7,6},{8,9},{9,8},{10,11... | collective-permute-start | bytes 1327112 | tf_op jit(solution)/shard_map/ppermute | solution.py:24
  44.2 3.9 %shard_map.310 = (bf16[128,768]{1,0:T(8,128)(2,1)S(1)}, bf16[3,1024,512]{2,1,0:T(8,128)(2,1)S(1)}) custom-call(bf16[512,192]{1,0:T(8,128)(2,1)S(1)} %get-tuple-element.111.refs_0_.refs_1_, bf16[512,384]{1,0:T(8,128)(2,1)S(1)} %get-tuple-element.112.refs_1_.refs_2_, bf16[512,384]{1,0:T(8,128)(2,1)S(1)} %collective-permute-done.4.refs_2_.refs_3_, ...), custom_call_target="tpu_custom_call" | custom-call | flops 1 | bytes 1 | tf_op jit(solution)/shard_map/pallas_call | solution.py:54
  48.1 3.7 %collective-permute-done.9.refs_1_ = bf16[288,768]{1,0:T(8,128)(2,1)S(1)} collective-permute-done((bf16[288,768]{1,0:T(8,128)(2,1)S(1)}, bf16[288,768]{1,0:T(8,128)(2,1)S(1)}, u32[]{:S(2)}, u32[]{:S(2)}) %collective-permute-start.9) | collective-permute-done | bytes 442400 | tf_op jit(solution)/shard_map/ppermute | solution.py:24
  53.9 1.5 collective-permute-start.7
  57.6 2.6 %collective-permute-done.6.refs_1_ = bf16[128,768]{1,0:T(8,128)(2,1)S(1)} collective-permute-done((bf16[128,768]{1,0:T(8,128)(2,1)S(1)}, bf16[128,768]{1,0:T(8,128)(2,1)S(1)}, u32[]{:S(2)}, u32[]{:S(2)}) %collective-permute-start.6) | collective-permute-done | bytes 196640 | tf_op jit(solution)/shard_map/ppermute | solution.py:24
  60.2 4.6 %collective-permute-done.7.refs_2_ = bf16[128,768]{1,0:T(8,128)(2,1)S(1)} collective-permute-done((bf16[128,768]{1,0:T(8,128)(2,1)S(1)}, bf16[128,768]{1,0:T(8,128)(2,1)S(1)}, u32[]{:S(2)}, u32[]{:S(2)}) %collective-permute-start.7) | collective-permute-done | bytes 196640 | tf_op jit(solution)/shard_map/ppermute | solution.py:24
  64.8 3.2 %shard_map.313 = (bf16[512,768]{1,0:T(8,128)(2,1)S(1)}, f32[128,768]{1,0:T(8,128)S(1)}, f32[128,1]{1,0:T(8,128)S(1)}, bf16[512,768]{1,0:T(8,128)(2,1)S(1)}, bf16...) custom-call(bf16[128,768]{1,0:T(8,128)(2,1)S(1)} %get-tuple-element., ...), custom_call_target="tpu_custom_call" | custom-call | flops 1 | bytes 1 | tf_op jit(solution)/shard_map/pallas_call | solution.py:54
  71.5 4.1 %collective-permute-done.14.refs_1_ = bf16[128,768]{1,0:T(8,128)(2,1)S(1)} collective-permute-done((bf16[128,768]{1,0:T(8,128)(2,1)S(1)}, bf16[128,768]{1,0:T(8,128)(2,1)S(1)}, u32[]{:S(2)}, u32[]{:S(2)}) %collective-permute-start.14) | collective-permute-done | bytes 196640 | tf_op jit(solution)/shard_map/ppermute | solution.py:24
  75.7 3.6 %collective-permute-done.15.refs_2_ = bf16[128,768]{1,0:T(8,128)(2,1)S(1)} collective-permute-done((bf16[128,768]{1,0:T(8,128)(2,1)S(1)}, bf16[128,768]{1,0:T(8,128)(2,1)S(1)}, u32[]{:S(2)}, u32[]{:S(2)}) %collective-permute-start.15) | collective-permute-done | bytes 196640 | tf_op jit(solution)/shard_map/ppermute | solution.py:24
  80.9 1.5 collective-permute-start.18
  83.8 2.9 %collective-permute-done.17.refs_2_.refs_1_ = bf16[128,768]{1,0:T(8,128)(2,1)S(1)} collective-permute-done((bf16[128,768]{1,0:T(8,128)(2,1)S(1)}, bf16[128,768]{1,0:T(8,128)(2,1)S(1)}, u32[]{:S(2)}, u32[]{:S(2)}) %collective-permute-start.17) | collective-permute-done | bytes 196640 | tf_op jit(solution)/shard_map/ppermute | solution.py:24
  86.7 3.3 %collective-permute-done.18.refs_3_.refs_2_ = bf16[128,768]{1,0:T(8,128)(2,1)S(1)} collective-permute-done((bf16[128,768]{1,0:T(8,128)(2,1)S(1)}, bf16[128,768]{1,0:T(8,128)(2,1)S(1)}, u32[]{:S(2)}, u32[]{:S(2)}) %collective-permute-start.18) | collective-permute-done | bytes 196640 | tf_op jit(solution)/shard_map/ppermute | solution.py:24
  90.9 1.6 shard_map.317
  94.3 1.8 %collective-permute-start.30 = (bf16[128,768]{1,0:T(8,128)(2,1)S(1)}, bf16[128,768]{1,0:T(8,128)(2,1)S(1)}, u32[]{:S(2)}, u32[]{:S(2)}) collective-permute-start(bf16[128,768]{1,0:T(8,128)(2,1)S(1)} %get-tuple-element.156), channel_id=1, source_target_pairs={{0,24},{4,28},{8,16},{12,20},{16,8},{20,12},{24,0},{28,4},{1,25},{... | collective-permute-start | bytes 589832 | tf_op jit(solution)/shard_map/ppermute | solution.py:24
  96.4 1.8 %collective-permute-start.21 = (bf16[2,96,768]{2,1,0:T(8,128)(2,1)S(1)}, bf16[2,96,768]{2,1,0:T(8,128)(2,1)S(1)}, u32[]{:S(2)}, u32[]{:S(2)}) collective-permute-start(bf16[2,96,768]{2,1,0:T(8,128)(2,1)S(1)} %get-tuple-element.137), channel_id=1, source_target_pairs={{0,1},{1,0},{2,3},{3,2},{4,5},{5,4},{6,7},{7,6},{8,9},{9,8},{10,11... | collective-permute-start | bytes 884744 | tf_op jit(solution)/shard_map/ppermute | solution.py:24
  100.3 4.6 %collective-permute-done.29.refs_3_ = bf16[128,768]{1,0:T(8,128)(2,1)S(1)} collective-permute-done((bf16[128,768]{1,0:T(8,128)(2,1)S(1)}, bf16[128,768]{1,0:T(8,128)(2,1)S(1)}, u32[]{:S(2)}, u32[]{:S(2)}) %collective-permute-start.29) | collective-permute-done | bytes 196640 | tf_op jit(solution)/shard_map/ppermute | solution.py:24
  109.6 1.8 %collective-permute-start.27 = (bf16[2,96,768]{2,1,0:T(8,128)(2,1)S(1)}, bf16[2,96,768]{2,1,0:T(8,128)(2,1)S(1)}, u32[]{:S(2)}, u32[]{:S(2)}) collective-permute-start(bf16[2,96,768]{2,1,0:T(8,128)(2,1)S(1)} %get-tuple-element.150), channel_id=1, source_target_pairs={{0,1},{1,0},{2,3},{3,2},{4,5},{5,4},{6,7},{7,6},{8,9},{9,8},{10,11... | collective-permute-start | bytes 884744 | tf_op jit(solution)/shard_map/ppermute | solution.py:24
  113.6 3.9 %collective-permute-done.32.refs_6_ = bf16[128,768]{1,0:T(8,128)(2,1)S(1)} collective-permute-done((bf16[128,768]{1,0:T(8,128)(2,1)S(1)}, bf16[128,768]{1,0:T(8,128)(2,1)S(1)}, u32[]{:S(2)}, u32[]{:S(2)}) %collective-permute-start.32) | collective-permute-done | bytes 196640 | tf_op jit(solution)/shard_map/ppermute | solution.py:24
  117.5 5.4 %shard_map.324 = (bf16[512,768]{1,0:T(8,128)(2,1)S(1)}, bf16[512,192]{1,0:T(8,128)(2,1)S(1)}, f32[512,384]{1,0:T(8,128)S(1)}, bf16[128,384]{1,0:T(8,128)(2,1)S(1...) custom-call(bf16[96,768]{1,0:T(8,128)(2,1)S(1)} %get-tuple-element.147.refs_0_, ...), custom_call_target="tpu_custom_call" | custom-call | flops 1 | bytes 1 | tf_op jit(solution)/shard_map/pallas_call | solution.py:54
  126.6 1.8 %collective-permute-done.38.refs_1_ = bf16[4,112,768]{2,1,0:T(8,128)(2,1)S(1)} collective-permute-done((bf16[4,112,768]{2,1,0:T(8,128)(2,1)S(1)}, bf16[4,112,768]{2,1,0:T(8,128)(2,1)S(1)}, u32[]{:S(2)}, u32[]{:S(2)}) %collective-permute-start.38) | collective-permute-done | bytes 688160 | tf_op jit(solution)/shard_map/ppermute | solution.py:24
  128.6 1.8 %collective-permute-start.39 = (bf16[2,112,768]{2,1,0:T(8,128)(2,1)S(1)}, bf16[2,112,768]{2,1,0:T(8,128)(2,1)S(1)}, u32[]{:S(2)}, u32[]{:S(2)}) collective-permute-start(bf16[2,112,768]{2,1,0:T(8,128)(2,1)S(1)} %get-tuple-element.174.refs_1_), channel_id=1, source_target_pairs={{0,1},{1,0},{2,3},{3,2},{4,5},{5,4},{6,7},{7,6},{8,9},{9,8},{10,11... | collective-permute-start | bytes 1032200 | tf_op jit(solution)/shard_map/ppermute | solution.py:24
  133.0 1.7 %collective-permute-start.43 = (bf16[128,768]{1,0:T(8,128)(2,1)S(1)}, bf16[128,768]{1,0:T(8,128)(2,1)S(1)}, u32[]{:S(2)}, u32[]{:S(2)}) collective-permute-start(bf16[128,768]{1,0:T(8,128)(2,1)S(1)} %get-tuple-element.183), channel_id=1, source_target_pairs={{0,24},{4,28},{8,16},{12,20},{16,8},{20,12},{24,0},{28,4},{1,25},{... | collective-permute-start | bytes 589832 | tf_op jit(solution)/shard_map/ppermute | solution.py:24
  136.1 6.1 %collective-permute-done.39.refs_1_ = bf16[2,112,768]{2,1,0:T(8,128)(2,1)S(1)} collective-permute-done((bf16[2,112,768]{2,1,0:T(8,128)(2,1)S(1)}, bf16[2,112,768]{2,1,0:T(8,128)(2,1)S(1)}, u32[]{:S(2)}, u32[]{:S(2)}) %collective-permute-start.39) | collective-permute-done | bytes 344096 | tf_op jit(solution)/shard_map/ppermute | solution.py:24
  146.8 5.1 %collective-permute-done.40.refs_1_ = bf16[112,768]{1,0:T(8,128)(2,1)S(1)} collective-permute-done((bf16[112,768]{1,0:T(8,128)(2,1)S(1)}, bf16[112,768]{1,0:T(8,128)(2,1)S(1)}, u32[]{:S(2)}, u32[]{:S(2)}) %collective-permute-start.40) | collective-permute-done | bytes 172064 | tf_op jit(solution)/shard_map/ppermute | solution.py:24
  151.9 13.7 %all-gather.1 = bf16[448,768]{1,0:T(8,128)(2,1)S(1)} all-gather(bf16[112,768]{1,0:T(8,128)(2,1)S(1)} %shard_map.329.refs_0_), channel_id=3, replica_groups={{0,8,16,24},{4,12,20,28},{1,9,17,25},{5,13,21,29},{2,10,18,26},{6,14,22..., dimensions={0}, use_global_device_ids=true | all-gather | bytes 860160 | tf_op jit(solution)/shard_map/all_gather | solution.py:905
  167.8 1.8 %shard_map.332 = (f32[192,768]{1,0:T(8,128)}, f32[192,768]{1,0:T(8,128)}, f32[192,768]{1,0:T(8,128)}, f32[192,768]{1,0:T(8,128)}, f32[192]{0:T(256)}, /*index=5*...) custom-call(bf16[4,112,768]{2,1,0:T(8,128)(2,1)S(1)} %bitcast.4, ...), custom_call_target="tpu_custom_call" | custom-call | flops 1 | bytes 1 | tf_op jit(solution)/shard_map/pallas_call | solution.py:54
  169.6 2.7 %shard_map.335 = (f32[768,768]{1,0:T(8,128)}, f32[192,3072]{1,0:T(8,128)}, f32[8,128]{1,0:T(8,128)}) custom-call(bf16[4,112,768]{2,1,0:T(8,128)(2,1)S(1)} %bitcast.5, bf16[4,96,768]{2,1,0:T(8,128)(2,1)S(1)} %get-tuple-element.195.refs_1_, bf16[4,96,768]{2,1,0:T(8,128)(2,1)S(1)} %get-tuple-element.196.refs_2_, ...), custom_call_target="tpu_custom_call" | custom-call | flops 1 | bytes 1 | tf_op jit(solution)/shard_map/pallas_call | solution.py:54
  (105 shorter events, 42.6 us)
Async XLA Ops:
  2.3 34.5 %collective-permute-start = (bf16[384,768]{1,0:T(8,128)(2,1)S(1)}, bf16[384,768]{1,0:T(8,128)(2,1)S(1)}, u32[]{:S(2)}, u32[]{:S(2)}) collective-permute-start(bf16[384,768]{1,0:T(8,128)(2,1)S(1)} %shard_map.306.refs_1_.refs_0_), channel_id=1, source_target_pairs={{0,1},{1,0},{2,3},{3,2},{4,5},{5,4},{6,7},{7,6},{8,9},{9,8},{10,11... | collective-permute-start | bytes 1769480 | tf_op jit(solution)/shard_map/ppermute | solution.py:24
  5.4 32.0 %collective-permute-start.1 = (bf16[384,768]{1,0:T(8,128)(2,1)S(1)}, bf16[384,768]{1,0:T(8,128)(2,1)S(1)}, u32[]{:S(2)}, u32[]{:S(2)}) collective-permute-start(bf16[384,768]{1,0:T(8,128)(2,1)S(1)} %shard_map.306.refs_1_.refs_0_), channel_id=1, source_target_pairs={{0,2},{1,3},{2,0},{3,1},{4,6},{5,7},{6,4},{7,5},{8,10},{9,11},{10,... | collective-permute-start | bytes 1769480 | tf_op jit(solution)/shard_map/ppermute | solution.py:24
  20.8 16.0 %collective-permute-start.2 = (bf16[96,768]{1,0:T(8,128)(2,1)S(1)}, bf16[96,768]{1,0:T(8,128)(2,1)S(1)}, u32[]{:S(2)}, u32[]{:S(2)}) collective-permute-start(bf16[96,768]{1,0:T(8,128)(2,1)S(1)} %shard_map.307), channel_id=1, source_target_pairs={{0,3},{1,2},{2,1},{3,0},{4,7},{5,6},{6,5},{7,4},{8,11},{9,10},{10,... | collective-permute-start | bytes 442376 | tf_op jit(solution)/shard_map/ppermute | solution.py:24
  37.7 19.6 %collective-permute-start.10 = (bf16[3,288,768]{2,1,0:T(8,128)(2,1)S(1)}, bf16[3,288,768]{2,1,0:T(8,128)(2,1)S(1)}, u32[]{:S(2)}, u32[]{:S(2)}) collective-permute-start(bf16[3,288,768]{2,1,0:T(8,128)(2,1)S(1)} %get-tuple-element.116.refs_0_), channel_id=1, source_target_pairs={{0,4},{4,0},{8,12},{12,8},{16,20},{20,16},{24,28},{28,24},{1,5},{5... | collective-permute-start | bytes 3981320 | tf_op jit(solution)/shard_map/ppermute | solution.py:24
  38.2 13.6 %collective-permute-start.9 = (bf16[288,768]{1,0:T(8,128)(2,1)S(1)}, bf16[288,768]{1,0:T(8,128)(2,1)S(1)}, u32[]{:S(2)}, u32[]{:S(2)}) collective-permute-start(bf16[288,768]{1,0:T(8,128)(2,1)S(1)} %get-tuple-element.117), channel_id=1, source_target_pairs={{0,1},{1,0},{2,3},{3,2},{4,5},{5,4},{6,7},{7,6},{8,9},{9,8},{10,11... | collective-permute-start | bytes 1327112 | tf_op jit(solution)/shard_map/ppermute | solution.py:24
  52.4 7.8 %collective-permute-start.6 = (bf16[128,768]{1,0:T(8,128)(2,1)S(1)}, bf16[128,768]{1,0:T(8,128)(2,1)S(1)}, u32[]{:S(2)}, u32[]{:S(2)}) collective-permute-start(bf16[128,768]{1,0:T(8,128)(2,1)S(1)} %get-tuple-element.114.refs_0_), channel_id=1, source_target_pairs={{0,8},{4,12},{8,0},{12,4},{16,24},{20,28},{24,16},{28,20},{1,9},{5... | collective-permute-start | bytes 589832 | tf_op jit(solution)/shard_map/ppermute | solution.py:24
  53.9 10.8 %collective-permute-start.7 = (bf16[128,768]{1,0:T(8,128)(2,1)S(1)}, bf16[128,768]{1,0:T(8,128)(2,1)S(1)}, u32[]{:S(2)}, u32[]{:S(2)}) collective-permute-start(bf16[128,768]{1,0:T(8,128)(2,1)S(1)} %get-tuple-element.114.refs_0_), channel_id=1, source_target_pairs={{0,16},{4,20},{8,24},{12,28},{16,0},{20,4},{24,8},{28,12},{1,17},{... | collective-permute-start | bytes 589832 | tf_op jit(solution)/shard_map/ppermute | solution.py:24
  55.5 9.3 %collective-permute-start.8 = (bf16[128,768]{1,0:T(8,128)(2,1)S(1)}, bf16[128,768]{1,0:T(8,128)(2,1)S(1)}, u32[]{:S(2)}, u32[]{:S(2)}) collective-permute-start(bf16[128,768]{1,0:T(8,128)(2,1)S(1)} %get-tuple-element.114.refs_0_), channel_id=1, source_target_pairs={{0,24},{4,28},{8,16},{12,20},{16,8},{20,12},{24,0},{28,4},{1,25},{... | collective-permute-start | bytes 589832 | tf_op jit(solution)/shard_map/ppermute | solution.py:24
  68.0 7.7 %collective-permute-start.14 = (bf16[128,768]{1,0:T(8,128)(2,1)S(1)}, bf16[128,768]{1,0:T(8,128)(2,1)S(1)}, u32[]{:S(2)}, u32[]{:S(2)}) collective-permute-start(bf16[128,768]{1,0:T(8,128)(2,1)S(1)} %get-tuple-element.127), channel_id=1, source_target_pairs={{0,8},{4,12},{8,0},{12,4},{16,24},{20,28},{24,16},{28,20},{1,9},{5... | collective-permute-start | bytes 589832 | tf_op jit(solution)/shard_map/ppermute | solution.py:24
  69.3 10.0 %collective-permute-start.15 = (bf16[128,768]{1,0:T(8,128)(2,1)S(1)}, bf16[128,768]{1,0:T(8,128)(2,1)S(1)}, u32[]{:S(2)}, u32[]{:S(2)}) collective-permute-start(bf16[128,768]{1,0:T(8,128)(2,1)S(1)} %get-tuple-element.128), channel_id=1, source_target_pairs={{0,16},{4,20},{8,24},{12,28},{16,0},{20,4},{24,8},{28,12},{1,17},{... | collective-permute-start | bytes 589832 | tf_op jit(solution)/shard_map/ppermute | solution.py:24
  70.1 9.2 %collective-permute-start.16 = (bf16[128,768]{1,0:T(8,128)(2,1)S(1)}, bf16[128,768]{1,0:T(8,128)(2,1)S(1)}, u32[]{:S(2)}, u32[]{:S(2)}) collective-permute-start(bf16[128,768]{1,0:T(8,128)(2,1)S(1)} %get-tuple-element.129), channel_id=1, source_target_pairs={{0,24},{4,28},{8,16},{12,20},{16,8},{20,12},{24,0},{28,4},{1,25},{... | collective-permute-start | bytes 589832 | tf_op jit(solution)/shard_map/ppermute | solution.py:24
  80.9 9.0 %collective-permute-start.18 = (bf16[128,768]{1,0:T(8,128)(2,1)S(1)}, bf16[128,768]{1,0:T(8,128)(2,1)S(1)}, u32[]{:S(2)}, u32[]{:S(2)}) collective-permute-start(bf16[128,768]{1,0:T(8,128)(2,1)S(1)} %get-tuple-element.133.refs_1_.refs_0_), channel_id=1, source_target_pairs={{0,16},{4,20},{8,24},{12,28},{16,0},{20,4},{24,8},{28,12},{1,17},{... | collective-permute-start | bytes 589832 | tf_op jit(solution)/shard_map/ppermute | solution.py:24
  82.5 7.5 %collective-permute-start.19 = (bf16[128,768]{1,0:T(8,128)(2,1)S(1)}, bf16[128,768]{1,0:T(8,128)(2,1)S(1)}, u32[]{:S(2)}, u32[]{:S(2)}) collective-permute-start(bf16[128,768]{1,0:T(8,128)(2,1)S(1)} %get-tuple-element.133.refs_1_.refs_0_), channel_id=1, source_target_pairs={{0,24},{4,28},{8,16},{12,20},{16,8},{20,12},{24,0},{28,4},{1,25},{... | collective-permute-start | bytes 589832 | tf_op jit(solution)/shard_map/ppermute | solution.py:24
  92.5 7.8 %collective-permute-start.28 = (bf16[128,768]{1,0:T(8,128)(2,1)S(1)}, bf16[128,768]{1,0:T(8,128)(2,1)S(1)}, u32[]{:S(2)}, u32[]{:S(2)}) collective-permute-start(bf16[128,768]{1,0:T(8,128)(2,1)S(1)} %get-tuple-element.154), channel_id=1, source_target_pairs={{0,8},{4,12},{8,0},{12,4},{16,24},{20,28},{24,16},{28,20},{1,9},{5... | collective-permute-start | bytes 589832 | tf_op jit(solution)/shard_map/ppermute | solution.py:24
  93.7 11.2 %collective-permute-start.29 = (bf16[128,768]{1,0:T(8,128)(2,1)S(1)}, bf16[128,768]{1,0:T(8,128)(2,1)S(1)}, u32[]{:S(2)}, u32[]{:S(2)}) collective-permute-start(bf16[128,768]{1,0:T(8,128)(2,1)S(1)} %get-tuple-element.155), channel_id=1, source_target_pairs={{0,16},{4,20},{8,24},{12,28},{16,0},{20,4},{24,8},{28,12},{1,17},{... | collective-permute-start | bytes 589832 | tf_op jit(solution)/shard_map/ppermute | solution.py:24
  94.3 10.6 %collective-permute-start.30 = (bf16[128,768]{1,0:T(8,128)(2,1)S(1)}, bf16[128,768]{1,0:T(8,128)(2,1)S(1)}, u32[]{:S(2)}, u32[]{:S(2)}) collective-permute-start(bf16[128,768]{1,0:T(8,128)(2,1)S(1)} %get-tuple-element.156), channel_id=1, source_target_pairs={{0,24},{4,28},{8,16},{12,20},{16,8},{20,12},{24,0},{28,4},{1,25},{... | collective-permute-start | bytes 589832 | tf_op jit(solution)/shard_map/ppermute | solution.py:24
  96.4 13.1 %collective-permute-start.21 = (bf16[2,96,768]{2,1,0:T(8,128)(2,1)S(1)}, bf16[2,96,768]{2,1,0:T(8,128)(2,1)S(1)}, u32[]{:S(2)}, u32[]{:S(2)}) collective-permute-start(bf16[2,96,768]{2,1,0:T(8,128)(2,1)S(1)} %get-tuple-element.137), channel_id=1, source_target_pairs={{0,1},{1,0},{2,3},{3,2},{4,5},{5,4},{6,7},{7,6},{8,9},{9,8},{10,11... | collective-permute-start | bytes 884744 | tf_op jit(solution)/shard_map/ppermute | solution.py:24
  99.1 6.7 %collective-permute-start.22 = (bf16[96,768]{1,0:T(8,128)(2,1)S(1)}, bf16[96,768]{1,0:T(8,128)(2,1)S(1)}, u32[]{:S(2)}, u32[]{:S(2)}) collective-permute-start(bf16[96,768]{1,0:T(8,128)(2,1)S(1)} %get-tuple-element.142), channel_id=1, source_target_pairs={{0,4},{4,0},{8,12},{12,8},{16,20},{20,16},{24,28},{28,24},{1,5},{5... | collective-permute-start | bytes 442376 | tf_op jit(solution)/shard_map/ppermute | solution.py:24
  105.8 7.8 %collective-permute-start.31 = (bf16[128,768]{1,0:T(8,128)(2,1)S(1)}, bf16[128,768]{1,0:T(8,128)(2,1)S(1)}, u32[]{:S(2)}, u32[]{:S(2)}) collective-permute-start(bf16[128,768]{1,0:T(8,128)(2,1)S(1)} %get-tuple-element.158.refs_4_), channel_id=1, source_target_pairs={{0,8},{4,12},{8,0},{12,4},{16,24},{20,28},{24,16},{28,20},{1,9},{5... | collective-permute-start | bytes 589832 | tf_op jit(solution)/shard_map/ppermute | solution.py:24
  106.8 10.7 %collective-permute-start.32 = (bf16[128,768]{1,0:T(8,128)(2,1)S(1)}, bf16[128,768]{1,0:T(8,128)(2,1)S(1)}, u32[]{:S(2)}, u32[]{:S(2)}) collective-permute-start(bf16[128,768]{1,0:T(8,128)(2,1)S(1)} %get-tuple-element.158.refs_4_), channel_id=1, source_target_pairs={{0,16},{4,20},{8,24},{12,28},{16,0},{20,4},{24,8},{28,12},{1,17},{... | collective-permute-start | bytes 589832 | tf_op jit(solution)/shard_map/ppermute | solution.py:24
  108.0 9.6 %collective-permute-start.33 = (bf16[128,768]{1,0:T(8,128)(2,1)S(1)}, bf16[128,768]{1,0:T(8,128)(2,1)S(1)}, u32[]{:S(2)}, u32[]{:S(2)}) collective-permute-start(bf16[128,768]{1,0:T(8,128)(2,1)S(1)} %get-tuple-element.158.refs_4_), channel_id=1, source_target_pairs={{0,24},{4,28},{8,16},{12,20},{16,8},{20,12},{24,0},{28,4},{1,25},{... | collective-permute-start | bytes 589832 | tf_op jit(solution)/shard_map/ppermute | solution.py:24
  109.6 14.9 %collective-permute-start.27 = (bf16[2,96,768]{2,1,0:T(8,128)(2,1)S(1)}, bf16[2,96,768]{2,1,0:T(8,128)(2,1)S(1)}, u32[]{:S(2)}, u32[]{:S(2)}) collective-permute-start(bf16[2,96,768]{2,1,0:T(8,128)(2,1)S(1)} %get-tuple-element.150), channel_id=1, source_target_pairs={{0,1},{1,0},{2,3},{3,2},{4,5},{5,4},{6,7},{7,6},{8,9},{9,8},{10,11... | collective-permute-start | bytes 884744 | tf_op jit(solution)/shard_map/ppermute | solution.py:24
  111.4 12.2 %collective-permute-start.26 = (bf16[96,768]{1,0:T(8,128)(2,1)S(1)}, bf16[96,768]{1,0:T(8,128)(2,1)S(1)}, u32[]{:S(2)}, u32[]{:S(2)}) collective-permute-start(bf16[96,768]{1,0:T(8,128)(2,1)S(1)} %get-tuple-element.148), channel_id=1, source_target_pairs={{0,2},{1,3},{2,0},{3,1},{4,6},{5,7},{6,4},{7,5},{8,10},{9,11},{10,... | collective-permute-start | bytes 442376 | tf_op jit(solution)/shard_map/ppermute | solution.py:24
  128.6 13.6 %collective-permute-start.39 = (bf16[2,112,768]{2,1,0:T(8,128)(2,1)S(1)}, bf16[2,112,768]{2,1,0:T(8,128)(2,1)S(1)}, u32[]{:S(2)}, u32[]{:S(2)}) collective-permute-start(bf16[2,112,768]{2,1,0:T(8,128)(2,1)S(1)} %get-tuple-element.174.refs_1_), channel_id=1, source_target_pairs={{0,1},{1,0},{2,3},{3,2},{4,5},{5,4},{6,7},{7,6},{8,9},{9,8},{10,11... | collective-permute-start | bytes 1032200 | tf_op jit(solution)/shard_map/ppermute | solution.py:24
  131.2 11.2 %collective-permute-start.41 = (bf16[128,768]{1,0:T(8,128)(2,1)S(1)}, bf16[128,768]{1,0:T(8,128)(2,1)S(1)}, u32[]{:S(2)}, u32[]{:S(2)}) collective-permute-start(bf16[128,768]{1,0:T(8,128)(2,1)S(1)} %get-tuple-element.181), channel_id=1, source_target_pairs={{0,8},{4,12},{8,0},{12,4},{16,24},{20,28},{24,16},{28,20},{1,9},{5... | collective-permute-start | bytes 589832 | tf_op jit(solution)/shard_map/ppermute | solution.py:24
  132.4 10.8 %collective-permute-start.42 = (bf16[128,768]{1,0:T(8,128)(2,1)S(1)}, bf16[128,768]{1,0:T(8,128)(2,1)S(1)}, u32[]{:S(2)}, u32[]{:S(2)}) collective-permute-start(bf16[128,768]{1,0:T(8,128)(2,1)S(1)} %get-tuple-element.182), channel_id=1, source_target_pairs={{0,16},{4,20},{8,24},{12,28},{16,0},{20,4},{24,8},{28,12},{1,17},{... | collective-permute-start | bytes 589832 | tf_op jit(solution)/shard_map/ppermute | solution.py:24
  133.0 10.2 %collective-permute-start.43 = (bf16[128,768]{1,0:T(8,128)(2,1)S(1)}, bf16[128,768]{1,0:T(8,128)(2,1)S(1)}, u32[]{:S(2)}, u32[]{:S(2)}) collective-permute-start(bf16[128,768]{1,0:T(8,128)(2,1)S(1)} %get-tuple-element.183), channel_id=1, source_target_pairs={{0,24},{4,28},{8,16},{12,20},{16,8},{20,12},{24,0},{28,4},{1,25},{... | collective-permute-start | bytes 589832 | tf_op jit(solution)/shard_map/ppermute | solution.py:24
  134.8 7.7 %collective-permute-start.45 = (bf16[96,768]{1,0:T(8,128)(2,1)S(1)}, bf16[96,768]{1,0:T(8,128)(2,1)S(1)}, u32[]{:S(2)}, u32[]{:S(2)}) collective-permute-start(bf16[96,768]{1,0:T(8,128)(2,1)S(1)} %get-tuple-element.194), channel_id=1, source_target_pairs={{0,2},{1,3},{2,0},{3,1},{4,6},{5,7},{6,4},{7,5},{8,10},{9,11},{10,... | collective-permute-start | bytes 442376 | tf_op jit(solution)/shard_map/ppermute | solution.py:24
  142.2 9.7 %collective-permute-start.40 = (bf16[112,768]{1,0:T(8,128)(2,1)S(1)}, bf16[112,768]{1,0:T(8,128)(2,1)S(1)}, u32[]{:S(2)}, u32[]{:S(2)}) collective-permute-start(bf16[112,768]{1,0:T(8,128)(2,1)S(1)} %get-tuple-element.176), channel_id=1, source_target_pairs={{0,2},{1,3},{2,0},{3,1},{4,6},{5,7},{6,4},{7,5},{8,10},{9,11},{10,... | collective-permute-start | bytes 516104 | tf_op jit(solution)/shard_map/ppermute | solution.py:24
  143.2 22.4 %collective-permute-start.46 = (bf16[192,768]{1,0:T(8,128)(2,1)S(1)}, bf16[192,768]{1,0:T(8,128)(2,1)S(1)}, u32[]{:S(2)}, u32[]{:S(2)}) collective-permute-start(bf16[192,768]{1,0:T(8,128)(2,1)S(1)} %shard_map.333.refs_1_), channel_id=1, source_target_pairs={{0,8},{4,12},{8,0},{12,4},{16,24},{20,28},{24,16},{28,20},{1,9},{5... | collective-permute-start | bytes 884744 | tf_op jit(solution)/shard_map/ppermute | solution.py:24
  144.2 21.4 %collective-permute-start.47 = (bf16[192,768]{1,0:T(8,128)(2,1)S(1)}, bf16[192,768]{1,0:T(8,128)(2,1)S(1)}, u32[]{:S(2)}, u32[]{:S(2)}) collective-permute-start(bf16[192,768]{1,0:T(8,128)(2,1)S(1)} %shard_map.333.refs_1_), channel_id=1, source_target_pairs={{0,16},{4,20},{8,24},{12,28},{16,0},{20,4},{24,8},{28,12},{1,17},{... | collective-permute-start | bytes 884744 | tf_op jit(solution)/shard_map/ppermute | solution.py:24
  145.4 20.2 %collective-permute-start.48 = (bf16[192,768]{1,0:T(8,128)(2,1)S(1)}, bf16[192,768]{1,0:T(8,128)(2,1)S(1)}, u32[]{:S(2)}, u32[]{:S(2)}) collective-permute-start(bf16[192,768]{1,0:T(8,128)(2,1)S(1)} %shard_map.333.refs_1_), channel_id=1, source_target_pairs={{0,24},{4,28},{8,16},{12,20},{16,8},{20,12},{24,0},{28,4},{1,25},{... | collective-permute-start | bytes 884744 | tf_op jit(solution)/shard_map/ppermute | solution.py:24
  (20 other events, 73.8 us)

commit v5 on v4

--- a/solution.py
+++ b/solution.py
@@ -124,11 +124,13 @@
     core, _, _, chip, _ = places()
     part, width = wq.shape
     half = part // 2
+    most = 3 * half // 4
+    head = most + 8
     rows = rows_from(core * half, half)
     pairs = [(w.at[rows], blocks.at[j]) for j, w in enumerate((wq, wk, wv))]
-    pairs += [(wi.at[rows], block), (wo.at[rows], first.at[pl.ds(half, half)])]
+    pairs += [(wi.at[rows], block), (wo.at[rows], first.at[pl.ds(head, half)])]
     rows = rows_from((2 * chip + core) * half, half)
-    pairs += [(wu.at[rows], first.at[pl.ds(3 * half, half)])]
+    pairs += [(wu.at[rows], first.at[pl.ds(head + 2 * half, half)])]
     for copy in load(sems, *pairs, *zip(vectors, lines)):
         copy.wait()
     six, bias_inner, biases = lines_of(*lines[:6]), lines_of(lines[6]), lines_of(*lines[7:])
@@ -137,15 +139,18 @@
         @pl.when(chip == p)
         def _():
             span = slice(p * part, (p + 1) * part)
-            for j in range(3):
-                first[:half, j * part : (j + 1) * part] = blocks[j, :, span]
+            three = [blocks[j, :, span].astype(WIDE) for j in range(3)]
             for k in range(4):
                 start = k * width + p * part
-                first[2 * half : 3 * half, k * part : (k + 1) * part] = block[
+                first[head + half : head + 2 * half, k * part : (k + 1) * part] = block[
                     :, start : start + part
                 ]
-            small = [six[:6], bias_inner[:1, span], biases[:2], jnp.zeros((half - 9, part), WIDE)]
-            first[:half, 3 * part :] = jnp.concatenate(small).astype(LOW)
+            small = jnp.concatenate([six[:6], bias_inner[:1, span], biases[:1]])
+            after = jnp.concatenate([biases[1:2], jnp.zeros((7, part), WIDE)])
+            small = jnp.concatenate([small, after, jnp.zeros((8, 2 * part), WIDE)], 1)
+            beside = jnp.concatenate([block[most:] for block in three])
+            rows_q = jnp.concatenate([block[:most] for block in three] + [beside], 1)
+            first[:head] = jnp.concatenate([rows_q, small]).astype(LOW)
 
 
 def first_rows(block, out):
@@ -192,6 +197,7 @@
     rows_in, w_qkv, queries, keys_values, segs, vec, b_inner, stage = outs
     core, _, _, chip, place = places()
     width = seen.shape[2]
+    n = width // 32
     tokens = rows_in.shape[0] // CHIPS
     part, half = width // 4, width // 8
     for s in range(CHIPS):
@@ -202,8 +208,13 @@
     for r in range(4):
         for c, piece in enumerate(pieces):
             base = rows_from((2 * (place ^ r) + (core ^ c)) * half, half)
-            w_qkv[base] = piece[r, :, : 3 * part]
-        stage[place ^ r] = pieces[0][r, :16, 3 * part :].astype(WIDE)
+            rows = piece[r].astype(WIDE)
+            beside = [rows[j * n : (j + 1) * n, 3 * part :] for j in range(3)]
+            whole_rows = jnp.concatenate([rows[: 3 * n, : 3 * part], jnp.concatenate(beside, 1)])
+            w_qkv[base] = whole_rows.astype(LOW)
+            if not c:
+                small = [rows[3 * n :, :part], rows[3 * n :, part : 2 * part]]
+                stage[place ^ r] = jnp.concatenate(small)
     for k in range(4):
         span = slice(k * part, (k + 1) * part)
         vec[:6, span] = stage[k, :6]
@@ -616,6 +627,7 @@
     hidden = outer_weight.shape[0]
     count, half = CHIPS * tokens, part // 2
     heads = part // HEAD_DIM
+    head = 3 * half // 4 + 8
 
     def chips(block):
         return [partner(block, "ctx", s << 1) for s in (1, 2, 3)]
@@ -638,7 +650,7 @@
     seen = lax.all_gather(own, "ctx", axis_index_groups=teams)
     (first,) = kernel(
         prepare_weights,
-        [shape((4 * half, width))],
+        [shape((head + 3 * half, width))],
         query_weight,
         key_weight,
         value_weight,
@@ -663,11 +675,11 @@
         ],
         loads=15,
     )
-    (mine,) = kernel(first_rows, [shape((half, width))], first, after=(seen,))
+    (mine,) = kernel(first_rows, [shape((head, width))], first, after=(seen,))
     line = [first, partner(first, "fsdp", 1), partner(first, "fsdp", 2), partner(mine, "fsdp", 3)]
     projections, others, sent = kernel(
         sort_pieces,
-        [shape((4, half, width)), shape((3, 3 * half, width)), shape((3 * half, width))],
+        [shape((4, head, width)), shape((3, 3 * half, width)), shape((3 * half, width))],
         *line,
     )
     last = partner(sent, "fsdp", 1)

time: 172 us -> 170 us (0.988)
  waiting for transfers between devices: 69 us -> 67.1 us
    ppermute x51, waiting for transfers between devices: 69 us -> 67.1 us  [partner(): return lax.ppermute(block, axis, [(i, i ^ bit) for i in devices])]
  transfers between devices with their start and end apart: 51 -> 51, of which waited for: 22 -> 23; matrix products, arithmetic and copies ran while one was open for 0% -> 0% of each run, Pallas kernels for 11% -> 11%
where the time goes in v5:
time: 170 us
  waiting for transfers between devices  67.1 us (39%)
  starting transfers between devices  46.4 us (27%)
  Pallas kernels  30 us (18%)
  blocking collectives  25.5 us (15%)
    ppermute x51, waiting for transfers between devices, partner(): return lax.ppermute(block, axis, [(i, i ^ bit) for i in devices])  67.1 us
    ppermute x51, starting transfers between devices, partner(): return lax.ppermute(block, axis, [(i, i ^ bit) for i in devices])  46.4 us
    pallas_call x31, Pallas kernels, kernel(): pl.pallas_call(step, out_shape=[o if n in last else pltpu.VMEM(o.shape, o...  30 us
    all_gather x1, blocking collectives, per_device(): rest_all = lax.all_gather(rest_total, 'ctx', axis_index_groups=teams)  13.7 us
    all_gather x1, blocking collectives, per_device(): seen = lax.all_gather(own, 'ctx', axis_index_groups=teams)  11.8 us
  transfers between devices with their start and end apart: 51, of which 23 were waited for; matrix products, arithmetic and copies ran while one was open for 0% of the time, Pallas kernels for 11%

profile of v5, /device:TPU:0, one launch (start us, length us, event | category | flops | bytes accessed | tf_op | source)
XLA Modules:
  0.0 170.1 jit_solution(4566008948293766901)
XLA Ops:
  0.7 1.7 shard_map.306.refs_1_.refs_0_
  2.3 3.1 %collective-permute-start = (bf16[368,768]{1,0:T(8,128)(2,1)S(1)}, bf16[368,768]{1,0:T(8,128)(2,1)S(1)}, u32[]{:S(2)}, u32[]{:S(2)}) collective-permute-start(bf16[368,768]{1,0:T(8,128)(2,1)S(1)} %shard_map.306.refs_1_.refs_0_), channel_id=1, source_target_pairs={{0,1},{1,0},{2,3},{3,2},{4,5},{5,4},{6,7},{7,6},{8,9},{9,8},{10,11... | collective-permute-start | bytes 1695752 | tf_op jit(solution)/shard_map/ppermute | solution.py:24
  5.4 2.6 %collective-permute-start.1 = (bf16[368,768]{1,0:T(8,128)(2,1)S(1)}, bf16[368,768]{1,0:T(8,128)(2,1)S(1)}, u32[]{:S(2)}, u32[]{:S(2)}) collective-permute-start(bf16[368,768]{1,0:T(8,128)(2,1)S(1)} %shard_map.306.refs_1_.refs_0_), channel_id=1, source_target_pairs={{0,2},{1,3},{2,0},{3,1},{4,6},{5,7},{6,4},{7,5},{8,10},{9,11},{10,... | collective-permute-start | bytes 1695752 | tf_op jit(solution)/shard_map/ppermute | solution.py:24
  9.0 11.8 %all-gather = bf16[576,768]{1,0:T(8,128)(2,1)S(1)} all-gather(bf16[144,768]{1,0:T(8,128)(2,1)S(1)} %shard_map.305), channel_id=2, replica_groups={{0,8,16,24},{4,12,20,28},{1,9,17,25},{5,13,21,29},{2,10,18,26},{6,14,22..., dimensions={0}, use_global_device_ids=true | all-gather | bytes 1105920 | tf_op jit(solution)/shard_map/all_gather | solution.py:650
  21.1 14.2 %collective-permute-done.2.refs_3_ = bf16[80,768]{1,0:T(8,128)(2,1)S(1)} collective-permute-done((bf16[80,768]{1,0:T(8,128)(2,1)S(1)}, bf16[80,768]{1,0:T(8,128)(2,1)S(1)}, u32[]{:S(2)}, u32[]{:S(2)}) %collective-permute-start.2) | collective-permute-done | bytes 122912 | tf_op jit(solution)/shard_map/ppermute | solution.py:24
  36.4 2.9 %collective-permute-start.9 = (bf16[288,768]{1,0:T(8,128)(2,1)S(1)}, bf16[288,768]{1,0:T(8,128)(2,1)S(1)}, u32[]{:S(2)}, u32[]{:S(2)}) collective-permute-start(bf16[288,768]{1,0:T(8,128)(2,1)S(1)} %get-tuple-element.117), channel_id=1, source_target_pairs={{0,1},{1,0},{2,3},{3,2},{4,5},{5,4},{6,7},{7,6},{8,9},{9,8},{10,11... | collective-permute-start | bytes 1327112 | tf_op jit(solution)/shard_map/ppermute | solution.py:24
  42.5 3.9 %shard_map.310 = (bf16[128,768]{1,0:T(8,128)(2,1)S(1)}, bf16[3,1024,512]{2,1,0:T(8,128)(2,1)S(1)}) custom-call(bf16[512,192]{1,0:T(8,128)(2,1)S(1)} %get-tuple-element.111.refs_0_.refs_1_, bf16[512,384]{1,0:T(8,128)(2,1)S(1)} %get-tuple-element.112.refs_1_.refs_2_, bf16[512,384]{1,0:T(8,128)(2,1)S(1)} %collective-permute-done.4.refs_2_.refs_3_, ...), custom_call_target="tpu_custom_call" | custom-call | flops 1 | bytes 1 | tf_op jit(solution)/shard_map/pallas_call | solution.py:54
  46.4 3.4 %collective-permute-done.9.refs_1_ = bf16[288,768]{1,0:T(8,128)(2,1)S(1)} collective-permute-done((bf16[288,768]{1,0:T(8,128)(2,1)S(1)}, bf16[288,768]{1,0:T(8,128)(2,1)S(1)}, u32[]{:S(2)}, u32[]{:S(2)}) %collective-permute-start.9) | collective-permute-done | bytes 442400 | tf_op jit(solution)/shard_map/ppermute | solution.py:24
  51.8 1.5 collective-permute-start.7
  55.5 2.6 %collective-permute-done.6.refs_1_ = bf16[128,768]{1,0:T(8,128)(2,1)S(1)} collective-permute-done((bf16[128,768]{1,0:T(8,128)(2,1)S(1)}, bf16[128,768]{1,0:T(8,128)(2,1)S(1)}, u32[]{:S(2)}, u32[]{:S(2)}) %collective-permute-start.6) | collective-permute-done | bytes 196640 | tf_op jit(solution)/shard_map/ppermute | solution.py:24
  58.1 4.5 %collective-permute-done.7.refs_2_ = bf16[128,768]{1,0:T(8,128)(2,1)S(1)} collective-permute-done((bf16[128,768]{1,0:T(8,128)(2,1)S(1)}, bf16[128,768]{1,0:T(8,128)(2,1)S(1)}, u32[]{:S(2)}, u32[]{:S(2)}) %collective-permute-start.7) | collective-permute-done | bytes 196640 | tf_op jit(solution)/shard_map/ppermute | solution.py:24
  62.6 3.2 %shard_map.313 = (bf16[512,768]{1,0:T(8,128)(2,1)S(1)}, f32[128,768]{1,0:T(8,128)S(1)}, f32[128,1]{1,0:T(8,128)S(1)}, bf16[512,768]{1,0:T(8,128)(2,1)S(1)}, bf16...) custom-call(bf16[128,768]{1,0:T(8,128)(2,1)S(1)} %get-tuple-element., ...), custom_call_target="tpu_custom_call" | custom-call | flops 1 | bytes 1 | tf_op jit(solution)/shard_map/pallas_call | solution.py:54
  69.4 4.2 %collective-permute-done.14.refs_1_ = bf16[128,768]{1,0:T(8,128)(2,1)S(1)} collective-permute-done((bf16[128,768]{1,0:T(8,128)(2,1)S(1)}, bf16[128,768]{1,0:T(8,128)(2,1)S(1)}, u32[]{:S(2)}, u32[]{:S(2)}) %collective-permute-start.14) | collective-permute-done | bytes 196640 | tf_op jit(solution)/shard_map/ppermute | solution.py:24
  73.6 3.5 %collective-permute-done.15.refs_2_ = bf16[128,768]{1,0:T(8,128)(2,1)S(1)} collective-permute-done((bf16[128,768]{1,0:T(8,128)(2,1)S(1)}, bf16[128,768]{1,0:T(8,128)(2,1)S(1)}, u32[]{:S(2)}, u32[]{:S(2)}) %collective-permute-start.15) | collective-permute-done | bytes 196640 | tf_op jit(solution)/shard_map/ppermute | solution.py:24
  78.8 1.6 collective-permute-start.18
  81.7 2.6 %collective-permute-done.17.refs_2_.refs_1_ = bf16[128,768]{1,0:T(8,128)(2,1)S(1)} collective-permute-done((bf16[128,768]{1,0:T(8,128)(2,1)S(1)}, bf16[128,768]{1,0:T(8,128)(2,1)S(1)}, u32[]{:S(2)}, u32[]{:S(2)}) %collective-permute-start.17) | collective-permute-done | bytes 196640 | tf_op jit(solution)/shard_map/ppermute | solution.py:24
  84.3 3.5 %collective-permute-done.18.refs_3_.refs_2_ = bf16[128,768]{1,0:T(8,128)(2,1)S(1)} collective-permute-done((bf16[128,768]{1,0:T(8,128)(2,1)S(1)}, bf16[128,768]{1,0:T(8,128)(2,1)S(1)}, u32[]{:S(2)}, u32[]{:S(2)}) %collective-permute-start.18) | collective-permute-done | bytes 196640 | tf_op jit(solution)/shard_map/ppermute | solution.py:24
  88.8 1.6 shard_map.317
  92.1 1.8 %collective-permute-start.30 = (bf16[128,768]{1,0:T(8,128)(2,1)S(1)}, bf16[128,768]{1,0:T(8,128)(2,1)S(1)}, u32[]{:S(2)}, u32[]{:S(2)}) collective-permute-start(bf16[128,768]{1,0:T(8,128)(2,1)S(1)} %get-tuple-element.156), channel_id=1, source_target_pairs={{0,24},{4,28},{8,16},{12,20},{16,8},{20,12},{24,0},{28,4},{1,25},{... | collective-permute-start | bytes 589832 | tf_op jit(solution)/shard_map/ppermute | solution.py:24
  94.2 1.8 %collective-permute-start.21 = (bf16[2,96,768]{2,1,0:T(8,128)(2,1)S(1)}, bf16[2,96,768]{2,1,0:T(8,128)(2,1)S(1)}, u32[]{:S(2)}, u32[]{:S(2)}) collective-permute-start(bf16[2,96,768]{2,1,0:T(8,128)(2,1)S(1)} %get-tuple-element.137), channel_id=1, source_target_pairs={{0,1},{1,0},{2,3},{3,2},{4,5},{5,4},{6,7},{7,6},{8,9},{9,8},{10,11... | collective-permute-start | bytes 884744 | tf_op jit(solution)/shard_map/ppermute | solution.py:24
  98.1 4.7 %collective-permute-done.29.refs_3_ = bf16[128,768]{1,0:T(8,128)(2,1)S(1)} collective-permute-done((bf16[128,768]{1,0:T(8,128)(2,1)S(1)}, bf16[128,768]{1,0:T(8,128)(2,1)S(1)}, u32[]{:S(2)}, u32[]{:S(2)}) %collective-permute-start.29) | collective-permute-done | bytes 196640 | tf_op jit(solution)/shard_map/ppermute | solution.py:24
  107.5 1.8 %collective-permute-start.27 = (bf16[2,96,768]{2,1,0:T(8,128)(2,1)S(1)}, bf16[2,96,768]{2,1,0:T(8,128)(2,1)S(1)}, u32[]{:S(2)}, u32[]{:S(2)}) collective-permute-start(bf16[2,96,768]{2,1,0:T(8,128)(2,1)S(1)} %get-tuple-element.150), channel_id=1, source_target_pairs={{0,1},{1,0},{2,3},{3,2},{4,5},{5,4},{6,7},{7,6},{8,9},{9,8},{10,11... | collective-permute-start | bytes 884744 | tf_op jit(solution)/shard_map/ppermute | solution.py:24
  111.5 3.9 %collective-permute-done.32.refs_6_ = bf16[128,768]{1,0:T(8,128)(2,1)S(1)} collective-permute-done((bf16[128,768]{1,0:T(8,128)(2,1)S(1)}, bf16[128,768]{1,0:T(8,128)(2,1)S(1)}, u32[]{:S(2)}, u32[]{:S(2)}) %collective-permute-start.32) | collective-permute-done | bytes 196640 | tf_op jit(solution)/shard_map/ppermute | solution.py:24
  115.4 5.4 %shard_map.324 = (bf16[512,768]{1,0:T(8,128)(2,1)S(1)}, bf16[512,192]{1,0:T(8,128)(2,1)S(1)}, f32[512,384]{1,0:T(8,128)S(1)}, bf16[128,384]{1,0:T(8,128)(2,1)S(1...) custom-call(bf16[96,768]{1,0:T(8,128)(2,1)S(1)} %get-tuple-element.147.refs_0_, ...), custom_call_target="tpu_custom_call" | custom-call | flops 1 | bytes 1 | tf_op jit(solution)/shard_map/pallas_call | solution.py:54
  124.4 1.8 %collective-permute-done.38.refs_1_ = bf16[4,112,768]{2,1,0:T(8,128)(2,1)S(1)} collective-permute-done((bf16[4,112,768]{2,1,0:T(8,128)(2,1)S(1)}, bf16[4,112,768]{2,1,0:T(8,128)(2,1)S(1)}, u32[]{:S(2)}, u32[]{:S(2)}) %collective-permute-start.38) | collective-permute-done | bytes 688160 | tf_op jit(solution)/shard_map/ppermute | solution.py:24
  126.4 1.9 %collective-permute-start.39 = (bf16[2,112,768]{2,1,0:T(8,128)(2,1)S(1)}, bf16[2,112,768]{2,1,0:T(8,128)(2,1)S(1)}, u32[]{:S(2)}, u32[]{:S(2)}) collective-permute-start(bf16[2,112,768]{2,1,0:T(8,128)(2,1)S(1)} %get-tuple-element.174.refs_1_), channel_id=1, source_target_pairs={{0,1},{1,0},{2,3},{3,2},{4,5},{5,4},{6,7},{7,6},{8,9},{9,8},{10,11... | collective-permute-start | bytes 1032200 | tf_op jit(solution)/shard_map/ppermute | solution.py:24
  130.8 1.8 %collective-permute-start.43 = (bf16[128,768]{1,0:T(8,128)(2,1)S(1)}, bf16[128,768]{1,0:T(8,128)(2,1)S(1)}, u32[]{:S(2)}, u32[]{:S(2)}) collective-permute-start(bf16[128,768]{1,0:T(8,128)(2,1)S(1)} %get-tuple-element.183), channel_id=1, source_target_pairs={{0,24},{4,28},{8,16},{12,20},{16,8},{20,12},{24,0},{28,4},{1,25},{... | collective-permute-start | bytes 589832 | tf_op jit(solution)/shard_map/ppermute | solution.py:24
  133.9 6.1 %collective-permute-done.39.refs_1_ = bf16[2,112,768]{2,1,0:T(8,128)(2,1)S(1)} collective-permute-done((bf16[2,112,768]{2,1,0:T(8,128)(2,1)S(1)}, bf16[2,112,768]{2,1,0:T(8,128)(2,1)S(1)}, u32[]{:S(2)}, u32[]{:S(2)}) %collective-permute-start.39) | collective-permute-done | bytes 344096 | tf_op jit(solution)/shard_map/ppermute | solution.py:24
  144.7 5.1 %collective-permute-done.40.refs_1_ = bf16[112,768]{1,0:T(8,128)(2,1)S(1)} collective-permute-done((bf16[112,768]{1,0:T(8,128)(2,1)S(1)}, bf16[112,768]{1,0:T(8,128)(2,1)S(1)}, u32[]{:S(2)}, u32[]{:S(2)}) %collective-permute-start.40) | collective-permute-done | bytes 172064 | tf_op jit(solution)/shard_map/ppermute | solution.py:24
  149.8 13.7 %all-gather.1 = bf16[448,768]{1,0:T(8,128)(2,1)S(1)} all-gather(bf16[112,768]{1,0:T(8,128)(2,1)S(1)} %shard_map.329.refs_0_), channel_id=3, replica_groups={{0,8,16,24},{4,12,20,28},{1,9,17,25},{5,13,21,29},{2,10,18,26},{6,14,22..., dimensions={0}, use_global_device_ids=true | all-gather | bytes 860160 | tf_op jit(solution)/shard_map/all_gather | solution.py:917
  165.7 1.8 %shard_map.332 = (f32[192,768]{1,0:T(8,128)}, f32[192,768]{1,0:T(8,128)}, f32[192,768]{1,0:T(8,128)}, f32[192,768]{1,0:T(8,128)}, f32[192]{0:T(256)}, /*index=5*...) custom-call(bf16[4,112,768]{2,1,0:T(8,128)(2,1)S(1)} %bitcast.4, ...), custom_call_target="tpu_custom_call" | custom-call | flops 1 | bytes 1 | tf_op jit(solution)/shard_map/pallas_call | solution.py:54
  167.5 2.7 %shard_map.335 = (f32[768,768]{1,0:T(8,128)}, f32[192,3072]{1,0:T(8,128)}, f32[8,128]{1,0:T(8,128)}) custom-call(bf16[4,112,768]{2,1,0:T(8,128)(2,1)S(1)} %bitcast.5, bf16[4,96,768]{2,1,0:T(8,128)(2,1)S(1)} %get-tuple-element.195.refs_1_, bf16[4,96,768]{2,1,0:T(8,128)(2,1)S(1)} %get-tuple-element.196.refs_2_, ...), custom_call_target="tpu_custom_call" | custom-call | flops 1 | bytes 1 | tf_op jit(solution)/shard_map/pallas_call | solution.py:54
  (105 shorter events, 42.7 us)
Async XLA Ops:
  2.3 32.9 %collective-permute-start = (bf16[368,768]{1,0:T(8,128)(2,1)S(1)}, bf16[368,768]{1,0:T(8,128)(2,1)S(1)}, u32[]{:S(2)}, u32[]{:S(2)}) collective-permute-start(bf16[368,768]{1,0:T(8,128)(2,1)S(1)} %shard_map.306.refs_1_.refs_0_), channel_id=1, source_target_pairs={{0,1},{1,0},{2,3},{3,2},{4,5},{5,4},{6,7},{7,6},{8,9},{9,8},{10,11... | collective-permute-start | bytes 1695752 | tf_op jit(solution)/shard_map/ppermute | solution.py:24
  5.4 30.2 %collective-permute-start.1 = (bf16[368,768]{1,0:T(8,128)(2,1)S(1)}, bf16[368,768]{1,0:T(8,128)(2,1)S(1)}, u32[]{:S(2)}, u32[]{:S(2)}) collective-permute-start(bf16[368,768]{1,0:T(8,128)(2,1)S(1)} %shard_map.306.refs_1_.refs_0_), channel_id=1, source_target_pairs={{0,2},{1,3},{2,0},{3,1},{4,6},{5,7},{6,4},{7,5},{8,10},{9,11},{10,... | collective-permute-start | bytes 1695752 | tf_op jit(solution)/shard_map/ppermute | solution.py:24
  20.8 14.5 %collective-permute-start.2 = (bf16[80,768]{1,0:T(8,128)(2,1)S(1)}, bf16[80,768]{1,0:T(8,128)(2,1)S(1)}, u32[]{:S(2)}, u32[]{:S(2)}) collective-permute-start(bf16[80,768]{1,0:T(8,128)(2,1)S(1)} %shard_map.307), channel_id=1, source_target_pairs={{0,3},{1,2},{2,1},{3,0},{4,7},{5,6},{6,5},{7,4},{8,11},{9,10},{10,... | collective-permute-start | bytes 368648 | tf_op jit(solution)/shard_map/ppermute | solution.py:24
  35.8 19.4 %collective-permute-start.10 = (bf16[3,288,768]{2,1,0:T(8,128)(2,1)S(1)}, bf16[3,288,768]{2,1,0:T(8,128)(2,1)S(1)}, u32[]{:S(2)}, u32[]{:S(2)}) collective-permute-start(bf16[3,288,768]{2,1,0:T(8,128)(2,1)S(1)} %get-tuple-element.116.refs_0_), channel_id=1, source_target_pairs={{0,4},{4,0},{8,12},{12,8},{16,20},{20,16},{24,28},{28,24},{1,5},{5... | collective-permute-start | bytes 3981320 | tf_op jit(solution)/shard_map/ppermute | solution.py:24
  36.4 13.3 %collective-permute-start.9 = (bf16[288,768]{1,0:T(8,128)(2,1)S(1)}, bf16[288,768]{1,0:T(8,128)(2,1)S(1)}, u32[]{:S(2)}, u32[]{:S(2)}) collective-permute-start(bf16[288,768]{1,0:T(8,128)(2,1)S(1)} %get-tuple-element.117), channel_id=1, source_target_pairs={{0,1},{1,0},{2,3},{3,2},{4,5},{5,4},{6,7},{7,6},{8,9},{9,8},{10,11... | collective-permute-start | bytes 1327112 | tf_op jit(solution)/shard_map/ppermute | solution.py:24
  50.3 7.8 %collective-permute-start.6 = (bf16[128,768]{1,0:T(8,128)(2,1)S(1)}, bf16[128,768]{1,0:T(8,128)(2,1)S(1)}, u32[]{:S(2)}, u32[]{:S(2)}) collective-permute-start(bf16[128,768]{1,0:T(8,128)(2,1)S(1)} %get-tuple-element.114.refs_0_), channel_id=1, source_target_pairs={{0,8},{4,12},{8,0},{12,4},{16,24},{20,28},{24,16},{28,20},{1,9},{5... | collective-permute-start | bytes 589832 | tf_op jit(solution)/shard_map/ppermute | solution.py:24
  51.8 10.8 %collective-permute-start.7 = (bf16[128,768]{1,0:T(8,128)(2,1)S(1)}, bf16[128,768]{1,0:T(8,128)(2,1)S(1)}, u32[]{:S(2)}, u32[]{:S(2)}) collective-permute-start(bf16[128,768]{1,0:T(8,128)(2,1)S(1)} %get-tuple-element.114.refs_0_), channel_id=1, source_target_pairs={{0,16},{4,20},{8,24},{12,28},{16,0},{20,4},{24,8},{28,12},{1,17},{... | collective-permute-start | bytes 589832 | tf_op jit(solution)/shard_map/ppermute | solution.py:24
  53.3 9.3 %collective-permute-start.8 = (bf16[128,768]{1,0:T(8,128)(2,1)S(1)}, bf16[128,768]{1,0:T(8,128)(2,1)S(1)}, u32[]{:S(2)}, u32[]{:S(2)}) collective-permute-start(bf16[128,768]{1,0:T(8,128)(2,1)S(1)} %get-tuple-element.114.refs_0_), channel_id=1, source_target_pairs={{0,24},{4,28},{8,16},{12,20},{16,8},{20,12},{24,0},{28,4},{1,25},{... | collective-permute-start | bytes 589832 | tf_op jit(solution)/shard_map/ppermute | solution.py:24
  65.9 7.8 %collective-permute-start.14 = (bf16[128,768]{1,0:T(8,128)(2,1)S(1)}, bf16[128,768]{1,0:T(8,128)(2,1)S(1)}, u32[]{:S(2)}, u32[]{:S(2)}) collective-permute-start(bf16[128,768]{1,0:T(8,128)(2,1)S(1)} %get-tuple-element.127), channel_id=1, source_target_pairs={{0,8},{4,12},{8,0},{12,4},{16,24},{20,28},{24,16},{28,20},{1,9},{5... | collective-permute-start | bytes 589832 | tf_op jit(solution)/shard_map/ppermute | solution.py:24
  67.2 10.0 %collective-permute-start.15 = (bf16[128,768]{1,0:T(8,128)(2,1)S(1)}, bf16[128,768]{1,0:T(8,128)(2,1)S(1)}, u32[]{:S(2)}, u32[]{:S(2)}) collective-permute-start(bf16[128,768]{1,0:T(8,128)(2,1)S(1)} %get-tuple-element.128), channel_id=1, source_target_pairs={{0,16},{4,20},{8,24},{12,28},{16,0},{20,4},{24,8},{28,12},{1,17},{... | collective-permute-start | bytes 589832 | tf_op jit(solution)/shard_map/ppermute | solution.py:24
  68.0 9.2 %collective-permute-start.16 = (bf16[128,768]{1,0:T(8,128)(2,1)S(1)}, bf16[128,768]{1,0:T(8,128)(2,1)S(1)}, u32[]{:S(2)}, u32[]{:S(2)}) collective-permute-start(bf16[128,768]{1,0:T(8,128)(2,1)S(1)} %get-tuple-element.129), channel_id=1, source_target_pairs={{0,24},{4,28},{8,16},{12,20},{16,8},{20,12},{24,0},{28,4},{1,25},{... | collective-permute-start | bytes 589832 | tf_op jit(solution)/shard_map/ppermute | solution.py:24
  78.8 9.0 %collective-permute-start.18 = (bf16[128,768]{1,0:T(8,128)(2,1)S(1)}, bf16[128,768]{1,0:T(8,128)(2,1)S(1)}, u32[]{:S(2)}, u32[]{:S(2)}) collective-permute-start(bf16[128,768]{1,0:T(8,128)(2,1)S(1)} %get-tuple-element.133.refs_1_.refs_0_), channel_id=1, source_target_pairs={{0,16},{4,20},{8,24},{12,28},{16,0},{20,4},{24,8},{28,12},{1,17},{... | collective-permute-start | bytes 589832 | tf_op jit(solution)/shard_map/ppermute | solution.py:24
  80.3 7.5 %collective-permute-start.19 = (bf16[128,768]{1,0:T(8,128)(2,1)S(1)}, bf16[128,768]{1,0:T(8,128)(2,1)S(1)}, u32[]{:S(2)}, u32[]{:S(2)}) collective-permute-start(bf16[128,768]{1,0:T(8,128)(2,1)S(1)} %get-tuple-element.133.refs_1_.refs_0_), channel_id=1, source_target_pairs={{0,24},{4,28},{8,16},{12,20},{16,8},{20,12},{24,0},{28,4},{1,25},{... | collective-permute-start | bytes 589832 | tf_op jit(solution)/shard_map/ppermute | solution.py:24
  90.3 7.8 %collective-permute-start.28 = (bf16[128,768]{1,0:T(8,128)(2,1)S(1)}, bf16[128,768]{1,0:T(8,128)(2,1)S(1)}, u32[]{:S(2)}, u32[]{:S(2)}) collective-permute-start(bf16[128,768]{1,0:T(8,128)(2,1)S(1)} %get-tuple-element.154), channel_id=1, source_target_pairs={{0,8},{4,12},{8,0},{12,4},{16,24},{20,28},{24,16},{28,20},{1,9},{5... | collective-permute-start | bytes 589832 | tf_op jit(solution)/shard_map/ppermute | solution.py:24
  91.5 11.2 %collective-permute-start.29 = (bf16[128,768]{1,0:T(8,128)(2,1)S(1)}, bf16[128,768]{1,0:T(8,128)(2,1)S(1)}, u32[]{:S(2)}, u32[]{:S(2)}) collective-permute-start(bf16[128,768]{1,0:T(8,128)(2,1)S(1)} %get-tuple-element.155), channel_id=1, source_target_pairs={{0,16},{4,20},{8,24},{12,28},{16,0},{20,4},{24,8},{28,12},{1,17},{... | collective-permute-start | bytes 589832 | tf_op jit(solution)/shard_map/ppermute | solution.py:24
  92.1 10.6 %collective-permute-start.30 = (bf16[128,768]{1,0:T(8,128)(2,1)S(1)}, bf16[128,768]{1,0:T(8,128)(2,1)S(1)}, u32[]{:S(2)}, u32[]{:S(2)}) collective-permute-start(bf16[128,768]{1,0:T(8,128)(2,1)S(1)} %get-tuple-element.156), channel_id=1, source_target_pairs={{0,24},{4,28},{8,16},{12,20},{16,8},{20,12},{24,0},{28,4},{1,25},{... | collective-permute-start | bytes 589832 | tf_op jit(solution)/shard_map/ppermute | solution.py:24
  94.2 13.2 %collective-permute-start.21 = (bf16[2,96,768]{2,1,0:T(8,128)(2,1)S(1)}, bf16[2,96,768]{2,1,0:T(8,128)(2,1)S(1)}, u32[]{:S(2)}, u32[]{:S(2)}) collective-permute-start(bf16[2,96,768]{2,1,0:T(8,128)(2,1)S(1)} %get-tuple-element.137), channel_id=1, source_target_pairs={{0,1},{1,0},{2,3},{3,2},{4,5},{5,4},{6,7},{7,6},{8,9},{9,8},{10,11... | collective-permute-start | bytes 884744 | tf_op jit(solution)/shard_map/ppermute | solution.py:24
  96.9 6.7 %collective-permute-start.22 = (bf16[96,768]{1,0:T(8,128)(2,1)S(1)}, bf16[96,768]{1,0:T(8,128)(2,1)S(1)}, u32[]{:S(2)}, u32[]{:S(2)}) collective-permute-start(bf16[96,768]{1,0:T(8,128)(2,1)S(1)} %get-tuple-element.142), channel_id=1, source_target_pairs={{0,4},{4,0},{8,12},{12,8},{16,20},{20,16},{24,28},{28,24},{1,5},{5... | collective-permute-start | bytes 442376 | tf_op jit(solution)/shard_map/ppermute | solution.py:24
  103.6 7.8 %collective-permute-start.31 = (bf16[128,768]{1,0:T(8,128)(2,1)S(1)}, bf16[128,768]{1,0:T(8,128)(2,1)S(1)}, u32[]{:S(2)}, u32[]{:S(2)}) collective-permute-start(bf16[128,768]{1,0:T(8,128)(2,1)S(1)} %get-tuple-element.158.refs_4_), channel_id=1, source_target_pairs={{0,8},{4,12},{8,0},{12,4},{16,24},{20,28},{24,16},{28,20},{1,9},{5... | collective-permute-start | bytes 589832 | tf_op jit(solution)/shard_map/ppermute | solution.py:24
  104.6 10.7 %collective-permute-start.32 = (bf16[128,768]{1,0:T(8,128)(2,1)S(1)}, bf16[128,768]{1,0:T(8,128)(2,1)S(1)}, u32[]{:S(2)}, u32[]{:S(2)}) collective-permute-start(bf16[128,768]{1,0:T(8,128)(2,1)S(1)} %get-tuple-element.158.refs_4_), channel_id=1, source_target_pairs={{0,16},{4,20},{8,24},{12,28},{16,0},{20,4},{24,8},{28,12},{1,17},{... | collective-permute-start | bytes 589832 | tf_op jit(solution)/shard_map/ppermute | solution.py:24
  105.8 9.5 %collective-permute-start.33 = (bf16[128,768]{1,0:T(8,128)(2,1)S(1)}, bf16[128,768]{1,0:T(8,128)(2,1)S(1)}, u32[]{:S(2)}, u32[]{:S(2)}) collective-permute-start(bf16[128,768]{1,0:T(8,128)(2,1)S(1)} %get-tuple-element.158.refs_4_), channel_id=1, source_target_pairs={{0,24},{4,28},{8,16},{12,20},{16,8},{20,12},{24,0},{28,4},{1,25},{... | collective-permute-start | bytes 589832 | tf_op jit(solution)/shard_map/ppermute | solution.py:24
  107.5 14.8 %collective-permute-start.27 = (bf16[2,96,768]{2,1,0:T(8,128)(2,1)S(1)}, bf16[2,96,768]{2,1,0:T(8,128)(2,1)S(1)}, u32[]{:S(2)}, u32[]{:S(2)}) collective-permute-start(bf16[2,96,768]{2,1,0:T(8,128)(2,1)S(1)} %get-tuple-element.150), channel_id=1, source_target_pairs={{0,1},{1,0},{2,3},{3,2},{4,5},{5,4},{6,7},{7,6},{8,9},{9,8},{10,11... | collective-permute-start | bytes 884744 | tf_op jit(solution)/shard_map/ppermute | solution.py:24
  109.3 12.1 %collective-permute-start.26 = (bf16[96,768]{1,0:T(8,128)(2,1)S(1)}, bf16[96,768]{1,0:T(8,128)(2,1)S(1)}, u32[]{:S(2)}, u32[]{:S(2)}) collective-permute-start(bf16[96,768]{1,0:T(8,128)(2,1)S(1)} %get-tuple-element.148), channel_id=1, source_target_pairs={{0,2},{1,3},{2,0},{3,1},{4,6},{5,7},{6,4},{7,5},{8,10},{9,11},{10,... | collective-permute-start | bytes 442376 | tf_op jit(solution)/shard_map/ppermute | solution.py:24
  126.4 13.6 %collective-permute-start.39 = (bf16[2,112,768]{2,1,0:T(8,128)(2,1)S(1)}, bf16[2,112,768]{2,1,0:T(8,128)(2,1)S(1)}, u32[]{:S(2)}, u32[]{:S(2)}) collective-permute-start(bf16[2,112,768]{2,1,0:T(8,128)(2,1)S(1)} %get-tuple-element.174.refs_1_), channel_id=1, source_target_pairs={{0,1},{1,0},{2,3},{3,2},{4,5},{5,4},{6,7},{7,6},{8,9},{9,8},{10,11... | collective-permute-start | bytes 1032200 | tf_op jit(solution)/shard_map/ppermute | solution.py:24
  129.1 11.2 %collective-permute-start.41 = (bf16[128,768]{1,0:T(8,128)(2,1)S(1)}, bf16[128,768]{1,0:T(8,128)(2,1)S(1)}, u32[]{:S(2)}, u32[]{:S(2)}) collective-permute-start(bf16[128,768]{1,0:T(8,128)(2,1)S(1)} %get-tuple-element.181), channel_id=1, source_target_pairs={{0,8},{4,12},{8,0},{12,4},{16,24},{20,28},{24,16},{28,20},{1,9},{5... | collective-permute-start | bytes 589832 | tf_op jit(solution)/shard_map/ppermute | solution.py:24
  130.2 10.8 %collective-permute-start.42 = (bf16[128,768]{1,0:T(8,128)(2,1)S(1)}, bf16[128,768]{1,0:T(8,128)(2,1)S(1)}, u32[]{:S(2)}, u32[]{:S(2)}) collective-permute-start(bf16[128,768]{1,0:T(8,128)(2,1)S(1)} %get-tuple-element.182), channel_id=1, source_target_pairs={{0,16},{4,20},{8,24},{12,28},{16,0},{20,4},{24,8},{28,12},{1,17},{... | collective-permute-start | bytes 589832 | tf_op jit(solution)/shard_map/ppermute | solution.py:24
  130.8 10.2 %collective-permute-start.43 = (bf16[128,768]{1,0:T(8,128)(2,1)S(1)}, bf16[128,768]{1,0:T(8,128)(2,1)S(1)}, u32[]{:S(2)}, u32[]{:S(2)}) collective-permute-start(bf16[128,768]{1,0:T(8,128)(2,1)S(1)} %get-tuple-element.183), channel_id=1, source_target_pairs={{0,24},{4,28},{8,16},{12,20},{16,8},{20,12},{24,0},{28,4},{1,25},{... | collective-permute-start | bytes 589832 | tf_op jit(solution)/shard_map/ppermute | solution.py:24
  132.6 7.7 %collective-permute-start.45 = (bf16[96,768]{1,0:T(8,128)(2,1)S(1)}, bf16[96,768]{1,0:T(8,128)(2,1)S(1)}, u32[]{:S(2)}, u32[]{:S(2)}) collective-permute-start(bf16[96,768]{1,0:T(8,128)(2,1)S(1)} %get-tuple-element.194), channel_id=1, source_target_pairs={{0,2},{1,3},{2,0},{3,1},{4,6},{5,7},{6,4},{7,5},{8,10},{9,11},{10,... | collective-permute-start | bytes 442376 | tf_op jit(solution)/shard_map/ppermute | solution.py:24
  140.1 9.7 %collective-permute-start.40 = (bf16[112,768]{1,0:T(8,128)(2,1)S(1)}, bf16[112,768]{1,0:T(8,128)(2,1)S(1)}, u32[]{:S(2)}, u32[]{:S(2)}) collective-permute-start(bf16[112,768]{1,0:T(8,128)(2,1)S(1)} %get-tuple-element.176), channel_id=1, source_target_pairs={{0,2},{1,3},{2,0},{3,1},{4,6},{5,7},{6,4},{7,5},{8,10},{9,11},{10,... | collective-permute-start | bytes 516104 | tf_op jit(solution)/shard_map/ppermute | solution.py:24
  141.1 22.4 %collective-permute-start.46 = (bf16[192,768]{1,0:T(8,128)(2,1)S(1)}, bf16[192,768]{1,0:T(8,128)(2,1)S(1)}, u32[]{:S(2)}, u32[]{:S(2)}) collective-permute-start(bf16[192,768]{1,0:T(8,128)(2,1)S(1)} %shard_map.333.refs_1_), channel_id=1, source_target_pairs={{0,8},{4,12},{8,0},{12,4},{16,24},{20,28},{24,16},{28,20},{1,9},{5... | collective-permute-start | bytes 884744 | tf_op jit(solution)/shard_map/ppermute | solution.py:24
  142.1 21.5 %collective-permute-start.47 = (bf16[192,768]{1,0:T(8,128)(2,1)S(1)}, bf16[192,768]{1,0:T(8,128)(2,1)S(1)}, u32[]{:S(2)}, u32[]{:S(2)}) collective-permute-start(bf16[192,768]{1,0:T(8,128)(2,1)S(1)} %shard_map.333.refs_1_), channel_id=1, source_target_pairs={{0,16},{4,20},{8,24},{12,28},{16,0},{20,4},{24,8},{28,12},{1,17},{... | collective-permute-start | bytes 884744 | tf_op jit(solution)/shard_map/ppermute | solution.py:24
  143.3 20.3 %collective-permute-start.48 = (bf16[192,768]{1,0:T(8,128)(2,1)S(1)}, bf16[192,768]{1,0:T(8,128)(2,1)S(1)}, u32[]{:S(2)}, u32[]{:S(2)}) collective-permute-start(bf16[192,768]{1,0:T(8,128)(2,1)S(1)} %shard_map.333.refs_1_), channel_id=1, source_target_pairs={{0,24},{4,28},{8,16},{12,20},{16,8},{20,12},{24,0},{28,4},{1,25},{... | collective-permute-start | bytes 884744 | tf_op jit(solution)/shard_map/ppermute | solution.py:24
  (20 other events, 73.3 us)

commit v6 on v5

--- a/solution.py
+++ b/solution.py
@@ -247,7 +247,12 @@
         context[:, h * HEAD_DIM : (h + 1) * HEAD_DIM] = out.T.astype(LOW)
 
 
-def attend_back(queries, keys_values, grad_context, probs, grad_queries, grad_keys_values):
+def attend_back(
+    queries, keys_values, grad_context, probs, grad_queries, grad_keys_values, whole=True
+):
+    def add(span, term):
+        return term if whole else grad_keys_values[:, span] + term
+
     part = queries.shape[1]
     scale = HEAD_DIM ** (-0.5)
     for h in range(part // HEAD_DIM):
@@ -256,13 +261,13 @@
         keys, values = keys_values[:, span], keys_values[:, span_v]
         grads = grad_context[:, span]
         soft = probs[h]
-        grad_keys_values[:, span_v] += dot(soft, grads)
+        grad_keys_values[:, span_v] = add(span_v, dot(soft, grads))
         grad_probs = dot_rt(values, grads)
         wide = soft.astype(WIDE)
         delta = jnp.sum(wide * grad_probs, 0, keepdims=True)
         grad_scores = (wide * (grad_probs - delta)).astype(LOW)
         grad_queries[:, span] = (dot_lt(keys, grad_scores) * scale).T.astype(LOW)
-        grad_keys_values[:, span] += dot(grad_scores, queries[:, span])
+        grad_keys_values[:, span] = add(span, dot(grad_scores, queries[:, span]))
 
 
 def beside(rows, out):
@@ -299,7 +304,6 @@
     keys_values[:count] = kv_own[...]
     keys_values[count:] = kv_far[...]
     context_back(g0, g1, g2, g3, w_output, grad_low, grad_context)
-    total[...] = jnp.zeros(total.shape, WIDE)
     attend_back(queries, keys_values, grad_context, probs, grad_queries, total)
     grad_own[...] = total[:count]
     tokens = count // CHIPS
@@ -312,7 +316,7 @@
     def _():
         grad_keys_values[...] = jnp.zeros(grad_keys_values.shape, WIDE)
 
-    attend_back(queries, keys_values, grads, probs, grad_queries, grad_keys_values)
+    attend_back(queries, keys_values, grads, probs, grad_queries, grad_keys_values, False)
 
 
 def attention_block(queries, keys_values):

time: 170 us -> 170 us (level)
  no operation moved by 1% of the time
where the time goes in v6:
time: 170 us
  waiting for transfers between devices  67.1 us (39%)
  starting transfers between devices  46.4 us (27%)
  Pallas kernels  30 us (18%)
  blocking collectives  25.5 us (15%)
    ppermute x51, waiting for transfers between devices, partner(): return lax.ppermute(block, axis, [(i, i ^ bit) for i in devices])  67.1 us
    ppermute x51, starting transfers between devices, partner(): return lax.ppermute(block, axis, [(i, i ^ bit) for i in devices])  46.4 us
    pallas_call x31, Pallas kernels, kernel(): pl.pallas_call(step, out_shape=[o if n in last else pltpu.VMEM(o.shape, o...  30 us
    all_gather x1, blocking collectives, per_device(): rest_all = lax.all_gather(rest_total, 'ctx', axis_index_groups=teams)  13.7 us
    all_gather x1, blocking collectives, per_device(): seen = lax.all_gather(own, 'ctx', axis_index_groups=teams)  11.8 us
  transfers between devices with their start and end apart: 51, of which 23 were waited for; matrix products, arithmetic and copies ran while one was open for 0% of the time, Pallas kernels for 11%

profile of v6, /device:TPU:0, one launch (start us, length us, event | category | flops | bytes accessed | tf_op | source)
XLA Modules:
  0.0 170.1 jit_solution(12472214468052189606)
XLA Ops:
  0.7 1.7 shard_map.306.refs_1_.refs_0_
  2.3 3.1 %collective-permute-start = (bf16[368,768]{1,0:T(8,128)(2,1)S(1)}, bf16[368,768]{1,0:T(8,128)(2,1)S(1)}, u32[]{:S(2)}, u32[]{:S(2)}) collective-permute-start(bf16[368,768]{1,0:T(8,128)(2,1)S(1)} %shard_map.306.refs_1_.refs_0_), channel_id=1, source_target_pairs={{0,1},{1,0},{2,3},{3,2},{4,5},{5,4},{6,7},{7,6},{8,9},{9,8},{10,11... | collective-permute-start | bytes 1695752 | tf_op jit(solution)/shard_map/ppermute | solution.py:24
  5.4 2.6 %collective-permute-start.1 = (bf16[368,768]{1,0:T(8,128)(2,1)S(1)}, bf16[368,768]{1,0:T(8,128)(2,1)S(1)}, u32[]{:S(2)}, u32[]{:S(2)}) collective-permute-start(bf16[368,768]{1,0:T(8,128)(2,1)S(1)} %shard_map.306.refs_1_.refs_0_), channel_id=1, source_target_pairs={{0,2},{1,3},{2,0},{3,1},{4,6},{5,7},{6,4},{7,5},{8,10},{9,11},{10,... | collective-permute-start | bytes 1695752 | tf_op jit(solution)/shard_map/ppermute | solution.py:24
  9.0 11.8 %all-gather = bf16[576,768]{1,0:T(8,128)(2,1)S(1)} all-gather(bf16[144,768]{1,0:T(8,128)(2,1)S(1)} %shard_map.305), channel_id=2, replica_groups={{0,8,16,24},{4,12,20,28},{1,9,17,25},{5,13,21,29},{2,10,18,26},{6,14,22..., dimensions={0}, use_global_device_ids=true | all-gather | bytes 1105920 | tf_op jit(solution)/shard_map/all_gather | solution.py:654
  21.1 14.2 %collective-permute-done.2.refs_3_ = bf16[80,768]{1,0:T(8,128)(2,1)S(1)} collective-permute-done((bf16[80,768]{1,0:T(8,128)(2,1)S(1)}, bf16[80,768]{1,0:T(8,128)(2,1)S(1)}, u32[]{:S(2)}, u32[]{:S(2)}) %collective-permute-start.2) | collective-permute-done | bytes 122912 | tf_op jit(solution)/shard_map/ppermute | solution.py:24
  36.4 2.9 %collective-permute-start.9 = (bf16[288,768]{1,0:T(8,128)(2,1)S(1)}, bf16[288,768]{1,0:T(8,128)(2,1)S(1)}, u32[]{:S(2)}, u32[]{:S(2)}) collective-permute-start(bf16[288,768]{1,0:T(8,128)(2,1)S(1)} %get-tuple-element.117), channel_id=1, source_target_pairs={{0,1},{1,0},{2,3},{3,2},{4,5},{5,4},{6,7},{7,6},{8,9},{9,8},{10,11... | collective-permute-start | bytes 1327112 | tf_op jit(solution)/shard_map/ppermute | solution.py:24
  42.5 3.9 %shard_map.310 = (bf16[128,768]{1,0:T(8,128)(2,1)S(1)}, bf16[3,1024,512]{2,1,0:T(8,128)(2,1)S(1)}) custom-call(bf16[512,192]{1,0:T(8,128)(2,1)S(1)} %get-tuple-element.111.refs_0_.refs_1_, bf16[512,384]{1,0:T(8,128)(2,1)S(1)} %get-tuple-element.112.refs_1_.refs_2_, bf16[512,384]{1,0:T(8,128)(2,1)S(1)} %collective-permute-done.4.refs_2_.refs_3_, ...), custom_call_target="tpu_custom_call" | custom-call | flops 1 | bytes 1 | tf_op jit(solution)/shard_map/pallas_call | solution.py:54
  46.4 3.4 %collective-permute-done.9.refs_1_ = bf16[288,768]{1,0:T(8,128)(2,1)S(1)} collective-permute-done((bf16[288,768]{1,0:T(8,128)(2,1)S(1)}, bf16[288,768]{1,0:T(8,128)(2,1)S(1)}, u32[]{:S(2)}, u32[]{:S(2)}) %collective-permute-start.9) | collective-permute-done | bytes 442400 | tf_op jit(solution)/shard_map/ppermute | solution.py:24
  51.8 1.5 collective-permute-start.7
  55.5 2.6 %collective-permute-done.6.refs_1_ = bf16[128,768]{1,0:T(8,128)(2,1)S(1)} collective-permute-done((bf16[128,768]{1,0:T(8,128)(2,1)S(1)}, bf16[128,768]{1,0:T(8,128)(2,1)S(1)}, u32[]{:S(2)}, u32[]{:S(2)}) %collective-permute-start.6) | collective-permute-done | bytes 196640 | tf_op jit(solution)/shard_map/ppermute | solution.py:24
  58.1 4.5 %collective-permute-done.7.refs_2_ = bf16[128,768]{1,0:T(8,128)(2,1)S(1)} collective-permute-done((bf16[128,768]{1,0:T(8,128)(2,1)S(1)}, bf16[128,768]{1,0:T(8,128)(2,1)S(1)}, u32[]{:S(2)}, u32[]{:S(2)}) %collective-permute-start.7) | collective-permute-done | bytes 196640 | tf_op jit(solution)/shard_map/ppermute | solution.py:24
  62.6 3.2 %shard_map.313 = (bf16[512,768]{1,0:T(8,128)(2,1)S(1)}, f32[128,768]{1,0:T(8,128)S(1)}, f32[128,1]{1,0:T(8,128)S(1)}, bf16[512,768]{1,0:T(8,128)(2,1)S(1)}, bf16...) custom-call(bf16[128,768]{1,0:T(8,128)(2,1)S(1)} %get-tuple-element., ...), custom_call_target="tpu_custom_call" | custom-call | flops 1 | bytes 1 | tf_op jit(solution)/shard_map/pallas_call | solution.py:54
  69.4 4.2 %collective-permute-done.14.refs_1_ = bf16[128,768]{1,0:T(8,128)(2,1)S(1)} collective-permute-done((bf16[128,768]{1,0:T(8,128)(2,1)S(1)}, bf16[128,768]{1,0:T(8,128)(2,1)S(1)}, u32[]{:S(2)}, u32[]{:S(2)}) %collective-permute-start.14) | collective-permute-done | bytes 196640 | tf_op jit(solution)/shard_map/ppermute | solution.py:24
  73.6 3.5 %collective-permute-done.15.refs_2_ = bf16[128,768]{1,0:T(8,128)(2,1)S(1)} collective-permute-done((bf16[128,768]{1,0:T(8,128)(2,1)S(1)}, bf16[128,768]{1,0:T(8,128)(2,1)S(1)}, u32[]{:S(2)}, u32[]{:S(2)}) %collective-permute-start.15) | collective-permute-done | bytes 196640 | tf_op jit(solution)/shard_map/ppermute | solution.py:24
  78.8 1.6 collective-permute-start.18
  81.7 2.6 %collective-permute-done.17.refs_2_.refs_1_ = bf16[128,768]{1,0:T(8,128)(2,1)S(1)} collective-permute-done((bf16[128,768]{1,0:T(8,128)(2,1)S(1)}, bf16[128,768]{1,0:T(8,128)(2,1)S(1)}, u32[]{:S(2)}, u32[]{:S(2)}) %collective-permute-start.17) | collective-permute-done | bytes 196640 | tf_op jit(solution)/shard_map/ppermute | solution.py:24
  84.3 3.5 %collective-permute-done.18.refs_3_.refs_2_ = bf16[128,768]{1,0:T(8,128)(2,1)S(1)} collective-permute-done((bf16[128,768]{1,0:T(8,128)(2,1)S(1)}, bf16[128,768]{1,0:T(8,128)(2,1)S(1)}, u32[]{:S(2)}, u32[]{:S(2)}) %collective-permute-start.18) | collective-permute-done | bytes 196640 | tf_op jit(solution)/shard_map/ppermute | solution.py:24
  88.8 1.6 shard_map.317
  92.1 1.8 %collective-permute-start.30 = (bf16[128,768]{1,0:T(8,128)(2,1)S(1)}, bf16[128,768]{1,0:T(8,128)(2,1)S(1)}, u32[]{:S(2)}, u32[]{:S(2)}) collective-permute-start(bf16[128,768]{1,0:T(8,128)(2,1)S(1)} %get-tuple-element.156), channel_id=1, source_target_pairs={{0,24},{4,28},{8,16},{12,20},{16,8},{20,12},{24,0},{28,4},{1,25},{... | collective-permute-start | bytes 589832 | tf_op jit(solution)/shard_map/ppermute | solution.py:24
  94.2 1.8 %collective-permute-start.21 = (bf16[2,96,768]{2,1,0:T(8,128)(2,1)S(1)}, bf16[2,96,768]{2,1,0:T(8,128)(2,1)S(1)}, u32[]{:S(2)}, u32[]{:S(2)}) collective-permute-start(bf16[2,96,768]{2,1,0:T(8,128)(2,1)S(1)} %get-tuple-element.137), channel_id=1, source_target_pairs={{0,1},{1,0},{2,3},{3,2},{4,5},{5,4},{6,7},{7,6},{8,9},{9,8},{10,11... | collective-permute-start | bytes 884744 | tf_op jit(solution)/shard_map/ppermute | solution.py:24
  98.1 4.7 %collective-permute-done.29.refs_3_ = bf16[128,768]{1,0:T(8,128)(2,1)S(1)} collective-permute-done((bf16[128,768]{1,0:T(8,128)(2,1)S(1)}, bf16[128,768]{1,0:T(8,128)(2,1)S(1)}, u32[]{:S(2)}, u32[]{:S(2)}) %collective-permute-start.29) | collective-permute-done | bytes 196640 | tf_op jit(solution)/shard_map/ppermute | solution.py:24
  107.5 1.8 %collective-permute-start.27 = (bf16[2,96,768]{2,1,0:T(8,128)(2,1)S(1)}, bf16[2,96,768]{2,1,0:T(8,128)(2,1)S(1)}, u32[]{:S(2)}, u32[]{:S(2)}) collective-permute-start(bf16[2,96,768]{2,1,0:T(8,128)(2,1)S(1)} %get-tuple-element.150), channel_id=1, source_target_pairs={{0,1},{1,0},{2,3},{3,2},{4,5},{5,4},{6,7},{7,6},{8,9},{9,8},{10,11... | collective-permute-start | bytes 884744 | tf_op jit(solution)/shard_map/ppermute | solution.py:24
  111.5 3.9 %collective-permute-done.32.refs_6_ = bf16[128,768]{1,0:T(8,128)(2,1)S(1)} collective-permute-done((bf16[128,768]{1,0:T(8,128)(2,1)S(1)}, bf16[128,768]{1,0:T(8,128)(2,1)S(1)}, u32[]{:S(2)}, u32[]{:S(2)}) %collective-permute-start.32) | collective-permute-done | bytes 196640 | tf_op jit(solution)/shard_map/ppermute | solution.py:24
  115.4 5.4 %shard_map.324 = (bf16[512,768]{1,0:T(8,128)(2,1)S(1)}, bf16[512,192]{1,0:T(8,128)(2,1)S(1)}, f32[512,384]{1,0:T(8,128)S(1)}, bf16[128,384]{1,0:T(8,128)(2,1)S(1...) custom-call(bf16[96,768]{1,0:T(8,128)(2,1)S(1)} %get-tuple-element.147.refs_0_, ...), custom_call_target="tpu_custom_call" | custom-call | flops 1 | bytes 1 | tf_op jit(solution)/shard_map/pallas_call | solution.py:54
  124.5 1.8 %collective-permute-done.38.refs_1_ = bf16[4,112,768]{2,1,0:T(8,128)(2,1)S(1)} collective-permute-done((bf16[4,112,768]{2,1,0:T(8,128)(2,1)S(1)}, bf16[4,112,768]{2,1,0:T(8,128)(2,1)S(1)}, u32[]{:S(2)}, u32[]{:S(2)}) %collective-permute-start.38) | collective-permute-done | bytes 688160 | tf_op jit(solution)/shard_map/ppermute | solution.py:24
  126.4 1.8 %collective-permute-start.39 = (bf16[2,112,768]{2,1,0:T(8,128)(2,1)S(1)}, bf16[2,112,768]{2,1,0:T(8,128)(2,1)S(1)}, u32[]{:S(2)}, u32[]{:S(2)}) collective-permute-start(bf16[2,112,768]{2,1,0:T(8,128)(2,1)S(1)} %get-tuple-element.174.refs_1_), channel_id=1, source_target_pairs={{0,1},{1,0},{2,3},{3,2},{4,5},{5,4},{6,7},{7,6},{8,9},{9,8},{10,11... | collective-permute-start | bytes 1032200 | tf_op jit(solution)/shard_map/ppermute | solution.py:24
  130.8 1.7 %collective-permute-start.43 = (bf16[128,768]{1,0:T(8,128)(2,1)S(1)}, bf16[128,768]{1,0:T(8,128)(2,1)S(1)}, u32[]{:S(2)}, u32[]{:S(2)}) collective-permute-start(bf16[128,768]{1,0:T(8,128)(2,1)S(1)} %get-tuple-element.183), channel_id=1, source_target_pairs={{0,24},{4,28},{8,16},{12,20},{16,8},{20,12},{24,0},{28,4},{1,25},{... | collective-permute-start | bytes 589832 | tf_op jit(solution)/shard_map/ppermute | solution.py:24
  133.9 6.1 %collective-permute-done.39.refs_1_ = bf16[2,112,768]{2,1,0:T(8,128)(2,1)S(1)} collective-permute-done((bf16[2,112,768]{2,1,0:T(8,128)(2,1)S(1)}, bf16[2,112,768]{2,1,0:T(8,128)(2,1)S(1)}, u32[]{:S(2)}, u32[]{:S(2)}) %collective-permute-start.39) | collective-permute-done | bytes 344096 | tf_op jit(solution)/shard_map/ppermute | solution.py:24
  144.6 5.1 %collective-permute-done.40.refs_1_ = bf16[112,768]{1,0:T(8,128)(2,1)S(1)} collective-permute-done((bf16[112,768]{1,0:T(8,128)(2,1)S(1)}, bf16[112,768]{1,0:T(8,128)(2,1)S(1)}, u32[]{:S(2)}, u32[]{:S(2)}) %collective-permute-start.40) | collective-permute-done | bytes 172064 | tf_op jit(solution)/shard_map/ppermute | solution.py:24
  149.8 13.7 %all-gather.1 = bf16[448,768]{1,0:T(8,128)(2,1)S(1)} all-gather(bf16[112,768]{1,0:T(8,128)(2,1)S(1)} %shard_map.329.refs_0_), channel_id=3, replica_groups={{0,8,16,24},{4,12,20,28},{1,9,17,25},{5,13,21,29},{2,10,18,26},{6,14,22..., dimensions={0}, use_global_device_ids=true | all-gather | bytes 860160 | tf_op jit(solution)/shard_map/all_gather | solution.py:921
  165.7 1.8 %shard_map.332 = (f32[192,768]{1,0:T(8,128)}, f32[192,768]{1,0:T(8,128)}, f32[192,768]{1,0:T(8,128)}, f32[192,768]{1,0:T(8,128)}, f32[192]{0:T(256)}, /*index=5*...) custom-call(bf16[4,112,768]{2,1,0:T(8,128)(2,1)S(1)} %bitcast.4, ...), custom_call_target="tpu_custom_call" | custom-call | flops 1 | bytes 1 | tf_op jit(solution)/shard_map/pallas_call | solution.py:54
  167.4 2.7 %shard_map.335 = (f32[768,768]{1,0:T(8,128)}, f32[192,3072]{1,0:T(8,128)}, f32[8,128]{1,0:T(8,128)}) custom-call(bf16[4,112,768]{2,1,0:T(8,128)(2,1)S(1)} %bitcast.5, bf16[4,96,768]{2,1,0:T(8,128)(2,1)S(1)} %get-tuple-element.195.refs_1_, bf16[4,96,768]{2,1,0:T(8,128)(2,1)S(1)} %get-tuple-element.196.refs_2_, ...), custom_call_target="tpu_custom_call" | custom-call | flops 1 | bytes 1 | tf_op jit(solution)/shard_map/pallas_call | solution.py:54
  (105 shorter events, 42.8 us)
Async XLA Ops:
  2.3 32.9 %collective-permute-start = (bf16[368,768]{1,0:T(8,128)(2,1)S(1)}, bf16[368,768]{1,0:T(8,128)(2,1)S(1)}, u32[]{:S(2)}, u32[]{:S(2)}) collective-permute-start(bf16[368,768]{1,0:T(8,128)(2,1)S(1)} %shard_map.306.refs_1_.refs_0_), channel_id=1, source_target_pairs={{0,1},{1,0},{2,3},{3,2},{4,5},{5,4},{6,7},{7,6},{8,9},{9,8},{10,11... | collective-permute-start | bytes 1695752 | tf_op jit(solution)/shard_map/ppermute | solution.py:24
  5.4 30.2 %collective-permute-start.1 = (bf16[368,768]{1,0:T(8,128)(2,1)S(1)}, bf16[368,768]{1,0:T(8,128)(2,1)S(1)}, u32[]{:S(2)}, u32[]{:S(2)}) collective-permute-start(bf16[368,768]{1,0:T(8,128)(2,1)S(1)} %shard_map.306.refs_1_.refs_0_), channel_id=1, source_target_pairs={{0,2},{1,3},{2,0},{3,1},{4,6},{5,7},{6,4},{7,5},{8,10},{9,11},{10,... | collective-permute-start | bytes 1695752 | tf_op jit(solution)/shard_map/ppermute | solution.py:24
  20.8 14.5 %collective-permute-start.2 = (bf16[80,768]{1,0:T(8,128)(2,1)S(1)}, bf16[80,768]{1,0:T(8,128)(2,1)S(1)}, u32[]{:S(2)}, u32[]{:S(2)}) collective-permute-start(bf16[80,768]{1,0:T(8,128)(2,1)S(1)} %shard_map.307), channel_id=1, source_target_pairs={{0,3},{1,2},{2,1},{3,0},{4,7},{5,6},{6,5},{7,4},{8,11},{9,10},{10,... | collective-permute-start | bytes 368648 | tf_op jit(solution)/shard_map/ppermute | solution.py:24
  35.8 19.4 %collective-permute-start.10 = (bf16[3,288,768]{2,1,0:T(8,128)(2,1)S(1)}, bf16[3,288,768]{2,1,0:T(8,128)(2,1)S(1)}, u32[]{:S(2)}, u32[]{:S(2)}) collective-permute-start(bf16[3,288,768]{2,1,0:T(8,128)(2,1)S(1)} %get-tuple-element.116.refs_0_), channel_id=1, source_target_pairs={{0,4},{4,0},{8,12},{12,8},{16,20},{20,16},{24,28},{28,24},{1,5},{5... | collective-permute-start | bytes 3981320 | tf_op jit(solution)/shard_map/ppermute | solution.py:24
  36.4 13.3 %collective-permute-start.9 = (bf16[288,768]{1,0:T(8,128)(2,1)S(1)}, bf16[288,768]{1,0:T(8,128)(2,1)S(1)}, u32[]{:S(2)}, u32[]{:S(2)}) collective-permute-start(bf16[288,768]{1,0:T(8,128)(2,1)S(1)} %get-tuple-element.117), channel_id=1, source_target_pairs={{0,1},{1,0},{2,3},{3,2},{4,5},{5,4},{6,7},{7,6},{8,9},{9,8},{10,11... | collective-permute-start | bytes 1327112 | tf_op jit(solution)/shard_map/ppermute | solution.py:24
  50.3 7.8 %collective-permute-start.6 = (bf16[128,768]{1,0:T(8,128)(2,1)S(1)}, bf16[128,768]{1,0:T(8,128)(2,1)S(1)}, u32[]{:S(2)}, u32[]{:S(2)}) collective-permute-start(bf16[128,768]{1,0:T(8,128)(2,1)S(1)} %get-tuple-element.114.refs_0_), channel_id=1, source_target_pairs={{0,8},{4,12},{8,0},{12,4},{16,24},{20,28},{24,16},{28,20},{1,9},{5... | collective-permute-start | bytes 589832 | tf_op jit(solution)/shard_map/ppermute | solution.py:24
  51.8 10.8 %collective-permute-start.7 = (bf16[128,768]{1,0:T(8,128)(2,1)S(1)}, bf16[128,768]{1,0:T(8,128)(2,1)S(1)}, u32[]{:S(2)}, u32[]{:S(2)}) collective-permute-start(bf16[128,768]{1,0:T(8,128)(2,1)S(1)} %get-tuple-element.114.refs_0_), channel_id=1, source_target_pairs={{0,16},{4,20},{8,24},{12,28},{16,0},{20,4},{24,8},{28,12},{1,17},{... | collective-permute-start | bytes 589832 | tf_op jit(solution)/shard_map/ppermute | solution.py:24
  53.3 9.3 %collective-permute-start.8 = (bf16[128,768]{1,0:T(8,128)(2,1)S(1)}, bf16[128,768]{1,0:T(8,128)(2,1)S(1)}, u32[]{:S(2)}, u32[]{:S(2)}) collective-permute-start(bf16[128,768]{1,0:T(8,128)(2,1)S(1)} %get-tuple-element.114.refs_0_), channel_id=1, source_target_pairs={{0,24},{4,28},{8,16},{12,20},{16,8},{20,12},{24,0},{28,4},{1,25},{... | collective-permute-start | bytes 589832 | tf_op jit(solution)/shard_map/ppermute | solution.py:24
  65.9 7.8 %collective-permute-start.14 = (bf16[128,768]{1,0:T(8,128)(2,1)S(1)}, bf16[128,768]{1,0:T(8,128)(2,1)S(1)}, u32[]{:S(2)}, u32[]{:S(2)}) collective-permute-start(bf16[128,768]{1,0:T(8,128)(2,1)S(1)} %get-tuple-element.127), channel_id=1, source_target_pairs={{0,8},{4,12},{8,0},{12,4},{16,24},{20,28},{24,16},{28,20},{1,9},{5... | collective-permute-start | bytes 589832 | tf_op jit(solution)/shard_map/ppermute | solution.py:24
  67.2 10.0 %collective-permute-start.15 = (bf16[128,768]{1,0:T(8,128)(2,1)S(1)}, bf16[128,768]{1,0:T(8,128)(2,1)S(1)}, u32[]{:S(2)}, u32[]{:S(2)}) collective-permute-start(bf16[128,768]{1,0:T(8,128)(2,1)S(1)} %get-tuple-element.128), channel_id=1, source_target_pairs={{0,16},{4,20},{8,24},{12,28},{16,0},{20,4},{24,8},{28,12},{1,17},{... | collective-permute-start | bytes 589832 | tf_op jit(solution)/shard_map/ppermute | solution.py:24
  68.0 9.2 %collective-permute-start.16 = (bf16[128,768]{1,0:T(8,128)(2,1)S(1)}, bf16[128,768]{1,0:T(8,128)(2,1)S(1)}, u32[]{:S(2)}, u32[]{:S(2)}) collective-permute-start(bf16[128,768]{1,0:T(8,128)(2,1)S(1)} %get-tuple-element.129), channel_id=1, source_target_pairs={{0,24},{4,28},{8,16},{12,20},{16,8},{20,12},{24,0},{28,4},{1,25},{... | collective-permute-start | bytes 589832 | tf_op jit(solution)/shard_map/ppermute | solution.py:24
  78.8 9.0 %collective-permute-start.18 = (bf16[128,768]{1,0:T(8,128)(2,1)S(1)}, bf16[128,768]{1,0:T(8,128)(2,1)S(1)}, u32[]{:S(2)}, u32[]{:S(2)}) collective-permute-start(bf16[128,768]{1,0:T(8,128)(2,1)S(1)} %get-tuple-element.133.refs_1_.refs_0_), channel_id=1, source_target_pairs={{0,16},{4,20},{8,24},{12,28},{16,0},{20,4},{24,8},{28,12},{1,17},{... | collective-permute-start | bytes 589832 | tf_op jit(solution)/shard_map/ppermute | solution.py:24
  80.3 7.5 %collective-permute-start.19 = (bf16[128,768]{1,0:T(8,128)(2,1)S(1)}, bf16[128,768]{1,0:T(8,128)(2,1)S(1)}, u32[]{:S(2)}, u32[]{:S(2)}) collective-permute-start(bf16[128,768]{1,0:T(8,128)(2,1)S(1)} %get-tuple-element.133.refs_1_.refs_0_), channel_id=1, source_target_pairs={{0,24},{4,28},{8,16},{12,20},{16,8},{20,12},{24,0},{28,4},{1,25},{... | collective-permute-start | bytes 589832 | tf_op jit(solution)/shard_map/ppermute | solution.py:24
  90.3 7.8 %collective-permute-start.28 = (bf16[128,768]{1,0:T(8,128)(2,1)S(1)}, bf16[128,768]{1,0:T(8,128)(2,1)S(1)}, u32[]{:S(2)}, u32[]{:S(2)}) collective-permute-start(bf16[128,768]{1,0:T(8,128)(2,1)S(1)} %get-tuple-element.154), channel_id=1, source_target_pairs={{0,8},{4,12},{8,0},{12,4},{16,24},{20,28},{24,16},{28,20},{1,9},{5... | collective-permute-start | bytes 589832 | tf_op jit(solution)/shard_map/ppermute | solution.py:24
  91.5 11.2 %collective-permute-start.29 = (bf16[128,768]{1,0:T(8,128)(2,1)S(1)}, bf16[128,768]{1,0:T(8,128)(2,1)S(1)}, u32[]{:S(2)}, u32[]{:S(2)}) collective-permute-start(bf16[128,768]{1,0:T(8,128)(2,1)S(1)} %get-tuple-element.155), channel_id=1, source_target_pairs={{0,16},{4,20},{8,24},{12,28},{16,0},{20,4},{24,8},{28,12},{1,17},{... | collective-permute-start | bytes 589832 | tf_op jit(solution)/shard_map/ppermute | solution.py:24
  92.1 10.6 %collective-permute-start.30 = (bf16[128,768]{1,0:T(8,128)(2,1)S(1)}, bf16[128,768]{1,0:T(8,128)(2,1)S(1)}, u32[]{:S(2)}, u32[]{:S(2)}) collective-permute-start(bf16[128,768]{1,0:T(8,128)(2,1)S(1)} %get-tuple-element.156), channel_id=1, source_target_pairs={{0,24},{4,28},{8,16},{12,20},{16,8},{20,12},{24,0},{28,4},{1,25},{... | collective-permute-start | bytes 589832 | tf_op jit(solution)/shard_map/ppermute | solution.py:24
  94.2 13.2 %collective-permute-start.21 = (bf16[2,96,768]{2,1,0:T(8,128)(2,1)S(1)}, bf16[2,96,768]{2,1,0:T(8,128)(2,1)S(1)}, u32[]{:S(2)}, u32[]{:S(2)}) collective-permute-start(bf16[2,96,768]{2,1,0:T(8,128)(2,1)S(1)} %get-tuple-element.137), channel_id=1, source_target_pairs={{0,1},{1,0},{2,3},{3,2},{4,5},{5,4},{6,7},{7,6},{8,9},{9,8},{10,11... | collective-permute-start | bytes 884744 | tf_op jit(solution)/shard_map/ppermute | solution.py:24
  96.9 6.7 %collective-permute-start.22 = (bf16[96,768]{1,0:T(8,128)(2,1)S(1)}, bf16[96,768]{1,0:T(8,128)(2,1)S(1)}, u32[]{:S(2)}, u32[]{:S(2)}) collective-permute-start(bf16[96,768]{1,0:T(8,128)(2,1)S(1)} %get-tuple-element.142), channel_id=1, source_target_pairs={{0,4},{4,0},{8,12},{12,8},{16,20},{20,16},{24,28},{28,24},{1,5},{5... | collective-permute-start | bytes 442376 | tf_op jit(solution)/shard_map/ppermute | solution.py:24
  103.6 7.8 %collective-permute-start.31 = (bf16[128,768]{1,0:T(8,128)(2,1)S(1)}, bf16[128,768]{1,0:T(8,128)(2,1)S(1)}, u32[]{:S(2)}, u32[]{:S(2)}) collective-permute-start(bf16[128,768]{1,0:T(8,128)(2,1)S(1)} %get-tuple-element.158.refs_4_), channel_id=1, source_target_pairs={{0,8},{4,12},{8,0},{12,4},{16,24},{20,28},{24,16},{28,20},{1,9},{5... | collective-permute-start | bytes 589832 | tf_op jit(solution)/shard_map/ppermute | solution.py:24
  104.6 10.7 %collective-permute-start.32 = (bf16[128,768]{1,0:T(8,128)(2,1)S(1)}, bf16[128,768]{1,0:T(8,128)(2,1)S(1)}, u32[]{:S(2)}, u32[]{:S(2)}) collective-permute-start(bf16[128,768]{1,0:T(8,128)(2,1)S(1)} %get-tuple-element.158.refs_4_), channel_id=1, source_target_pairs={{0,16},{4,20},{8,24},{12,28},{16,0},{20,4},{24,8},{28,12},{1,17},{... | collective-permute-start | bytes 589832 | tf_op jit(solution)/shard_map/ppermute | solution.py:24
  105.8 9.5 %collective-permute-start.33 = (bf16[128,768]{1,0:T(8,128)(2,1)S(1)}, bf16[128,768]{1,0:T(8,128)(2,1)S(1)}, u32[]{:S(2)}, u32[]{:S(2)}) collective-permute-start(bf16[128,768]{1,0:T(8,128)(2,1)S(1)} %get-tuple-element.158.refs_4_), channel_id=1, source_target_pairs={{0,24},{4,28},{8,16},{12,20},{16,8},{20,12},{24,0},{28,4},{1,25},{... | collective-permute-start | bytes 589832 | tf_op jit(solution)/shard_map/ppermute | solution.py:24
  107.5 14.8 %collective-permute-start.27 = (bf16[2,96,768]{2,1,0:T(8,128)(2,1)S(1)}, bf16[2,96,768]{2,1,0:T(8,128)(2,1)S(1)}, u32[]{:S(2)}, u32[]{:S(2)}) collective-permute-start(bf16[2,96,768]{2,1,0:T(8,128)(2,1)S(1)} %get-tuple-element.150), channel_id=1, source_target_pairs={{0,1},{1,0},{2,3},{3,2},{4,5},{5,4},{6,7},{7,6},{8,9},{9,8},{10,11... | collective-permute-start | bytes 884744 | tf_op jit(solution)/shard_map/ppermute | solution.py:24
  109.3 12.1 %collective-permute-start.26 = (bf16[96,768]{1,0:T(8,128)(2,1)S(1)}, bf16[96,768]{1,0:T(8,128)(2,1)S(1)}, u32[]{:S(2)}, u32[]{:S(2)}) collective-permute-start(bf16[96,768]{1,0:T(8,128)(2,1)S(1)} %get-tuple-element.148), channel_id=1, source_target_pairs={{0,2},{1,3},{2,0},{3,1},{4,6},{5,7},{6,4},{7,5},{8,10},{9,11},{10,... | collective-permute-start | bytes 442376 | tf_op jit(solution)/shard_map/ppermute | solution.py:24
  126.4 13.6 %collective-permute-start.39 = (bf16[2,112,768]{2,1,0:T(8,128)(2,1)S(1)}, bf16[2,112,768]{2,1,0:T(8,128)(2,1)S(1)}, u32[]{:S(2)}, u32[]{:S(2)}) collective-permute-start(bf16[2,112,768]{2,1,0:T(8,128)(2,1)S(1)} %get-tuple-element.174.refs_1_), channel_id=1, source_target_pairs={{0,1},{1,0},{2,3},{3,2},{4,5},{5,4},{6,7},{7,6},{8,9},{9,8},{10,11... | collective-permute-start | bytes 1032200 | tf_op jit(solution)/shard_map/ppermute | solution.py:24
  129.0 11.2 %collective-permute-start.41 = (bf16[128,768]{1,0:T(8,128)(2,1)S(1)}, bf16[128,768]{1,0:T(8,128)(2,1)S(1)}, u32[]{:S(2)}, u32[]{:S(2)}) collective-permute-start(bf16[128,768]{1,0:T(8,128)(2,1)S(1)} %get-tuple-element.181), channel_id=1, source_target_pairs={{0,8},{4,12},{8,0},{12,4},{16,24},{20,28},{24,16},{28,20},{1,9},{5... | collective-permute-start | bytes 589832 | tf_op jit(solution)/shard_map/ppermute | solution.py:24
  130.2 10.8 %collective-permute-start.42 = (bf16[128,768]{1,0:T(8,128)(2,1)S(1)}, bf16[128,768]{1,0:T(8,128)(2,1)S(1)}, u32[]{:S(2)}, u32[]{:S(2)}) collective-permute-start(bf16[128,768]{1,0:T(8,128)(2,1)S(1)} %get-tuple-element.182), channel_id=1, source_target_pairs={{0,16},{4,20},{8,24},{12,28},{16,0},{20,4},{24,8},{28,12},{1,17},{... | collective-permute-start | bytes 589832 | tf_op jit(solution)/shard_map/ppermute | solution.py:24
  130.8 10.2 %collective-permute-start.43 = (bf16[128,768]{1,0:T(8,128)(2,1)S(1)}, bf16[128,768]{1,0:T(8,128)(2,1)S(1)}, u32[]{:S(2)}, u32[]{:S(2)}) collective-permute-start(bf16[128,768]{1,0:T(8,128)(2,1)S(1)} %get-tuple-element.183), channel_id=1, source_target_pairs={{0,24},{4,28},{8,16},{12,20},{16,8},{20,12},{24,0},{28,4},{1,25},{... | collective-permute-start | bytes 589832 | tf_op jit(solution)/shard_map/ppermute | solution.py:24
  132.6 7.7 %collective-permute-start.45 = (bf16[96,768]{1,0:T(8,128)(2,1)S(1)}, bf16[96,768]{1,0:T(8,128)(2,1)S(1)}, u32[]{:S(2)}, u32[]{:S(2)}) collective-permute-start(bf16[96,768]{1,0:T(8,128)(2,1)S(1)} %get-tuple-element.194), channel_id=1, source_target_pairs={{0,2},{1,3},{2,0},{3,1},{4,6},{5,7},{6,4},{7,5},{8,10},{9,11},{10,... | collective-permute-start | bytes 442376 | tf_op jit(solution)/shard_map/ppermute | solution.py:24
  140.0 9.7 %collective-permute-start.40 = (bf16[112,768]{1,0:T(8,128)(2,1)S(1)}, bf16[112,768]{1,0:T(8,128)(2,1)S(1)}, u32[]{:S(2)}, u32[]{:S(2)}) collective-permute-start(bf16[112,768]{1,0:T(8,128)(2,1)S(1)} %get-tuple-element.176), channel_id=1, source_target_pairs={{0,2},{1,3},{2,0},{3,1},{4,6},{5,7},{6,4},{7,5},{8,10},{9,11},{10,... | collective-permute-start | bytes 516104 | tf_op jit(solution)/shard_map/ppermute | solution.py:24
  141.1 22.4 %collective-permute-start.46 = (bf16[192,768]{1,0:T(8,128)(2,1)S(1)}, bf16[192,768]{1,0:T(8,128)(2,1)S(1)}, u32[]{:S(2)}, u32[]{:S(2)}) collective-permute-start(bf16[192,768]{1,0:T(8,128)(2,1)S(1)} %shard_map.333.refs_1_), channel_id=1, source_target_pairs={{0,8},{4,12},{8,0},{12,4},{16,24},{20,28},{24,16},{28,20},{1,9},{5... | collective-permute-start | bytes 884744 | tf_op jit(solution)/shard_map/ppermute | solution.py:24
  142.1 21.5 %collective-permute-start.47 = (bf16[192,768]{1,0:T(8,128)(2,1)S(1)}, bf16[192,768]{1,0:T(8,128)(2,1)S(1)}, u32[]{:S(2)}, u32[]{:S(2)}) collective-permute-start(bf16[192,768]{1,0:T(8,128)(2,1)S(1)} %shard_map.333.refs_1_), channel_id=1, source_target_pairs={{0,16},{4,20},{8,24},{12,28},{16,0},{20,4},{24,8},{28,12},{1,17},{... | collective-permute-start | bytes 884744 | tf_op jit(solution)/shard_map/ppermute | solution.py:24
  143.3 20.3 %collective-permute-start.48 = (bf16[192,768]{1,0:T(8,128)(2,1)S(1)}, bf16[192,768]{1,0:T(8,128)(2,1)S(1)}, u32[]{:S(2)}, u32[]{:S(2)}) collective-permute-start(bf16[192,768]{1,0:T(8,128)(2,1)S(1)} %shard_map.333.refs_1_), channel_id=1, source_target_pairs={{0,24},{4,28},{8,16},{12,20},{16,8},{20,12},{24,0},{28,4},{1,25},{... | collective-permute-start | bytes 884744 | tf_op jit(solution)/shard_map/ppermute | solution.py:24
  (20 other events, 73.3 us)
